TPU v7x, 128 devices: a whole 4x4x4 slice. The times are simulated.
128 devices in a mesh: sub: 16 (over x, y), code: 8 (over z, core).
Axes of the slice: x: 4, y: 4, z: 4, core: 2. Of those that a mesh axis runs over, the one named last changes fastest.
Arguments:
- inputs: bfloat16 [4096, 1024], P('sub'), may hold values from -6 to 6
- upstream: bfloat16 [4096, 1024], P('sub'), may hold values from -6 to 6
- codebook: bfloat16 [16, 64, 32768], P('sub', None, 'code'), may hold values from -8 to 8
Outputs:
- quantized: bfloat16 [4096, 1024], P('sub')
- grad_inputs: bfloat16 [4096, 1024], P('sub')
- grad_codebook: float32 [16, 64, 32768], P('sub', None, 'code')
All inputs are finite; a program needn't handle non-finite values.
Results may differ from a plain program's by a relative error of at most 0.012.
Values may be sent and summed in bfloat16 or wider, within the bound.
No kernel may reach another device: no remote copies, remote signals or barrier semaphores. Data moves between devices by JAX's collectives and lax.ppermute only.
A program may use at most 256 MiB of HBM per device.

v0:
```python
import jax
import jax.numpy as jnp
from jax import lax
from jax.sharding import PartitionSpec as P

score_scale = 0.25


def first_pass(x_sub, book, blk):
    blocks = x_sub.reshape(x_sub.shape[0] // blk, blk, x_sub.shape[1])

    def one_block(xb):
        scores = score_scale * jnp.dot(xb, book, preferred_element_type=jnp.float32)
        top = jnp.max(scores, axis=1)
        expo = jnp.exp(scores - top[:, None])
        total = jnp.sum(expo, axis=1)
        part = jnp.einsum(
            "bk,dk->bd", expo.astype(jnp.bfloat16), book, preferred_element_type=jnp.float32
        )
        return (top, total, part)

    found = lax.map(one_block, blocks)
    rows = x_sub.shape[0]
    stored = None
    return (
        found[0].reshape(rows),
        found[1].reshape(rows),
        found[2].reshape(rows, x_sub.shape[1]),
        stored,
    )


def second_pass(x_sub, g_sub, book, top, total, quant, stored, blk):
    rows, width = x_sub.shape
    count = rows // blk

    def step(acc, item):
        xb, gb, tb, zb, qb, sb = item
        sb = score_scale * jnp.dot(xb, book, preferred_element_type=jnp.float32)
        prob = jnp.exp(sb - tb[:, None]) / zb[:, None]
        dprob = jnp.dot(gb, book, preferred_element_type=jnp.float32)
        gq = jnp.sum(gb.astype(jnp.float32) * qb, axis=1)
        dscore = prob * (dprob - gq[:, None])
        dsb = dscore.astype(jnp.bfloat16)
        pb = prob.astype(jnp.bfloat16)
        dx = score_scale * jnp.einsum("bk,dk->bd", dsb, book, preferred_element_type=jnp.float32)
        dbook = score_scale * jnp.einsum("bd,bk->dk", xb, dsb, preferred_element_type=jnp.float32)
        dbook = dbook + jnp.einsum("bd,bk->dk", gb, pb, preferred_element_type=jnp.float32)
        return (acc + dbook, dx)

    items = (
        x_sub.reshape(count, blk, width),
        g_sub.reshape(count, blk, width),
        top.reshape(count, blk),
        total.reshape(count, blk),
        quant.reshape(count, blk, width),
        stored,
    )
    dbook, dx = lax.scan(step, jnp.zeros(book.shape, jnp.float32), items)
    return (dx.reshape(rows, width), dbook)


def local(inputs, upstream, codebook):
    x_all, g_all = (
        lax.all_to_all(inputs, "sub", split_axis=1, concat_axis=0, tiled=True),
        lax.all_to_all(upstream, "sub", split_axis=1, concat_axis=0, tiled=True),
    )
    blk = 512
    tops, totals, parts, stores = ([], [], [], [])
    index = 0
    top, total, part, stored = first_pass(x_all, codebook[index], blk)
    tops.append(top)
    totals.append(total)
    parts.append(part)
    stores.append(stored)
    top_c = jnp.stack(tops)
    total_c = jnp.stack(totals)
    part_c = jnp.stack(parts)
    top = lax.pmax(top_c, "code")
    factor = jnp.exp(top_c - top)
    total, weighted = lax.psum((total_c * factor, part_c * factor[..., None]), "code")
    quant = weighted / total[..., None]
    grads, books = ([], [])
    index = 0
    dx, dbook = second_pass(
        x_all, g_all, codebook[index], top[index], total[index], quant[index], stores[index], blk
    )
    grads.append(dx)
    books.append(dbook)
    grad_cols = grads[0]
    quant_cols = quant[0]
    grad_full = lax.psum(grad_cols, "code").astype(jnp.bfloat16)
    quantized, grad_inputs = (
        lax.all_to_all(
            quant_cols.astype(jnp.bfloat16), "sub", split_axis=0, concat_axis=1, tiled=True
        ),
        lax.all_to_all(grad_full, "sub", split_axis=0, concat_axis=1, tiled=True),
    )
    return (quantized, grad_inputs, jnp.stack(books))


def solution(mesh):
    in_specs = (P("sub", None), P("sub", None), P("sub", None, "code"))
    out_specs = (P("sub", None), P("sub", None), P("sub", None, "code"))
    return jax.shard_map(local, mesh=mesh, in_specs=in_specs, out_specs=out_specs, check_vma=False)
```

profile of v0, /device:TPU:1, one launch (start us, length us, event | category | flops | bytes accessed | tf_op | source)
XLA Modules:
  0.0 375.8 jit_solution(15206589982974240991)
XLA Ops:
  7.2 2.0 copy.31
  9.2 7.6 %all-to-all-start = ((bf16[256,16,64]{0,2,1:T(8,128)(2,1)}), bf16[256,16,64]{0,2,1:T(8,128)(2,1)S(1)}, u32[]{:S(2)}, u32[]{:S(2)}) async-start(bf16[256,16,64]{0,2,1:T(8,128)(2,1)} %bitcast.4), calls=%async_computation | async-start | bytes 1048576 | tf_op jit(solution)/shard_map/all_to_all | solution.py:65
  16.9 10.2 %all-to-all-done = bf16[256,16,64]{0,2,1:T(8,128)(2,1)S(1)} async-done(((bf16[256,16,64]{0,2,1:T(8,128)(2,1)}), bf16[256,16,64]{0,2,1:T(8,128)(2,1)S(1)}, u32[]{:S(2)}, u32[]{:S(2)}) %all-to-all-start) | async-done | bytes 524320 | tf_op jit(solution)/shard_map/all_to_all | solution.py:65
  27.7 58.6 %while.27 = (s32[]{:T(128)}, f32[8,512]{1,0:T(8,128)S(1)}, f32[8,512]{1,0:T(8,128)S(1)}, f32[8,512,64]{1,0,2:T(8,128)S(1)}, bf16[8,512,64]{2,1,0:T(8,128)(2,1)S(...) while((s32[]{:T(128)}, f32[8,512]{1,0:T(8,128)S(1)}, f32[8,512]{1,0:T(8,128)S(1)}, ...), condition=%wide.region_3.4_spmd, body=%wide.region_0.3_spmd.sunk | while | flops 553647104 | bytes 29114504 | solution.py:22
  27.7 2.4 multiply_reduce_fusion.2
  30.2 1.5 fusion.58
  31.7 1.9 fusion.59
  35.1 2.4 multiply_reduce_fusion.2
  37.5 1.5 fusion.58
  39.0 1.9 fusion.59
  42.4 2.4 multiply_reduce_fusion.2
  44.8 1.5 fusion.58
  46.3 1.9 fusion.59
  49.7 2.4 multiply_reduce_fusion.2
  52.1 1.5 fusion.58
  53.7 1.9 fusion.59
  57.0 2.4 multiply_reduce_fusion.2
  59.5 1.5 fusion.58
  61.0 1.9 fusion.59
  64.4 2.4 multiply_reduce_fusion.2
  66.8 1.5 fusion.58
  68.3 1.9 fusion.59
  71.7 2.4 multiply_reduce_fusion.2
  75.6 1.9 fusion.59
  79.0 2.4 multiply_reduce_fusion.2
  82.9 1.9 fusion.59
  87.3 1.8 stack_reshape.9
  89.1 24.0 %pmax.7 = f32[1,4096]{1,0:T(1,128)S(1)} all-reduce(f32[1,4096]{1,0:T(1,128)S(1)} %bitcast.130), channel_id=1, replica_groups=mesh['sub'=16,'code'=8] {'code'}, use_global_device_ids=true, to_apply=%region_4.5 | all-reduce | flops 4096 | bytes 32768 | tf_op jit(solution)/shard_map/pmax | solution.py:79
  116.5 3.6 all-to-all-start.2
  120.1 8.9 %all-to-all-done.2 = bf16[256,16,64]{0,2,1:T(8,128)(2,1)S(1)} async-done(((bf16[256,16,64]{0,2,1:T(8,128)(2,1)}), bf16[256,16,64]{0,2,1:T(8,128)(2,1)S(1)}, u32[]{:S(2)}, u32[]{:S(2)}) %all-to-all-start.2) | async-done | bytes 524320 | tf_op jit(solution)/shard_map/all_to_all | solution.py:66
  129.5 25.9 %psum.22 = f32[1,4096]{1,0:T(1,128)S(1)} all-reduce(f32[1,4096]{1,0:T(1,128)S(1)} %get-tuple-element.200), channel_id=1, replica_groups=mesh['sub'=16,'code'=8] {'code'}, use_global_device_ids=true, to_apply=%region_6.7 | all-reduce | flops 4096 | bytes 32768 | tf_op jit(solution)/shard_map/psum | solution.py:81
  156.1 18.8 %all-reduce.3.cloned.1.call-done = f32[1,4096,64]{1,2,0:T(8,128)} async-done(((f32[1,4096,64]{1,2,0:T(8,128)}), f32[1,4096,64]{1,2,0:T(8,128)}) %all-reduce.3.cloned.1.call-update) | async-done | bytes 1048592 | tf_op jit(solution)/shard_map/psum | solution.py:81
  174.9 2.3 fusion.28
  178.3 6.5 %all-to-all-start.1 = ((bf16[16,256,64]{1,2,0:T(8,128)(2,1)}), bf16[16,256,64]{1,2,0:T(8,128)(2,1)S(1)}, u32[]{:S(2)}, u32[]{:S(2)}) async-start(bf16[16,256,64]{1,2,0:T(8,128)(2,1)} %copy.35), calls=%async_computation.1 | async-start | bytes 1048576 | tf_op jit(solution)/shard_map/all_to_all | solution.py:94
  184.8 3.2 copy.46
  189.1 107.6 %while.28 = (s32[]{:T(128)}, f32[64,4096]{1,0:T(8,128)S(1)}, f32[8,512,64]{1,0,2:T(8,128)}, bf16[8,512,64]{2,1,0:T(8,128)(2,1)}, bf16[64,4096]{1,0:T(8,128)(2,1)...) while((s32[]{:T(128)}, f32[64,4096]{1,0:T(8,128)S(1)}, ...), condition=%wide.region_9.10_spmd.clone, body=%wide.region_7.9_spmd.clone.sunk | while | flops 1358036480 | bytes 44908696 | solution.py:59
  190.3 2.9 exponential_divide_fusion.2
  195.9 1.8 convolution_multiply_fusion.3
  198.8 3.8 %dynamic_update_slice.22 = f32[8,512,64]{1,0,2:T(8,128)} dynamic-update-slice(f32[8,512,64]{1,0,2:T(8,128)} %get-tuple-element.344, f32[1,512,64]{1,0,2:T(1,128)S(1)} %copy.64, s32[]{:T(128)S(6)} %copy.85, s32[]{:T(128)} %constant.41.clone.1..sunk.1, s32[]{:T(128)} %constant.41.clone.1..sunk.1) | dynamic-update-slice | bytes 262148 | tf_op jit(solution)/shard_map/while/body/jit(dynamic_update_index_in_dim)/dynamic_update_slice | solution.py:22
  203.7 2.9 exponential_divide_fusion.2
  209.3 1.8 convolution_multiply_fusion.3
  212.3 3.8 %dynamic_update_slice.22 = f32[8,512,64]{1,0,2:T(8,128)} dynamic-update-slice(f32[8,512,64]{1,0,2:T(8,128)} %get-tuple-element.344, f32[1,512,64]{1,0,2:T(1,128)S(1)} %copy.64, s32[]{:T(128)S(6)} %copy.85, s32[]{:T(128)} %constant.41.clone.1..sunk.1, s32[]{:T(128)} %constant.41.clone.1..sunk.1) | dynamic-update-slice | bytes 262148 | tf_op jit(solution)/shard_map/while/body/jit(dynamic_update_index_in_dim)/dynamic_update_slice | solution.py:22
  217.2 2.9 exponential_divide_fusion.2
  222.8 1.8 convolution_multiply_fusion.3
  225.7 3.8 %dynamic_update_slice.22 = f32[8,512,64]{1,0,2:T(8,128)} dynamic-update-slice(f32[8,512,64]{1,0,2:T(8,128)} %get-tuple-element.344, f32[1,512,64]{1,0,2:T(1,128)S(1)} %copy.64, s32[]{:T(128)S(6)} %copy.85, s32[]{:T(128)} %constant.41.clone.1..sunk.1, s32[]{:T(128)} %constant.41.clone.1..sunk.1) | dynamic-update-slice | bytes 262148 | tf_op jit(solution)/shard_map/while/body/jit(dynamic_update_index_in_dim)/dynamic_update_slice | solution.py:22
  230.6 2.9 exponential_divide_fusion.2
  236.2 1.8 convolution_multiply_fusion.3
  239.2 3.8 %dynamic_update_slice.22 = f32[8,512,64]{1,0,2:T(8,128)} dynamic-update-slice(f32[8,512,64]{1,0,2:T(8,128)} %get-tuple-element.344, f32[1,512,64]{1,0,2:T(1,128)S(1)} %copy.64, s32[]{:T(128)S(6)} %copy.85, s32[]{:T(128)} %constant.41.clone.1..sunk.1, s32[]{:T(128)} %constant.41.clone.1..sunk.1) | dynamic-update-slice | bytes 262148 | tf_op jit(solution)/shard_map/while/body/jit(dynamic_update_index_in_dim)/dynamic_update_slice | solution.py:22
  244.0 2.9 exponential_divide_fusion.2
  249.7 1.8 convolution_multiply_fusion.3
  252.6 3.8 %dynamic_update_slice.22 = f32[8,512,64]{1,0,2:T(8,128)} dynamic-update-slice(f32[8,512,64]{1,0,2:T(8,128)} %get-tuple-element.344, f32[1,512,64]{1,0,2:T(1,128)S(1)} %copy.64, s32[]{:T(128)S(6)} %copy.85, s32[]{:T(128)} %constant.41.clone.1..sunk.1, s32[]{:T(128)} %constant.41.clone.1..sunk.1) | dynamic-update-slice | bytes 262148 | tf_op jit(solution)/shard_map/while/body/jit(dynamic_update_index_in_dim)/dynamic_update_slice | solution.py:22
  257.5 2.9 exponential_divide_fusion.2
  263.1 1.8 convolution_multiply_fusion.3
  266.1 3.8 %dynamic_update_slice.22 = f32[8,512,64]{1,0,2:T(8,128)} dynamic-update-slice(f32[8,512,64]{1,0,2:T(8,128)} %get-tuple-element.344, f32[1,512,64]{1,0,2:T(1,128)S(1)} %copy.64, s32[]{:T(128)S(6)} %copy.85, s32[]{:T(128)} %constant.41.clone.1..sunk.1, s32[]{:T(128)} %constant.41.clone.1..sunk.1) | dynamic-update-slice | bytes 262148 | tf_op jit(solution)/shard_map/while/body/jit(dynamic_update_index_in_dim)/dynamic_update_slice | solution.py:22
  270.9 2.9 exponential_divide_fusion.2
  276.6 1.8 convolution_multiply_fusion.3
  279.5 3.8 %dynamic_update_slice.22 = f32[8,512,64]{1,0,2:T(8,128)} dynamic-update-slice(f32[8,512,64]{1,0,2:T(8,128)} %get-tuple-element.344, f32[1,512,64]{1,0,2:T(1,128)S(1)} %copy.64, s32[]{:T(128)S(6)} %copy.85, s32[]{:T(128)} %constant.41.clone.1..sunk.1, s32[]{:T(128)} %constant.41.clone.1..sunk.1) | dynamic-update-slice | bytes 262148 | tf_op jit(solution)/shard_map/while/body/jit(dynamic_update_index_in_dim)/dynamic_update_slice | solution.py:22
  284.4 2.9 exponential_divide_fusion.2
  290.0 1.8 convolution_multiply_fusion.3
  293.0 3.8 %dynamic_update_slice.22 = f32[8,512,64]{1,0,2:T(8,128)} dynamic-update-slice(f32[8,512,64]{1,0,2:T(8,128)} %get-tuple-element.344, f32[1,512,64]{1,0,2:T(1,128)S(1)} %copy.64, s32[]{:T(128)S(6)} %copy.85, s32[]{:T(128)} %constant.41.clone.1..sunk.1, s32[]{:T(128)} %constant.41.clone.1..sunk.1) | dynamic-update-slice | bytes 262148 | tf_op jit(solution)/shard_map/while/body/jit(dynamic_update_index_in_dim)/dynamic_update_slice | solution.py:22
  296.7 2.2 copy.58
  298.9 52.0 %all-reduce.4 = bf16[4096,64]{0,1:T(8,128)(2,1)S(1)} all-reduce(f32[4096,64]{0,1:T(8,128)S(1)} %bitcast.119), channel_id=1, replica_groups=mesh['sub'=16,'code'=8] {'code'}, use_global_device_ids=true, to_apply=%region_10.11 | all-reduce | flops 262144 | bytes 1572864 | tf_op jit(solution)/shard_map/psum | solution.py:92
  351.8 6.9 %all-to-all-start.3 = ((bf16[16,256,64]{1,2,0:T(8,128)(2,1)}), bf16[16,256,64]{1,2,0:T(8,128)(2,1)S(1)}, u32[]{:S(2)}, u32[]{:S(2)}) async-start(bf16[16,256,64]{1,2,0:T(8,128)(2,1)} %bitcast.72), calls=%async_computation.3 | async-start | bytes 1048576 | tf_op jit(solution)/shard_map/all_to_all | solution.py:97
  359.7 8.2 %all-to-all-done.3 = bf16[16,256,64]{1,2,0:T(8,128)(2,1)S(1)} async-done(((bf16[16,256,64]{1,2,0:T(8,128)(2,1)}), bf16[16,256,64]{1,2,0:T(8,128)(2,1)S(1)}, u32[]{:S(2)}, u32[]{:S(2)}) %all-to-all-start.3) | async-done | bytes 524320 | tf_op jit(solution)/shard_map/all_to_all | solution.py:97
  (132 shorter events, 64.6 us)
Async XLA Ops:
  9.2 17.9 %all-to-all-start = ((bf16[256,16,64]{0,2,1:T(8,128)(2,1)}), bf16[256,16,64]{0,2,1:T(8,128)(2,1)S(1)}, u32[]{:S(2)}, u32[]{:S(2)}) async-start(bf16[256,16,64]{0,2,1:T(8,128)(2,1)} %bitcast.4), calls=%async_computation | async-start | bytes 1048576 | tf_op jit(solution)/shard_map/all_to_all | solution.py:65
  16.8 158.1 %all-reduce.3.cloned.1.call-start = ((), (), s32[]{:S(2)}) async-start(), calls=%async_computation.4 | async-start | bytes 2097152 | tf_op jit(solution)/shard_map/psum | solution.py:81
  27.7 87.8 %copy-start.5 = (bf16[256,1024]{1,0:T(8,128)(2,1)S(1)}, bf16[256,1024]{1,0:T(8,128)(2,1)}, u32[]{:S(2)}) copy-start(bf16[256,1024]{1,0:T(8,128)(2,1)} %param.8) | copy-start | bytes 1572868
  27.7 4.0 %copy-start = (bf16[64,4096]{1,0:T(8,128)(2,1)S(1)}, bf16[64,4096]{1,0:T(8,128)(2,1)}, u32[]{:S(2)}) copy-start(bf16[64,4096]{1,0:T(8,128)(2,1)} %get-tuple-element.328) | copy-start | bytes 1572868 | tf_op jit(solution)/shard_map/while
  35.1 3.9 %copy-start = (bf16[64,4096]{1,0:T(8,128)(2,1)S(1)}, bf16[64,4096]{1,0:T(8,128)(2,1)}, u32[]{:S(2)}) copy-start(bf16[64,4096]{1,0:T(8,128)(2,1)} %get-tuple-element.328) | copy-start | bytes 1572868 | tf_op jit(solution)/shard_map/while
  42.4 3.9 %copy-start = (bf16[64,4096]{1,0:T(8,128)(2,1)S(1)}, bf16[64,4096]{1,0:T(8,128)(2,1)}, u32[]{:S(2)}) copy-start(bf16[64,4096]{1,0:T(8,128)(2,1)} %get-tuple-element.328) | copy-start | bytes 1572868 | tf_op jit(solution)/shard_map/while
  49.7 3.9 %copy-start = (bf16[64,4096]{1,0:T(8,128)(2,1)S(1)}, bf16[64,4096]{1,0:T(8,128)(2,1)}, u32[]{:S(2)}) copy-start(bf16[64,4096]{1,0:T(8,128)(2,1)} %get-tuple-element.328) | copy-start | bytes 1572868 | tf_op jit(solution)/shard_map/while
  57.0 3.9 %copy-start = (bf16[64,4096]{1,0:T(8,128)(2,1)S(1)}, bf16[64,4096]{1,0:T(8,128)(2,1)}, u32[]{:S(2)}) copy-start(bf16[64,4096]{1,0:T(8,128)(2,1)} %get-tuple-element.328) | copy-start | bytes 1572868 | tf_op jit(solution)/shard_map/while
  64.3 3.9 %copy-start = (bf16[64,4096]{1,0:T(8,128)(2,1)S(1)}, bf16[64,4096]{1,0:T(8,128)(2,1)}, u32[]{:S(2)}) copy-start(bf16[64,4096]{1,0:T(8,128)(2,1)} %get-tuple-element.328) | copy-start | bytes 1572868 | tf_op jit(solution)/shard_map/while
  71.7 3.9 %copy-start = (bf16[64,4096]{1,0:T(8,128)(2,1)S(1)}, bf16[64,4096]{1,0:T(8,128)(2,1)}, u32[]{:S(2)}) copy-start(bf16[64,4096]{1,0:T(8,128)(2,1)} %get-tuple-element.328) | copy-start | bytes 1572868 | tf_op jit(solution)/shard_map/while
  79.0 3.9 %copy-start = (bf16[64,4096]{1,0:T(8,128)(2,1)S(1)}, bf16[64,4096]{1,0:T(8,128)(2,1)}, u32[]{:S(2)}) copy-start(bf16[64,4096]{1,0:T(8,128)(2,1)} %get-tuple-element.328) | copy-start | bytes 1572868 | tf_op jit(solution)/shard_map/while
  86.3 1.0 copy-start.4
  87.3 27.1 %copy-start.3 = (bf16[8,512,64]{2,1,0:T(8,128)(2,1)}, bf16[8,512,64]{2,1,0:T(8,128)(2,1)S(1)}, u32[]{:S(2)}) copy-start(bf16[8,512,64]{2,1,0:T(8,128)(2,1)S(1)} %get-tuple-element.366) | copy-start | bytes 1572868
  114.4 74.8 %copy-start.1 = (bf16[64,4096]{1,0:T(8,128)(2,1)S(1)}, bf16[64,4096]{1,0:T(8,128)(2,1)}, u32[]{:S(2)}) copy-start(bf16[64,4096]{1,0:T(8,128)(2,1)} %get-tuple-element.365) | copy-start | bytes 1572868
  116.5 12.5 %all-to-all-start.2 = ((bf16[256,16,64]{0,2,1:T(8,128)(2,1)}), bf16[256,16,64]{0,2,1:T(8,128)(2,1)S(1)}, u32[]{:S(2)}, u32[]{:S(2)}) async-start(bf16[256,16,64]{0,2,1:T(8,128)(2,1)} %bitcast.11), calls=%async_computation.2 | async-start | bytes 1048576 | tf_op jit(solution)/shard_map/all_to_all | solution.py:66
  178.3 173.5 %all-to-all-start.1 = ((bf16[16,256,64]{1,2,0:T(8,128)(2,1)}), bf16[16,256,64]{1,2,0:T(8,128)(2,1)S(1)}, u32[]{:S(2)}, u32[]{:S(2)}) async-start(bf16[16,256,64]{1,2,0:T(8,128)(2,1)} %copy.35), calls=%async_computation.1 | async-start | bytes 1048576 | tf_op jit(solution)/shard_map/all_to_all | solution.py:94
  296.7 72.2 %copy-start.2 = (f32[64,4096]{1,0:T(8,128)}, f32[64,4096]{1,0:T(8,128)S(1)}, u32[]{:S(2)}) copy-start(f32[64,4096]{1,0:T(8,128)S(1)} %get-tuple-element.89) | copy-start | bytes 3145732
  351.8 16.1 %all-to-all-start.3 = ((bf16[16,256,64]{1,2,0:T(8,128)(2,1)}), bf16[16,256,64]{1,2,0:T(8,128)(2,1)S(1)}, u32[]{:S(2)}, u32[]{:S(2)}) async-start(bf16[16,256,64]{1,2,0:T(8,128)(2,1)} %bitcast.72), calls=%async_computation.3 | async-start | bytes 1048576 | tf_op jit(solution)/shard_map/all_to_all | solution.py:97
Sparse Core Ops, SparseCore 0:
  115.6 59.2 all-reduce.2
where the time goes:
time: 380 us; the launch traced here: 376 us
  matrix products  102 us (27%)
  blocking collectives  102 us (27%)
  local copies, waits for them, and re-layouts  60.4 us (16%)
  waiting for transfers between devices  46.2 us (12%)
  other arithmetic  25.6 us (7%)
  starting transfers between devices  24.7 us (6%)
  between operations  14.2 us (4%)
    psum x1, blocking collectives, local(): grad_full = lax.psum(grad_cols, 'code').astype(jnp.bfloat16)  52 us
    dynamic_update_slice x48, local copies, waits for them, and re-layouts, first_pass(): found = lax.map(one_block, blocks)  42.4 us
    psum x1, blocking collectives, local(): lax.psum((total_c * factor, part_c * factor[..., None]), 'code')  25.9 us
    pmax x1, blocking collectives, local(): top = lax.pmax(top_c, 'code')  24 us
    dot_general x8, matrix products, step(): sb = score_scale * jnp.dot(xb, book, preferred_element_type=jnp.float32)  23.5 us
    dot_general x8, matrix products, one_block(): scores = score_scale * jnp.dot(xb, book, preferred_element_type=jnp.float32)  19.4 us
    psum x1, waiting for transfers between devices, local(): lax.psum((total_c * factor, part_c * factor[..., None]), 'code')  18.8 us
    dot_general x8, matrix products, one_block(): jnp.einsum('bk,dk->bd', expo.astype(jnp.bfloat16), book, preferred_elemen...  15.4 us
  transfers between devices with their start and end apart: 5, of which 4 were waited for; matrix products, arithmetic and copies ran while one was open for 31% of the time, Pallas kernels for 0%

commit v1 on v0

v1 whole, which is shorter than its diff:
```python
import functools

import jax
import jax.numpy as jnp
from jax import lax
from jax.experimental import pallas as pl
from jax.experimental.pallas import tpu as pltpu
from jax.sharding import PartitionSpec as P

BF16 = jnp.bfloat16
F32 = jnp.float32
DS = 64
LANES = 128
SCALE = 0.25
LOG2E = 1.4426950408889634
VMEM_LIMIT = 56 * 2**20


def scores_body(chunk, xa_ref, xb_ref, book_ref, bookt_ref, e_ref, part_ref, stat_ref, xgt_ref, s0, s1, m0, m1):
    t = pl.program_id(0)
    rows, codes = s0.shape

    def step(s_new, m_new, s_old, m_old):
        x = xa_ref[:, :DS]
        top = m_old[...]
        wide = jnp.concatenate([top] * (chunk // LANES), axis=1)
        most = None
        acc = jnp.zeros((rows, LANES), F32)
        for c in range(0, codes, chunk):
            s = jnp.dot(x, book_ref[:, c : c + chunk], preferred_element_type=F32)
            s_new[:, c : c + chunk] = s
            for k in range(0, chunk, LANES):
                piece = s[:, k : k + LANES]
                most = piece if most is None else jnp.maximum(most, piece)
            e = jnp.exp2(s_old[:, c : c + chunk] * (SCALE * LOG2E) - wide).astype(BF16)
            e_ref[:, c : c + chunk] = e
            acc = acc + jnp.dot(e, bookt_ref[c : c + chunk, :], preferred_element_type=F32)
        m_new[...] = jnp.broadcast_to(jnp.max(most, axis=1, keepdims=True) * (SCALE * LOG2E), (rows, LANES))
        part_ref[...] = acc
        lane = lax.broadcasted_iota(jnp.int32, (rows, LANES), 1)
        total = jnp.sum(jnp.where(lane == DS, acc, 0.0), axis=1, keepdims=True)
        g = xb_ref[:, DS:].astype(F32)
        h = jnp.sum(acc[:, :DS] * g, axis=1, keepdims=True)
        stat = jnp.where(lane == 0, top, jnp.where(lane == 1, total, h))
        stat_ref[...] = stat.T[:8]
        xgt_ref[...] = xb_ref[...].T

    @pl.when(t % 2 == 0)
    def _():
        step(s0, m0, s1, m1)

    @pl.when(t % 2 == 1)
    def _():
        step(s1, m1, s0, m0)


def scores(xg, book, bookt, tile=128, chunk=1024):
    rows, codes = xg.shape[0], book.shape[1]
    tiles = rows // tile
    now = lambda t: jnp.minimum(t, tiles - 1)
    old = lambda t: jnp.maximum(t - 1, 0)
    pairs = rows * codes
    return pl.pallas_call(
        functools.partial(scores_body, chunk),
        grid=(tiles + 1,),
        in_specs=[
            pl.BlockSpec((tile, LANES), lambda t: (now(t), 0)),
            pl.BlockSpec((tile, LANES), lambda t: (old(t), 0)),
            pl.BlockSpec((DS, codes), lambda t: (0, 0)),
            pl.BlockSpec((codes, LANES), lambda t: (0, 0)),
        ],
        out_specs=[
            pl.BlockSpec((tile, codes), lambda t: (old(t), 0)),
            pl.BlockSpec((tile, LANES), lambda t: (old(t), 0)),
            pl.BlockSpec((8, tile), lambda t: (0, old(t))),
            pl.BlockSpec((LANES, tile), lambda t: (0, old(t))),
        ],
        out_shape=[
            jax.ShapeDtypeStruct((rows, codes), BF16),
            jax.ShapeDtypeStruct((rows, LANES), F32),
            jax.ShapeDtypeStruct((8, rows), F32),
            jax.ShapeDtypeStruct((LANES, rows), BF16),
        ],
        scratch_shapes=[pltpu.VMEM((tile, codes), F32)] * 2 + [pltpu.VMEM((tile, LANES), F32)] * 2,
        compiler_params=pltpu.CompilerParams(vmem_limit_bytes=VMEM_LIMIT),
        cost_estimate=pl.CostEstimate(flops=pairs * 1024, bytes_accessed=pairs * 2, transcendentals=pairs),
        name="scores",
    )(xg, xg, book, bookt)


def slopes_body(chunk, xg_ref, book_ref, bookt_ref, e_ref, part_ref, own_ref, o1, o2, o3, ds_ref, out_ref, f_ref, d0, d1):
    rows, codes = e_ref.shape
    stats = [own_ref[...], o1[...], o2[...], o3[...]]
    top = functools.reduce(jnp.maximum, [s[0:1] for s in stats])
    rel = [jnp.exp2(s[0:1] - top) for s in stats]
    z = sum(r * s[1:2] for r, s in zip(rel, stats))
    gq_row = sum(r * s[2:3] for r, s in zip(rel, stats)) / z
    f_row = rel[0] / z
    f_ref[...] = jnp.broadcast_to(f_row, f_ref.shape)
    sub = lax.broadcasted_iota(jnp.int32, (LANES, rows), 0)
    turned = jnp.where(sub == 0, f_row, gq_row).T
    f = jnp.broadcast_to(turned[:, 0:1], (rows, LANES))
    gq = jnp.broadcast_to(turned[:, 1:2], (rows, LANES))
    wide = jnp.concatenate([gq] * (chunk // LANES), axis=1)

    g = xg_ref[:, DS:]
    acc = jnp.zeros((rows, LANES), F32)
    slots = [d0, d1]
    steps = codes // chunk
    for c in range(steps + 1):
        if c < steps:
            at = slice(c * chunk, (c + 1) * chunk)
            slots[c % 2][...] = jnp.dot(g, book_ref[:, at], preferred_element_type=F32) - wide
        if c > 0:
            at = slice((c - 1) * chunk, c * chunk)
            ds = (slots[(c - 1) % 2][...] * e_ref[:, at].astype(F32)).astype(BF16)
            ds_ref[:, at] = ds
            acc = acc + jnp.dot(ds, bookt_ref[at, :], preferred_element_type=F32)
    q = (part_ref[...] * f)[:, :DS]
    dx = (acc * (SCALE * f))[:, :DS]
    out_ref[...] = jnp.concatenate([q, dx], axis=1).astype(BF16)


def slopes(xg, book, bookt, e, part, stats, tile=256, chunk=1024):
    rows, codes = e.shape
    pairs = rows * codes
    by_row = lambda w: pl.BlockSpec((tile, w), lambda t: (t, 0))
    stat = pl.BlockSpec((8, tile), lambda t: (0, t))
    return pl.pallas_call(
        functools.partial(slopes_body, chunk),
        grid=(rows // tile,),
        in_specs=[
            by_row(LANES),
            pl.BlockSpec((DS, codes), lambda t: (0, 0)),
            pl.BlockSpec((codes, LANES), lambda t: (0, 0)),
            by_row(codes),
            by_row(LANES),
        ]
        + [stat] * 4,
        out_specs=[by_row(codes), by_row(LANES), stat],
        out_shape=[
            jax.ShapeDtypeStruct((rows, codes), BF16),
            jax.ShapeDtypeStruct((rows, LANES), BF16),
            jax.ShapeDtypeStruct((8, rows), F32),
        ],
        scratch_shapes=[pltpu.VMEM((tile, chunk), F32)] * 2,
        compiler_params=pltpu.CompilerParams(vmem_limit_bytes=VMEM_LIMIT),
        cost_estimate=pl.CostEstimate(flops=pairs * 1024, bytes_accessed=pairs * 4, transcendentals=0),
        name="slopes",
    )(xg, book, bookt, e, part, *stats)


def book_body(xgt_ref, f_ref, ds_ref, e_ref, out_ref, w_ref):
    @pl.when(pl.program_id(0) == 0)
    def _():
        f = f_ref[0:1, :]
        w_ref[:DS] = (xgt_ref[:DS].astype(F32) * (SCALE * f)).astype(BF16)
        w_ref[DS:] = (xgt_ref[DS:].astype(F32) * f).astype(BF16)

    out_ref[...] = jnp.dot(w_ref[:DS], ds_ref[...], preferred_element_type=F32) + jnp.dot(
        w_ref[DS:], e_ref[...], preferred_element_type=F32
    )


def book_grad(xgt, f, ds, e, first, width, tile=1024):
    rows, codes = e.shape
    pairs = rows * width
    start = first // tile
    return pl.pallas_call(
        book_body,
        grid=(width // tile,),
        in_specs=[
            pl.BlockSpec((LANES, rows), lambda t: (0, 0)),
            pl.BlockSpec((8, rows), lambda t: (0, 0)),
            pl.BlockSpec((rows, tile), lambda t: (0, start + t)),
            pl.BlockSpec((rows, tile), lambda t: (0, start + t)),
        ],
        out_specs=pl.BlockSpec((DS, tile), lambda t: (0, t)),
        out_shape=jax.ShapeDtypeStruct((DS, width), F32),
        scratch_shapes=[pltpu.VMEM((LANES, rows), BF16)],
        compiler_params=pltpu.CompilerParams(vmem_limit_bytes=VMEM_LIMIT),
        cost_estimate=pl.CostEstimate(flops=pairs * 1024, bytes_accessed=pairs * 4, transcendentals=0),
        name="book_grad",
    )(xgt, f, ds, e)


def local(n_sub, n_code, inputs, upstream, codebook):
    n_z = n_code // 2
    place = lax.axis_index("code")
    core, z = place % 2, place // 2
    mine = inputs.shape[0] // 2

    def to_mate(v):
        return lax.ppermute(v, "code", [(j, j ^ 1) for j in range(n_code)])

    def along_z(v, d):
        return lax.ppermute(v, "code", [(j, (j + 2 * d) % n_code) for j in range(n_code)])

    def cut(v):
        return lax.dynamic_slice_in_dim(v, core * mine, mine, 0).reshape(mine, n_sub, DS)

    xg = jnp.concatenate([cut(inputs), cut(upstream)], axis=2).transpose(1, 0, 2)
    xg = lax.all_to_all(xg, "sub", 0, 0, tiled=True).reshape(n_sub * mine, LANES)

    own_book = codebook[0]
    width = own_book.shape[1]
    book = jnp.concatenate([own_book, to_mate(own_book)], axis=1)
    codes = book.shape[1]
    bookt = jnp.concatenate(
        [book.T, jnp.ones((codes, 1), BF16), jnp.zeros((codes, LANES - DS - 1), BF16)], axis=1
    )

    e, part, stat, xgt = scores(xg, book, bookt)
    stats = [stat] + [along_z(stat, d) for d in range(1, n_z)]
    ds, out, f = slopes(xg, book, bookt, e, part, stats)

    out = lax.all_to_all(out, "sub", 0, 0, tiled=True)
    step = mine // n_z
    pieces = out.reshape(n_sub, n_z, step, LANES)
    piece = lambda k: lax.dynamic_index_in_dim(pieces, k, 1, keepdims=False)
    total = piece(z).astype(F32)
    for d in range(1, n_z):
        total = total + along_z(piece((z + d) % n_z), d).astype(F32)
    total = total.astype(BF16)
    ring = [along_z(total, d) for d in range(n_z - 1, 0, -1)] + [total]
    whole = lax.dynamic_slice_in_dim(jnp.stack(ring + ring), n_z - 1 - z, n_z, 0)
    half = whole.reshape(n_z, n_sub, step, 2, DS).transpose(3, 0, 2, 1, 4).reshape(2, mine, n_sub * DS)
    other = to_mate(half)
    both = jnp.concatenate([jnp.where(core == 0, half, other), jnp.where(core == 0, other, half)], axis=1)

    far = book_grad(xgt, f, ds, e, width, width)
    near = book_grad(xgt, f, ds, e, 0, width)
    grad_book = near + to_mate(far)
    return both[0], both[1], grad_book[None]


def solution(mesh):
    in_specs = (P("sub", None), P("sub", None), P("sub", None, "code"))
    out_specs = (P("sub", None), P("sub", None), P("sub", None, "code"))
    body = functools.partial(local, mesh.shape["sub"], mesh.shape["code"])
    return jax.shard_map(body, mesh=mesh, in_specs=in_specs, out_specs=out_specs, check_vma=False)
```

time: 380 us -> 165 us (0.43); the launches traced: 376 us -> 165 us
  matrix products: 102 us -> 0 us
  blocking collectives: 102 us -> 0 us
  Pallas kernels: 0 us -> 86.2 us
  local copies, waits for them, and re-layouts: 60.4 us -> 9.74 us
  waiting for transfers between devices: 46.2 us -> 27.9 us
  other arithmetic: 25.6 us -> 9.46 us
  between operations: 14.2 us -> 0.92 us
  starting transfers between devices: 24.7 us -> 30.8 us
    dot_general x56 -> x0, matrix products: 102 us -> none  [the longest x8 23.5 us: step(): sb = score_scale * jnp.dot(xb, book, preferred_element_type=jnp.float32)]
    pallas_call x0 -> x4, Pallas kernels: none -> 86.2 us  [the longest x1 30.5 us: slopes(): pl.pallas_call(functools.partial(slopes_body, chunk), grid=(rows // tile,...]
    psum x2 -> x0, blocking collectives: 77.9 us -> none  [the longest x1 52 us: local(): grad_full = lax.psum(grad_cols, 'code').astype(jnp.bfloat16)]
    dynamic_update_slice x48 -> x0, local copies, waits for them, and re-layouts: 42.4 us -> none  [first_pass(): found = lax.map(one_block, blocks)]
    pmax x1 -> x0, blocking collectives: 24 us -> none  [local(): top = lax.pmax(top_c, 'code')]
    reduce_sum x16 -> x0, other arithmetic: 20.8 us -> none  [the longest x8 12 us: one_block(): total = jnp.sum(expo, axis=1)]
    ppermute x0 -> x12, starting transfers between devices: none -> 19.2 us  [the longest x9 12.4 us: along_z(): lax.ppermute(v, 'code', [(j, (j + 2 * d) % n_code) for j in range(n_code)])]
    psum x1 -> x0, waiting for transfers between devices: 18.8 us -> none  [local(): lax.psum((total_c * factor, part_c * factor[..., None]), 'code')]
  transfers between devices with their start and end apart: 5 -> 14, of which waited for: 4 -> 6; matrix products, arithmetic and copies ran while one was open for 31% -> 5% of each run, Pallas kernels for 0% -> 17%
where the time goes in v1:
time: 165 us
  Pallas kernels  86.2 us (52%)
  starting transfers between devices  30.8 us (19%)
  waiting for transfers between devices  27.9 us (17%)
  local copies, waits for them, and re-layouts  9.74 us (6%)
  other arithmetic  9.46 us (6%)
    pallas_call x1, Pallas kernels, slopes(): pl.pallas_call(functools.partial(slopes_body, chunk), grid=(rows // tile,...  30.5 us
    pallas_call x1, Pallas kernels, scores(): pl.pallas_call(functools.partial(scores_body, chunk), grid=(tiles + 1,),...  28.2 us
    pallas_call x2, Pallas kernels, book_grad(): pl.pallas_call(book_body, grid=(width // tile,), in_specs=[pl.BlockSpec((...  27.5 us
    ppermute x9, starting transfers between devices, along_z(): lax.ppermute(v, 'code', [(j, (j + 2 * d) % n_code) for j in range(n_code)])  12.4 us
    all_to_all x1, waiting for transfers between devices, local(): lax.all_to_all(xg, 'sub', 0, 0, tiled=True).reshape(n_sub * mine, LANES)  9.48 us
    ppermute x9, waiting for transfers between devices, along_z(): lax.ppermute(v, 'code', [(j, (j + 2 * d) % n_code) for j in range(n_code)])  9.29 us
    all_to_all x1, waiting for transfers between devices, local(): out = lax.all_to_all(out, 'sub', 0, 0, tiled=True)  9.13 us
    all_to_all x1, starting transfers between devices, local(): lax.all_to_all(xg, 'sub', 0, 0, tiled=True).reshape(n_sub * mine, LANES)  6.84 us
  transfers between devices with their start and end apart: 14, of which 6 were waited for; matrix products, arithmetic and copies ran while one was open for 5% of the time, Pallas kernels for 17%

profile of v1, /device:TPU:1, one launch (start us, length us, event | category | flops | bytes accessed | tf_op | source)
XLA Modules:
  0.0 165.0 jit_solution(8888880522967107131)
XLA Ops:
  0.6 1.5 collective-permute-start
  2.1 0.0 copy-start.1
  2.1 1.1 constant_dynamic-slice_fusion.1
  3.3 0.2 copy.32
  3.4 0.2 copy.33
  3.6 0.8 maximum_bitcast_fusion
  4.4 6.8 %all-to-all-start = ((bf16[16,128,128]{1,2,0:T(8,128)(2,1)}), bf16[16,128,128]{1,2,0:T(8,128)(2,1)S(1)}, u32[]{:S(2)}, u32[]{:S(2)}) async-start(bf16[16,128,128]{1,2,0:T(8,128)(2,1)} %maximum_bitcast_fusion), calls=%async_computation | async-start | bytes 1048576 | tf_op jit(solution)/shard_map/all_to_all | solution.py:203
  11.3 0.0 copy-done.1
  11.3 0.5 copy.25
  11.8 0.1 pad.4.clone
  11.9 0.1 pad.3.clone
  11.9 9.5 %all-to-all-done = bf16[16,128,128]{1,2,0:T(8,128)(2,1)S(1)} async-done(((bf16[16,128,128]{1,2,0:T(8,128)(2,1)}), bf16[16,128,128]{1,2,0:T(8,128)(2,1)S(1)}, u32[]{:S(2)}, u32[]{:S(2)}) %all-to-all-start) | async-done | bytes 524320 | tf_op jit(solution)/shard_map/all_to_all | solution.py:203
  21.4 1.0 copy.24
  22.4 0.0 collective-permute-done
  22.4 1.3 copy.27
  23.8 3.1 %fusion.6 = (bf16[8192,64]{1,0:T(8,128)(2,1)S(1)}, bf16[64,8192]{0,1:T(8,128)(2,1)}) fusion(bf16[64,4096]{0,1:T(8,128)(2,1)} %copy.27, bf16[64,4096]{0,1:T(8,128)(2,1)S(1)} %bitcast.45), kind=kLoop, calls=%fused_computation.30 | loop fusion | flops 2097152 | bytes 3145728 | tf_op jit(solution)/shard_map/transpose | solution.py:210
  26.9 2.7 %copy.29.book_ref = bf16[64,8192]{1,0:T(8,128)(2,1)} copy(bf16[64,8192]{0,1:T(8,128)(2,1)} %get-tuple-element.18) | data formatting | bytes 2097152 | tf_op jit(solution)/shard_map/concatenate | solution.py:207
  29.5 2.0 %maximum_maximum_fusion.bookt_ref = bf16[8192,128]{1,0:T(8,128)(2,1)} fusion(bf16[8192,64]{1,0:T(8,128)(2,1)S(1)} %get-tuple-element.17, bf16[128]{0:T(256)(128)(2,1)S(1)} %pad.4.clone, bf16[128]{0:T(256)(128)(2,1)S(1)} %pad.3.clone), kind=kLoop, calls=%fused_computation.1 | loop fusion | flops 6291456 | bytes 3146240 | tf_op jit(solution)/shard_map/concatenate | solution.py:209
  31.6 28.2 %scores.1 = (bf16[2048,8192]{1,0:T(8,128)(2,1)}, f32[2048,128]{1,0:T(8,128)}, f32[8,2048]{1,0:T(8,128)}, bf16[128,2048]{1,0:T(8,128)(2,1)}) custom-call(bf16[2048,128]{1,0:T(8,128)(2,1)} %bitcast.52, bf16[2048,128]{1,0:T(8,128)(2,1)} %bitcast.53, bf16[64,8192]{1,0:T(8,128)(2,1)} %copy.29.book_ref, bf16[8192,128]{1,0:T(8,128)(2,1)} %maximum_maximum_fusion.bookt_ref), custom_call_target="tpu_custom_call" | custom-call | flops 17179869184 | bytes 33554432 | tf_op jit(solution)/shard_map/scores/pallas_call | solution.py:63
  59.8 1.7 %collective-permute-start.1 = (f32[8,2048]{1,0:T(8,128)}, f32[8,2048]{1,0:T(8,128)S(1)}, u32[]{:S(2)}, u32[]{:S(2)}) collective-permute-start(f32[8,2048]{1,0:T(8,128)} %get-tuple-element.12.own_ref), channel_id=1, source_target_pairs={{0,2},{1,3},{2,4},{3,5},{4,6},{5,7},{6,0},{7,1},{8,10},{9,11},{10,... | collective-permute-start | bytes 196616 | tf_op jit(solution)/shard_map/ppermute | solution.py:197
  61.5 3.3 %collective-permute-start.2 = (f32[8,2048]{1,0:T(8,128)}, f32[8,2048]{1,0:T(8,128)S(1)}, u32[]{:S(2)}, u32[]{:S(2)}) collective-permute-start(f32[8,2048]{1,0:T(8,128)} %get-tuple-element.12.own_ref), channel_id=1, source_target_pairs={{0,4},{1,5},{2,6},{3,7},{4,0},{5,1},{6,2},{7,3},{8,12},{9,13},{10,... | collective-permute-start | bytes 196616 | tf_op jit(solution)/shard_map/ppermute | solution.py:197
  64.8 0.7 collective-permute-start.3
  65.5 0.0 collective-permute-done.1.o1
  65.5 0.0 copy-start.2
  65.5 1.8 %collective-permute-done.2.o2 = f32[8,2048]{1,0:T(8,128)S(1)} collective-permute-done((f32[8,2048]{1,0:T(8,128)}, f32[8,2048]{1,0:T(8,128)S(1)}, u32[]{:S(2)}, u32[]{:S(2)}) %collective-permute-start.2) | collective-permute-done | bytes 65568 | tf_op jit(solution)/shard_map/ppermute | solution.py:197
  67.3 0.0 copy-start.3
  67.3 1.0 collective-permute-done.3.o3
  68.3 0.0 copy-start.4
  68.3 0.0 copy-done.2
  68.3 0.0 copy-done.3
  68.3 0.6 copy-done.4
  68.9 30.5 %slopes.1 = (bf16[2048,8192]{1,0:T(8,128)(2,1)}, bf16[2048,128]{1,0:T(8,128)(2,1)}, f32[8,2048]{1,0:T(8,128)}) custom-call(bf16[2048,128]{1,0:T(8,128)(2,1)} %bitcast.54, bf16[64,8192]{1,0:T(8,128)(2,1)} %copy.29.book_ref, bf16[8192,128]{1,0:T(8,128)(2,1)} %maximum_maximum_fusion.bookt_ref, bf16[2048,8192]{1,0:T(8,128)(2,1)} %get-tuple-element.10.e_ref, ...), custom_call_target="tpu_custom_call" | custom-call | flops 17179869184 | bytes 67108864 | tf_op jit(solution)/shard_map/slopes/pallas_call | solution.py:129
  99.5 4.8 %all-to-all-start.1 = ((bf16[16,128,128]{2,1,0:T(8,128)(2,1)}), bf16[16,128,128]{2,1,0:T(8,128)(2,1)S(1)}, u32[]{:S(2)}, u32[]{:S(2)}) async-start(bf16[16,128,128]{2,1,0:T(8,128)(2,1)} %bitcast.51), calls=%async_computation.1 | async-start | bytes 1048576 | tf_op jit(solution)/shard_map/all_to_all | solution.py:217
  104.4 9.1 %all-to-all-done.1 = bf16[16,128,128]{2,1,0:T(8,128)(2,1)S(1)} async-done(((bf16[16,128,128]{2,1,0:T(8,128)(2,1)}), bf16[16,128,128]{2,1,0:T(8,128)(2,1)S(1)}, u32[]{:S(2)}, u32[]{:S(2)}) %all-to-all-start.1) | async-done | bytes 524320 | tf_op jit(solution)/shard_map/all_to_all | solution.py:217
  113.5 0.1 collective-permute-start.4
  113.6 3.2 %collective-permute-start.5 = (bf16[16,32,128]{2,1,0:T(8,128)(2,1)S(1)}, bf16[16,32,128]{2,1,0:T(8,128)(2,1)S(1)}, u32[]{:S(2)}, u32[]{:S(2)}) collective-permute-start(bf16[16,32,128]{2,1,0:T(8,128)(2,1)S(1)} %get-tuple-element.25), channel_id=1, source_target_pairs={{0,4},{1,5},{2,6},{3,7},{4,0},{5,1},{6,2},{7,3},{8,12},{9,13},{10,... | collective-permute-start | bytes 393224 | tf_op jit(solution)/shard_map/ppermute | solution.py:197
  116.8 0.0 collective-permute-start.6
  116.8 13.8 %book_grad.3 = f32[64,4096]{1,0:T(8,128)} custom-call(bf16[128,2048]{1,0:T(8,128)(2,1)} %get-tuple-element.14.xgt_ref, f32[8,2048]{1,0:T(8,128)} %get-tuple-element.15.f_ref, bf16[2048,8192]{1,0:T(8,128)(2,1)} %get-tuple-element.16.ds_ref, bf16[2048,8192]{1,0:T(8,128)(2,1)} %get-tuple-element.10.e_ref), custom_call_target="tpu_custom_call" | custom-call | flops 8589934592 | bytes 33554432 | tf_op jit(solution)/shard_map/book_grad/pallas_call | solution.py:169
  130.6 0.0 collective-permute-done.4
  130.6 0.0 collective-permute-done.5
  130.6 0.0 collective-permute-done.6
  130.6 0.1 fusion.5
  130.7 0.3 collective-permute-start.7
  131.0 13.7 %book_grad.2 = f32[64,4096]{1,0:T(8,128)} custom-call(bf16[128,2048]{1,0:T(8,128)(2,1)} %get-tuple-element.14.xgt_ref, f32[8,2048]{1,0:T(8,128)} %get-tuple-element.15.f_ref, bf16[2048,8192]{1,0:T(8,128)(2,1)} %get-tuple-element.16.ds_ref, bf16[2048,8192]{1,0:T(8,128)(2,1)} %get-tuple-element.10.e_ref), custom_call_target="tpu_custom_call" | custom-call | flops 8589934592 | bytes 33554432 | tf_op jit(solution)/shard_map/book_grad/pallas_call | solution.py:169
  144.8 4.3 %collective-permute-start.11 = (f32[64,4096]{1,0:T(8,128)}, f32[64,4096]{1,0:T(8,128)}, u32[]{:S(2)}, u32[]{:S(2)}) collective-permute-start(f32[64,4096]{1,0:T(8,128)} %book_grad.3), channel_id=1, source_target_pairs={{0,1},{1,0},{2,3},{3,2},{4,5},{5,4},{6,7},{7,6},{8,9},{9,8},{10,11... | collective-permute-start | bytes 3145736 | tf_op jit(solution)/shard_map/ppermute | solution.py:194
  149.0 3.1 %collective-permute-start.8 = (bf16[16,32,128]{2,1,0:T(8,128)(2,1)S(1)}, bf16[16,32,128]{2,1,0:T(8,128)(2,1)S(1)}, u32[]{:S(2)}, u32[]{:S(2)}) collective-permute-start(bf16[16,32,128]{2,1,0:T(8,128)(2,1)S(1)} %fusion.5), channel_id=1, source_target_pairs={{0,4},{1,5},{2,6},{3,7},{4,0},{5,1},{6,2},{7,3},{8,12},{9,13},{10,... | collective-permute-start | bytes 393224 | tf_op jit(solution)/shard_map/ppermute | solution.py:197
  152.1 0.0 collective-permute-start.9
  152.1 0.0 collective-permute-done.7
  152.2 3.7 %collective-permute-done.8 = bf16[16,32,128]{2,1,0:T(8,128)(2,1)S(1)} collective-permute-done((bf16[16,32,128]{2,1,0:T(8,128)(2,1)S(1)}, bf16[16,32,128]{2,1,0:T(8,128)(2,1)S(1)}, u32[]{:S(2)}, u32[]{:S(2)}) %collective-permute-start.8) | collective-permute-done | bytes 131104 | tf_op jit(solution)/shard_map/ppermute | solution.py:197
  155.9 2.7 %collective-permute-done.9 = bf16[16,32,128]{2,1,0:T(8,128)(2,1)S(1)} collective-permute-done((bf16[16,32,128]{2,1,0:T(8,128)(2,1)S(1)}, bf16[16,32,128]{2,1,0:T(8,128)(2,1)S(1)}, u32[]{:S(2)}, u32[]{:S(2)}) %collective-permute-start.9) | collective-permute-done | bytes 131104 | tf_op jit(solution)/shard_map/ppermute | solution.py:197
  158.8 0.4 reshape.33
  159.2 0.0 copy-start
  159.2 0.7 copy.30
  159.9 0.7 reshape.34
  160.7 1.0 collective-permute-start.10
  161.6 0.0 collective-permute-done.11
  161.6 0.0 copy-done
  161.6 2.3 %add_bitcast_fusion = f32[1,64,4096]{2,1,0:T(8,128)} fusion(f32[64,4096]{1,0:T(8,128)S(1)} %copy-done, f32[64,4096]{1,0:T(8,128)} %collective-permute-done.11), kind=kLoop, calls=%fused_computation.4 | loop fusion | flops 262144 | bytes 3145728 | tf_op jit(solution)/shard_map/broadcast_in_dim | solution.py:234
  163.9 0.0 collective-permute-done.10
  163.9 0.1 broadcast_select_fusion
  164.0 1.0 fusion.2
  (11 shorter events, 0.2 us)
Async XLA Ops:
  0.6 21.8 %collective-permute-start = (bf16[64,4096]{1,0:T(8,128)(2,1)}, bf16[64,4096]{1,0:T(8,128)(2,1)S(1)}, u32[]{:S(2)}, u32[]{:S(2)}) collective-permute-start(bf16[64,4096]{1,0:T(8,128)(2,1)} %bitcast.50), channel_id=1, source_target_pairs={{0,1},{1,0},{2,3},{3,2},{4,5},{5,4},{6,7},{7,6},{8,9},{9,8},{10,11... | collective-permute-start | bytes 1572872 | tf_op jit(solution)/shard_map/ppermute | solution.py:194
  2.1 9.2 %copy-start.1 = (bf16[1,64,4096]{2,1,0:T(8,128)(2,1)S(1)}, bf16[1,64,4096]{2,1,0:T(8,128)(2,1)}, u32[]{:S(2)}) copy-start(bf16[1,64,4096]{2,1,0:T(8,128)(2,1)} %param.5) | copy-start | bytes 1572868
  4.4 17.0 %all-to-all-start = ((bf16[16,128,128]{1,2,0:T(8,128)(2,1)}), bf16[16,128,128]{1,2,0:T(8,128)(2,1)S(1)}, u32[]{:S(2)}, u32[]{:S(2)}) async-start(bf16[16,128,128]{1,2,0:T(8,128)(2,1)} %maximum_bitcast_fusion), calls=%async_computation | async-start | bytes 1048576 | tf_op jit(solution)/shard_map/all_to_all | solution.py:203
  59.8 5.7 %collective-permute-start.1 = (f32[8,2048]{1,0:T(8,128)}, f32[8,2048]{1,0:T(8,128)S(1)}, u32[]{:S(2)}, u32[]{:S(2)}) collective-permute-start(f32[8,2048]{1,0:T(8,128)} %get-tuple-element.12.own_ref), channel_id=1, source_target_pairs={{0,2},{1,3},{2,4},{3,5},{4,6},{5,7},{6,0},{7,1},{8,10},{9,11},{10,... | collective-permute-start | bytes 196616 | tf_op jit(solution)/shard_map/ppermute | solution.py:197
  61.5 5.9 %collective-permute-start.2 = (f32[8,2048]{1,0:T(8,128)}, f32[8,2048]{1,0:T(8,128)S(1)}, u32[]{:S(2)}, u32[]{:S(2)}) collective-permute-start(f32[8,2048]{1,0:T(8,128)} %get-tuple-element.12.own_ref), channel_id=1, source_target_pairs={{0,4},{1,5},{2,6},{3,7},{4,0},{5,1},{6,2},{7,3},{8,12},{9,13},{10,... | collective-permute-start | bytes 196616 | tf_op jit(solution)/shard_map/ppermute | solution.py:197
  64.8 3.6 %collective-permute-start.3 = (f32[8,2048]{1,0:T(8,128)}, f32[8,2048]{1,0:T(8,128)S(1)}, u32[]{:S(2)}, u32[]{:S(2)}) collective-permute-start(f32[8,2048]{1,0:T(8,128)} %get-tuple-element.12.own_ref), channel_id=1, source_target_pairs={{0,6},{1,7},{2,0},{3,1},{4,2},{5,3},{6,4},{7,5},{8,14},{9,15},{10,... | collective-permute-start | bytes 196616 | tf_op jit(solution)/shard_map/ppermute | solution.py:197
  65.5 2.9 %copy-start.2 = (f32[8,2048]{1,0:T(8,128)}, f32[8,2048]{1,0:T(8,128)S(1)}, u32[]{:S(2)}) copy-start(f32[8,2048]{1,0:T(8,128)S(1)} %collective-permute-done.1.o1) | copy-start | bytes 196612
  67.3 1.0 copy-start.3
  68.3 0.6 copy-start.4
  99.5 14.0 %all-to-all-start.1 = ((bf16[16,128,128]{2,1,0:T(8,128)(2,1)}), bf16[16,128,128]{2,1,0:T(8,128)(2,1)S(1)}, u32[]{:S(2)}, u32[]{:S(2)}) async-start(bf16[16,128,128]{2,1,0:T(8,128)(2,1)} %bitcast.51), calls=%async_computation.1 | async-start | bytes 1048576 | tf_op jit(solution)/shard_map/all_to_all | solution.py:217
  113.5 17.1 %collective-permute-start.4 = (bf16[16,32,128]{2,1,0:T(8,128)(2,1)S(1)}, bf16[16,32,128]{2,1,0:T(8,128)(2,1)S(1)}, u32[]{:S(2)}, u32[]{:S(2)}) collective-permute-start(bf16[16,32,128]{2,1,0:T(8,128)(2,1)S(1)} %get-tuple-element.23), channel_id=1, source_target_pairs={{0,2},{1,3},{2,4},{3,5},{4,6},{5,7},{6,0},{7,1},{8,10},{9,11},{10,... | collective-permute-start | bytes 393224 | tf_op jit(solution)/shard_map/ppermute | solution.py:197
  113.6 17.0 %collective-permute-start.5 = (bf16[16,32,128]{2,1,0:T(8,128)(2,1)S(1)}, bf16[16,32,128]{2,1,0:T(8,128)(2,1)S(1)}, u32[]{:S(2)}, u32[]{:S(2)}) collective-permute-start(bf16[16,32,128]{2,1,0:T(8,128)(2,1)S(1)} %get-tuple-element.25), channel_id=1, source_target_pairs={{0,4},{1,5},{2,6},{3,7},{4,0},{5,1},{6,2},{7,3},{8,12},{9,13},{10,... | collective-permute-start | bytes 393224 | tf_op jit(solution)/shard_map/ppermute | solution.py:197
  116.8 13.8 %collective-permute-start.6 = (bf16[16,32,128]{2,1,0:T(8,128)(2,1)S(1)}, bf16[16,32,128]{2,1,0:T(8,128)(2,1)S(1)}, u32[]{:S(2)}, u32[]{:S(2)}) collective-permute-start(bf16[16,32,128]{2,1,0:T(8,128)(2,1)S(1)} %get-tuple-element.24), channel_id=1, source_target_pairs={{0,6},{1,7},{2,0},{3,1},{4,2},{5,3},{6,4},{7,5},{8,14},{9,15},{10,... | collective-permute-start | bytes 393224 | tf_op jit(solution)/shard_map/ppermute | solution.py:197
  130.7 21.4 %collective-permute-start.7 = (bf16[16,32,128]{2,1,0:T(8,128)(2,1)S(1)}, bf16[16,32,128]{2,1,0:T(8,128)(2,1)S(1)}, u32[]{:S(2)}, u32[]{:S(2)}) collective-permute-start(bf16[16,32,128]{2,1,0:T(8,128)(2,1)S(1)} %fusion.5), channel_id=1, source_target_pairs={{0,6},{1,7},{2,0},{3,1},{4,2},{5,3},{6,4},{7,5},{8,14},{9,15},{10,... | collective-permute-start | bytes 393224 | tf_op jit(solution)/shard_map/ppermute | solution.py:197
  144.8 16.9 %collective-permute-start.11 = (f32[64,4096]{1,0:T(8,128)}, f32[64,4096]{1,0:T(8,128)}, u32[]{:S(2)}, u32[]{:S(2)}) collective-permute-start(f32[64,4096]{1,0:T(8,128)} %book_grad.3), channel_id=1, source_target_pairs={{0,1},{1,0},{2,3},{3,2},{4,5},{5,4},{6,7},{7,6},{8,9},{9,8},{10,11... | collective-permute-start | bytes 3145736 | tf_op jit(solution)/shard_map/ppermute | solution.py:194
  149.0 6.8 %collective-permute-start.8 = (bf16[16,32,128]{2,1,0:T(8,128)(2,1)S(1)}, bf16[16,32,128]{2,1,0:T(8,128)(2,1)S(1)}, u32[]{:S(2)}, u32[]{:S(2)}) collective-permute-start(bf16[16,32,128]{2,1,0:T(8,128)(2,1)S(1)} %fusion.5), channel_id=1, source_target_pairs={{0,4},{1,5},{2,6},{3,7},{4,0},{5,1},{6,2},{7,3},{8,12},{9,13},{10,... | collective-permute-start | bytes 393224 | tf_op jit(solution)/shard_map/ppermute | solution.py:197
  152.1 6.5 %collective-permute-start.9 = (bf16[16,32,128]{2,1,0:T(8,128)(2,1)S(1)}, bf16[16,32,128]{2,1,0:T(8,128)(2,1)S(1)}, u32[]{:S(2)}, u32[]{:S(2)}) collective-permute-start(bf16[16,32,128]{2,1,0:T(8,128)(2,1)S(1)} %fusion.5), channel_id=1, source_target_pairs={{0,2},{1,3},{2,4},{3,5},{4,6},{5,7},{6,0},{7,1},{8,10},{9,11},{10,... | collective-permute-start | bytes 393224 | tf_op jit(solution)/shard_map/ppermute | solution.py:197
  159.2 2.4 %copy-start = (f32[64,4096]{1,0:T(8,128)S(1)}, f32[64,4096]{1,0:T(8,128)}, u32[]{:S(2)}) copy-start(f32[64,4096]{1,0:T(8,128)} %book_grad.2) | copy-start | bytes 3145732
  160.7 3.3 %collective-permute-start.10 = (bf16[2,128,1024]{2,1,0:T(8,128)(2,1)S(1)}, bf16[2,128,1024]{2,1,0:T(8,128)(2,1)S(1)}, u32[]{:S(2)}, u32[]{:S(2)}) collective-permute-start(bf16[2,128,1024]{2,1,0:T(8,128)(2,1)S(1)} %reshape.34), channel_id=1, source_target_pairs={{0,1},{1,0},{2,3},{3,2},{4,5},{5,4},{6,7},{7,6},{8,9},{9,8},{10,11... | collective-permute-start | bytes 1572872 | tf_op jit(solution)/shard_map/ppermute | solution.py:194

commit v2 on v0

v2 whole, which is shorter than its diff:
```python
import functools

import jax
import jax.numpy as jnp
from jax import lax
from jax.experimental import pallas as pl
from jax.experimental.pallas import tpu as pltpu
from jax.sharding import PartitionSpec as P

BF16 = jnp.bfloat16
F32 = jnp.float32
DS = 64
LANES = 128
SCALE = 0.25
LOG2E = 1.4426950408889634
MIB = 2**20
WHOLE = pl.BlockSpec(memory_space=pltpu.VMEM)
SCALAR = pl.BlockSpec(memory_space=pltpu.SMEM)


def span(start, size):
    return pl.ds(pl.multiple_of(start, size), size)


def small(body, name, n_in, outs, flops=10**8):
    return pl.pallas_call(
        body,
        in_specs=[SCALAR] + [WHOLE] * n_in,
        out_specs=[WHOLE] * len(outs),
        out_shape=outs,
        compiler_params=pltpu.CompilerParams(vmem_limit_bytes=12 * MIB),
        cost_estimate=pl.CostEstimate(flops=flops, bytes_accessed=2**21, transcendentals=0),
        name=name,
    )


def pack_body(place_ref, x_ref, g_ref, out_ref):
    subs, rows, _ = out_ref.shape
    at = pl.ds(pl.multiple_of(place_ref[0] * rows, rows), rows)
    for k in range(0, subs, 2):
        cols = slice(k * DS, (k + 2) * DS)
        x, g = x_ref[at, cols], g_ref[at, cols]
        out_ref[k] = jnp.concatenate([x[:, :DS], g[:, :DS]], axis=1)
        out_ref[k + 1] = jnp.concatenate([x[:, DS:], g[:, DS:]], axis=1)


def book_body_prep(place_ref, own_ref, mate_ref, book_ref, bookt_ref):
    width = own_ref.shape[1]
    step = 512
    lane = lax.broadcasted_iota(jnp.int32, (step, LANES), 1)
    for n, ref in enumerate((own_ref, mate_ref)):
        book_ref[:, n * width : (n + 1) * width] = ref[...]
        for c in range(0, width, step):
            v = ref[:, c : c + step].astype(F32)
            turned = jnp.concatenate([v, jnp.zeros_like(v)], axis=0).T
            bookt_ref[n * width + c : n * width + c + step, :] = jnp.where(lane == DS, 1.0, turned).astype(BF16)


def local_pass_body(chunk, tiles, xg_ref, book_ref, bookt_ref, e_ref, ds_ref, part_ref, dx_ref, stat_ref, xgt_ref, *scratch):
    s_slots, m_slots, e_slots, gq_slots, d_slots = (scratch[k : k + 2] for k in range(0, 10, 2))
    t = pl.program_id(0)
    tile, codes = e_ref.shape
    steps = codes // chunk

    def look(n):
        x = xg_ref[span(t * tile, tile), :][:, :DS]
        most = None

        def one(c):
            nonlocal most
            if c == steps:
                return
            s = jnp.dot(x, book_ref[:, c * chunk : (c + 1) * chunk], preferred_element_type=F32)
            s_slots[n][:, c * chunk : (c + 1) * chunk] = s
            for k in range(0, chunk, LANES):
                piece = s[:, k : k + LANES]
                most = piece if most is None else jnp.maximum(most, piece)

        def end():
            top = jnp.max(most, axis=1, keepdims=True) * (SCALE * LOG2E)
            m_slots[n][...] = jnp.broadcast_to(top, (tile, LANES))

        return one, end

    def weigh(n):
        top = m_slots[n][...]
        wide = jnp.concatenate([top] * (chunk // LANES), axis=1)
        acc = jnp.zeros((tile, LANES), F32)

        def one(c):
            nonlocal acc
            if c == steps:
                return
            at = slice(c * chunk, (c + 1) * chunk)
            e = jnp.exp2(s_slots[n][:, at] * (SCALE * LOG2E) - wide).astype(BF16)
            e_ref[:, at] = e
            e_slots[n][:, at] = e
            acc = acc + jnp.dot(e, bookt_ref[at, :], preferred_element_type=F32)

        def end():
            part_ref[...] = acc
            lane = lax.broadcasted_iota(jnp.int32, (tile, LANES), 1)
            total = jnp.sum(jnp.where(lane == DS, acc, 0.0), axis=1, keepdims=True)
            xg = xg_ref[span((t - 1) * tile, tile), :]
            h = jnp.sum(acc[:, :DS] * xg[:, DS:].astype(F32), axis=1, keepdims=True)
            gq = h / total
            gq_slots[n][...] = jnp.broadcast_to(gq, (tile, LANES))
            stat = jnp.where(lane == 0, top, jnp.where(lane == 1, total, jnp.where(lane == 2, h, gq)))
            stat_ref[...] = stat.T[:8]
            xgt_ref[...] = xg.T

        return one, end

    def lean(n):
        g = xg_ref[span((t - 2) * tile, tile), :][:, DS:]
        wide = jnp.concatenate([gq_slots[n][...]] * (chunk // LANES), axis=1)
        acc = jnp.zeros((tile, LANES), F32)

        def one(c):
            nonlocal acc
            if c < steps:
                at = slice(c * chunk, (c + 1) * chunk)
                d_slots[c % 2][...] = jnp.dot(g, book_ref[:, at], preferred_element_type=F32) - wide
            if c > 0:
                at = slice((c - 1) * chunk, c * chunk)
                ds = (d_slots[(c - 1) % 2][...] * e_slots[n][:, at].astype(F32)).astype(BF16)
                ds_ref[:, at] = ds
                acc = acc + jnp.dot(ds, bookt_ref[at, :], preferred_element_type=F32)

        def end():
            dx_ref[...] = acc

        return one, end

    def run(*works):
        for c in range(steps + 1):
            for one, _ in works:
                one(c)
        for _, end in works:
            end()

    for n in range(2):
        full = jnp.logical_and(jnp.logical_and(t >= 2, t < tiles), t % 2 == n)

        @pl.when(full)
        def _():
            run(look(n), weigh(1 - n), lean(n))

    last = tiles % 2

    @pl.when(t == 0)
    def _():
        run(look(0))

    @pl.when(t == 1)
    def _():
        run(look(1), weigh(0))

    @pl.when(t == tiles)
    def _():
        run(weigh(1 - last), lean(last))

    @pl.when(t == tiles + 1)
    def _():
        run(lean(1 - last))


def local_pass(xg, book, bookt, tile=128, chunk=1024):
    rows, codes = xg.shape[0], book.shape[1]
    tiles = rows // tile
    pairs = rows * codes
    back = lambda n: lambda t: jnp.clip(t - n, 0, tiles - 1)
    by_row = lambda w, n: pl.BlockSpec((tile, w), lambda t: (back(n)(t), 0))
    by_col = lambda h, n: pl.BlockSpec((h, tile), lambda t: (0, back(n)(t)))
    fixed = lambda *shape: pl.BlockSpec(shape, lambda t: (0, 0))
    wide, narrow = pltpu.VMEM((tile, codes), F32), pltpu.VMEM((tile, LANES), F32)
    return pl.pallas_call(
        functools.partial(local_pass_body, chunk, tiles),
        grid=(tiles + 2,),
        in_specs=[fixed(rows, LANES), fixed(DS, codes), fixed(codes, LANES)],
        out_specs=[by_row(codes, 1), by_row(codes, 2), by_row(LANES, 1), by_row(LANES, 2), by_col(8, 1), by_col(LANES, 1)],
        out_shape=[
            jax.ShapeDtypeStruct((rows, codes), BF16),
            jax.ShapeDtypeStruct((rows, codes), BF16),
            jax.ShapeDtypeStruct((rows, LANES), F32),
            jax.ShapeDtypeStruct((rows, LANES), F32),
            jax.ShapeDtypeStruct((8, rows), F32),
            jax.ShapeDtypeStruct((LANES, rows), BF16),
        ],
        scratch_shapes=[wide, wide, narrow, narrow]
        + [pltpu.VMEM((tile, codes), BF16)] * 2
        + [narrow, narrow]
        + [pltpu.VMEM((tile, chunk), F32)] * 2,
        compiler_params=pltpu.CompilerParams(vmem_limit_bytes=44 * MIB),
        cost_estimate=pl.CostEstimate(flops=pairs * 2048, bytes_accessed=pairs * 4, transcendentals=pairs),
        name="local_pass",
    )(xg, book, bookt)


def mix_body(part_ref, dx_ref, xgt_ref, own_ref, o1, o2, o3, out_ref, w_ref):
    rows = part_ref.shape[0]
    stats = [r[...] for r in (own_ref, o1, o2, o3)]
    top = functools.reduce(jnp.maximum, [s[0:1] for s in stats])
    rel = [jnp.exp2(s[0:1] - top) for s in stats]
    z = sum(r * s[1:2] for r, s in zip(rel, stats))
    gq = sum(r * s[2:3] for r, s in zip(rel, stats)) / z
    f_row = rel[0] / z
    off_row = stats[0][3:4] - gq
    x, g = xgt_ref[:DS].astype(F32), xgt_ref[DS:].astype(F32)
    w_ref[:DS] = (x * (SCALE * f_row)).astype(BF16)
    w_ref[DS:] = ((g + (SCALE * off_row) * x) * f_row).astype(BF16)
    step = LANES
    sub = lax.broadcasted_iota(jnp.int32, (LANES, step), 0)
    for r in range(0, rows, step):
        at = slice(r, r + step)
        turned = jnp.where(sub == 0, f_row[:, at], off_row[:, at]).T
        f, off = turned[:, 0:1], turned[:, 1:2]
        part = part_ref[at, :]
        q = (part * f)[:, :DS]
        dx = ((dx_ref[at, :] + part * off) * (SCALE * f))[:, :DS]
        out_ref[at, :] = jnp.concatenate([q, dx], axis=1).astype(BF16)


def mix(part, dx, xgt, stats):
    rows = part.shape[0]
    return pl.pallas_call(
        mix_body,
        in_specs=[WHOLE] * 7,
        out_specs=[WHOLE] * 2,
        out_shape=[jax.ShapeDtypeStruct((rows, LANES), BF16), jax.ShapeDtypeStruct((LANES, rows), BF16)],
        compiler_params=pltpu.CompilerParams(vmem_limit_bytes=12 * MIB),
        cost_estimate=pl.CostEstimate(flops=10**8, bytes_accessed=2**22, transcendentals=0),
        name="mix",
    )(part, dx, xgt, *stats)


def book_body(w_ref, ds_ref, e_ref, *rest):
    out_ref = rest[-1]
    grad = jnp.dot(w_ref[:DS], ds_ref[...], preferred_element_type=F32)
    grad += jnp.dot(w_ref[DS:], e_ref[...], preferred_element_type=F32)
    if len(rest) > 1:
        grad += rest[0][...]
    out_ref[...] = grad


def book_grad(w, ds, e, first, width, whole, other=None, before=None, tile=1024):
    rows, codes = e.shape
    pairs = rows * width
    start = first // tile
    into = first % whole // tile
    tall = pl.BlockSpec((rows, tile), lambda t: (0, start + t))
    flat = pl.BlockSpec((DS, tile), lambda t: (0, into + t))
    more = [] if other is None else [other]
    kept = [] if before is None else [before]
    return pl.pallas_call(
        book_body,
        grid=(width // tile,),
        in_specs=[pl.BlockSpec((LANES, rows), lambda t: (0, 0)), tall, tall]
        + [flat] * len(more)
        + [pl.BlockSpec(memory_space=pl.ANY)] * len(kept),
        out_specs=flat,
        out_shape=jax.ShapeDtypeStruct((DS, whole), F32),
        input_output_aliases={4: 0} if kept else {},
        compiler_params=pltpu.CompilerParams(vmem_limit_bytes=28 * MIB),
        cost_estimate=pl.CostEstimate(flops=pairs * 1024, bytes_accessed=pairs * 4, transcendentals=0),
        name="book_grad",
    )(w, ds, e, *more, *kept)


def pieces_body(n_z, place_ref, a_ref, own_ref, *send_refs):
    part = own_ref.shape[1]
    for d, out in enumerate((own_ref, *send_refs)):
        out[...] = a_ref[:, span(lax.rem(place_ref[1] + d, n_z) * part, part)]


def sum_body(place_ref, *refs):
    *ins, out = refs
    out[...] = sum(r[...].astype(F32) for r in ins).astype(BF16)


def spread_body(n_z, place_ref, *refs):
    *ins, q_ref, dx_ref = refs
    subs, part, _ = ins[0].shape
    for n, ref in enumerate(ins):
        swap, d = n // n_z, n % n_z
        core = place_ref[0] if swap == 0 else 1 - place_ref[0]
        at = span((core * n_z + lax.rem(place_ref[1] + n_z - d, n_z)) * part, part)
        for k in range(0, subs, 2):
            a, b = ref[k], ref[k + 1]
            cols = slice(k * DS, (k + 2) * DS)
            q_ref[at, cols] = jnp.concatenate([a[:, :DS], b[:, :DS]], axis=1)
            dx_ref[at, cols] = jnp.concatenate([a[:, DS:], b[:, DS:]], axis=1)


def local(n_sub, n_code, inputs, upstream, codebook):
    n_z = n_code // 2
    index = lax.axis_index("code")
    place = jnp.stack([index % 2, index // 2]).astype(jnp.int32)
    n_rows, width_all = inputs.shape
    mine = n_rows // 2
    shaped = jax.ShapeDtypeStruct
    then = lax.optimization_barrier

    def to_peer(v, d, swap=0):
        pairs = [(j, ((j // 2 + d) % n_z) * 2 + (j % 2 ^ swap)) for j in range(n_code)]
        return lax.ppermute(v, "code", pairs)

    own_book = codebook[0]
    width = own_book.shape[1]
    mate_book = to_peer(own_book, 0, 1)
    (xg,) = small(pack_body, "pack", 2, [shaped((n_sub, mine, LANES), BF16)])(place, inputs, upstream)
    xg = lax.all_to_all(xg, "sub", 0, 0, tiled=True)
    book, bookt = small(
        book_body_prep, "books", 2, [shaped((DS, 2 * width), BF16), shaped((2 * width, LANES), BF16)], 10**10
    )(place, own_book, mate_book)

    xg = xg.reshape(n_sub * mine, LANES)
    e, ds, part, dxl, stat, xgt = local_pass(xg, book, bookt)
    stats = [stat] + [to_peer(stat, d) for d in range(1, n_z)]
    out, w = mix(part, dxl, xgt, stats)

    moved = lax.all_to_all(out.reshape(n_sub, mine, LANES), "sub", 0, 0, tiled=True)
    far = book_grad(w, ds, e, width, width, width)
    moved, far = then((moved, far))
    from_far = to_peer(far, 0, 1)
    piece = shaped((n_sub, mine // n_z, LANES), BF16)
    own, *sends = small(functools.partial(pieces_body, n_z), "pieces", 1, [piece] * n_z)(place, moved)
    w, own, sends, from_far = then((w, own, sends, from_far))
    near = book_grad(w, ds, e, 0, width // 2, width, from_far)
    got, near = then(([to_peer(v, d) for d, v in enumerate(sends, 1)], near))
    (total,) = small(sum_body, "sums", n_z, [piece])(place, own, *got)
    w, total = then((w, total))
    near = book_grad(w, ds, e, width // 2, width // 2, width, from_far, near)
    ring = [total] + [to_peer(total, d) for d in range(1, n_z)]
    ring, near = then((ring, near))
    every = ring + [to_peer(v, 0, 1) for v in ring]
    quantized, grads = small(functools.partial(spread_body, n_z), "spread", n_code, [shaped(inputs.shape, BF16)] * 2)(
        place, *every
    )
    return quantized, grads, near[None]


def solution(mesh):
    in_specs = (P("sub", None), P("sub", None), P("sub", None, "code"))
    out_specs = (P("sub", None), P("sub", None), P("sub", None, "code"))
    body = functools.partial(local, mesh.shape["sub"], mesh.shape["code"])
    return jax.shard_map(body, mesh=mesh, in_specs=in_specs, out_specs=out_specs, check_vma=False)
```

time: 380 us -> 134 us (0.35); the launches traced: 376 us -> 134 us
  matrix products: 102 us -> 0 us
  blocking collectives: 102 us -> 0 us
  Pallas kernels: 0 us -> 84 us
  local copies, waits for them, and re-layouts: 60.4 us -> 6.05 us
  waiting for transfers between devices: 46.2 us -> 13.8 us
  other arithmetic: 25.6 us -> 0.07 us
  between operations: 14.2 us -> 0.75 us
  starting transfers between devices: 24.7 us -> 28.9 us
    dot_general x56 -> x0, matrix products: 102 us -> none  [the longest x8 23.5 us: step(): sb = score_scale * jnp.dot(xb, book, preferred_element_type=jnp.float32)]
    pallas_call x0 -> x10, Pallas kernels: none -> 84 us  [the longest x1 45.6 us: local_pass(): pl.pallas_call(functools.partial(local_pass_body, chunk, tiles), grid=(ti...]
    psum x2 -> x0, blocking collectives: 77.9 us -> none  [the longest x1 52 us: local(): grad_full = lax.psum(grad_cols, 'code').astype(jnp.bfloat16)]
    dynamic_update_slice x48 -> x0, local copies, waits for them, and re-layouts: 42.4 us -> none  [first_pass(): found = lax.map(one_block, blocks)]
    pmax x1 -> x0, blocking collectives: 24 us -> none  [local(): top = lax.pmax(top_c, 'code')]
    reduce_sum x16 -> x0, other arithmetic: 20.8 us -> none  [the longest x8 12 us: one_block(): total = jnp.sum(expo, axis=1)]
    all_to_all x4 -> x2, waiting for transfers between devices: 27.4 us -> 6.55 us  [the longest x1 6.54 us: local(): xg = lax.all_to_all(xg, 'sub', 0, 0, tiled=True)]
    psum x1 -> x0, waiting for transfers between devices: 18.8 us -> none  [local(): lax.psum((total_c * factor, part_c * factor[..., None]), 'code')]
  transfers between devices with their start and end apart: 5 -> 17, of which waited for: 4 -> 9; matrix products, arithmetic and copies ran while one was open for 31% -> 0% of each run, Pallas kernels for 0% -> 24%
where the time goes in v2:
time: 134 us
  Pallas kernels  84 us (63%)
  starting transfers between devices  28.9 us (22%)
  waiting for transfers between devices  13.8 us (10%)
  local copies, waits for them, and re-layouts  6.05 us (5%)
    pallas_call x1, Pallas kernels, local_pass(): pl.pallas_call(functools.partial(local_pass_body, chunk, tiles), grid=(ti...  45.6 us
    pallas_call x3, Pallas kernels, book_grad(): pl.pallas_call(book_body, grid=(width // tile,), in_specs=[pl.BlockSpec((...  29.1 us
    ppermute x15, starting transfers between devices, to_peer(): return lax.ppermute(v, 'code', pairs)  17.7 us
    ppermute x15, waiting for transfers between devices, to_peer(): return lax.ppermute(v, 'code', pairs)  7.3 us
    all_to_all x1, starting transfers between devices, local(): xg = lax.all_to_all(xg, 'sub', 0, 0, tiled=True)  6.84 us
    all_to_all x1, waiting for transfers between devices, local(): xg = lax.all_to_all(xg, 'sub', 0, 0, tiled=True)  6.54 us
    unnamed x10, local copies, waits for them, and re-layouts  6.05 us
    all_to_all x1, starting transfers between devices, local(): lax.all_to_all(out.reshape(n_sub, mine, LANES), 'sub', 0, 0, tiled=True)  4.34 us
  transfers between devices with their start and end apart: 17, of which 9 were waited for; matrix products, arithmetic and copies ran while one was open for 0% of the time, Pallas kernels for 24%

profile of v2, /device:TPU:1, one launch (start us, length us, event | category | flops | bytes accessed | tf_op | source)
XLA Modules:
  0.0 133.6 jit_solution(10981268829288612330)
XLA Ops:
  0.6 1.5 %collective-permute-start = (bf16[64,4096]{1,0:T(8,128)(2,1)}, bf16[64,4096]{1,0:T(8,128)(2,1)S(1)}, u32[]{:S(2)}, u32[]{:S(2)}) collective-permute-start(bf16[64,4096]{1,0:T(8,128)(2,1)} %bitcast.7), channel_id=1, source_target_pairs={{0,1},{1,0},{2,3},{3,2},{4,5},{5,4},{6,7},{7,6},{8,9},{9,8},{10,11... | collective-permute-start | bytes 1572872 | tf_op jit(solution)/shard_map/ppermute | solution.py:306
  2.1 0.1 pad_add_fusion.place_ref
  2.2 0.0 copy-start
  2.2 1.0 copy-done
  3.2 0.0 copy-start.1
  3.2 1.0 copy-done.1
  4.3 1.5 %pack.1 = bf16[16,128,128]{2,1,0:T(8,128)(2,1)} custom-call(s32[2]{0:T(128)S(1)} %pad_add_fusion.place_ref, bf16[256,1024]{1,0:T(8,128)(2,1)S(1)} %copy-done, bf16[256,1024]{1,0:T(8,128)(2,1)S(1)} %copy-done.1), custom_call_target="tpu_custom_call" | custom-call | flops 100000000 | bytes 2097152 | tf_op jit(solution)/shard_map/pack/pallas_call | solution.py:311
  5.8 6.8 %all-to-all-start = ((bf16[16,128,128]{2,1,0:T(8,128)(2,1)}), bf16[16,128,128]{2,1,0:T(8,128)(2,1)S(1)}, u32[]{:S(2)}, u32[]{:S(2)}) async-start(bf16[16,128,128]{2,1,0:T(8,128)(2,1)} %pack.1), calls=%async_computation | async-start | bytes 1048576 | tf_op jit(solution)/shard_map/all_to_all | solution.py:312
  12.7 0.0 collective-permute-done.mate_ref
  12.7 0.0 copy-start.2
  12.7 1.0 copy-done.2
  13.7 1.2 books.1
  14.9 0.0 copy-start.3
  14.9 1.3 copy-done.3
  16.3 6.5 %all-to-all-done = bf16[16,128,128]{2,1,0:T(8,128)(2,1)S(1)} async-done(((bf16[16,128,128]{2,1,0:T(8,128)(2,1)}), bf16[16,128,128]{2,1,0:T(8,128)(2,1)S(1)}, u32[]{:S(2)}, u32[]{:S(2)}) %all-to-all-start) | async-done | bytes 524320 | tf_op jit(solution)/shard_map/all_to_all | solution.py:312
  22.8 0.0 copy-start.4
  22.8 1.6 %copy-done.4 = bf16[8192,128]{1,0:T(8,128)(2,1)S(1)} copy-done((bf16[8192,128]{1,0:T(8,128)(2,1)S(1)}, bf16[8192,128]{1,0:T(8,128)(2,1)}, u32[]{:S(2)}) %copy-start.4) | copy-done | bytes 2097176
  24.4 45.6 %local_pass.1 = (bf16[2048,8192]{1,0:T(8,128)(2,1)}, bf16[2048,8192]{1,0:T(8,128)(2,1)}, f32[2048,128]{1,0:T(8,128)S(1)}, f32[2048,128]{1,0:T(8,128)S(1)}, f32[8...) custom-call(bf16[2048,128]{1,0:T(8,128)(2,1)S(1)} %bitcast.6, bf16[64,8192]{1,0:T(8,128)(2,1)S(1)} %get-tuple-element.38.book_ref, ...), custom_call_target="tpu_custom_call" | custom-call | flops 34359738368 | bytes 67108864 | tf_op jit(solution)/shard_map/local_pass/pallas_call | solution.py:177
  70.0 3.8 %collective-permute-start.3 = (f32[8,2048]{1,0:T(8,128)S(1)}, f32[8,2048]{1,0:T(8,128)S(1)}, u32[]{:S(2)}, u32[]{:S(2)}) collective-permute-start(f32[8,2048]{1,0:T(8,128)S(1)} %get-tuple-element.43.own_ref), channel_id=1, source_target_pairs={{0,6},{1,7},{2,0},{3,1},{4,2},{5,3},{6,4},{7,5},{8,14},{9,15},{10,... | collective-permute-start | bytes 196616 | tf_op jit(solution)/shard_map/ppermute | solution.py:306
  73.8 0.0 collective-permute-start.2
  73.8 0.7 collective-permute-start.1
  74.5 0.7 collective-permute-done.3.o3
  75.2 3.4 %collective-permute-done.2.o2 = f32[8,2048]{1,0:T(8,128)S(1)} collective-permute-done((f32[8,2048]{1,0:T(8,128)S(1)}, f32[8,2048]{1,0:T(8,128)S(1)}, u32[]{:S(2)}, u32[]{:S(2)}) %collective-permute-start.2) | collective-permute-done | bytes 65568 | tf_op jit(solution)/shard_map/ppermute | solution.py:306
  78.5 0.3 collective-permute-done.1.o1
  78.8 3.5 %mix.1 = (bf16[2048,128]{1,0:T(8,128)(2,1)}, bf16[128,2048]{1,0:T(8,128)(2,1)S(1)}) custom-call(f32[2048,128]{1,0:T(8,128)S(1)} %get-tuple-element.40.part_ref, f32[2048,128]{1,0:T(8,128)S(1)} %get-tuple-element.41.dx_ref, bf16[128,2048]{1,0:T(8,128)(2,1)S(1)} %get-tuple-element.42.xgt_ref, f32[8,2048]{1,0:T(8,128)S(1)} %get-tuple-element.43.own_ref, ...), custom_call_target="tpu_custom_call" | custom-call | flops 100000000 | bytes 4194304 | tf_op jit(solution)/shard_map/mix/pallas_call | solution.py:226
  82.3 4.3 %all-to-all-start.1 = ((bf16[16,128,128]{2,1,0:T(8,128)(2,1)}), bf16[16,128,128]{2,1,0:T(8,128)(2,1)S(1)}, u32[]{:S(2)}, u32[]{:S(2)}) async-start(bf16[16,128,128]{2,1,0:T(8,128)(2,1)} %bitcast.4), calls=%async_computation.1 | async-start | bytes 1048576 | tf_op jit(solution)/shard_map/all_to_all | solution.py:322
  86.7 12.8 %book_grad.3 = f32[64,4096]{1,0:T(8,128)S(1)} custom-call(bf16[128,2048]{1,0:T(8,128)(2,1)S(1)} %get-tuple-element.64.w_ref, bf16[2048,8192]{1,0:T(8,128)(2,1)} %get-tuple-element.46.ds_ref, bf16[2048,8192]{1,0:T(8,128)(2,1)} %get-tuple-element.47.e_ref), custom_call_target="tpu_custom_call" | custom-call | flops 8589934592 | bytes 33554432 | tf_op jit(solution)/shard_map/book_grad/pallas_call | solution.py:255
  99.5 0.0 all-to-all-done.1.a_ref
  99.5 3.0 %collective-permute-start.4 = (f32[64,4096]{1,0:T(8,128)S(1)}, f32[64,4096]{1,0:T(8,128)S(1)}, u32[]{:S(2)}, u32[]{:S(2)}) collective-permute-start(f32[64,4096]{1,0:T(8,128)S(1)} %book_grad.3), channel_id=1, source_target_pairs={{0,1},{1,0},{2,3},{3,2},{4,5},{5,4},{6,7},{7,6},{8,9},{9,8},{10,11... | collective-permute-start | bytes 3145736 | tf_op jit(solution)/shard_map/ppermute | solution.py:306
  102.5 0.6 pieces.1
  103.1 1.7 %collective-permute-done.4.rest_0_ = f32[64,4096]{1,0:T(8,128)S(1)} collective-permute-done((f32[64,4096]{1,0:T(8,128)S(1)}, f32[64,4096]{1,0:T(8,128)S(1)}, u32[]{:S(2)}, u32[]{:S(2)}) %collective-permute-start.4) | collective-permute-done | bytes 1048608 | tf_op jit(solution)/shard_map/ppermute | solution.py:306
  104.8 0.0 collective-permute-start.5
  104.8 1.8 %collective-permute-start.6 = (bf16[16,32,128]{2,1,0:T(8,128)(2,1)S(1)}, bf16[16,32,128]{2,1,0:T(8,128)(2,1)S(1)}, u32[]{:S(2)}, u32[]{:S(2)}) collective-permute-start(bf16[16,32,128]{2,1,0:T(8,128)(2,1)S(1)} %get-tuple-element.57), channel_id=1, source_target_pairs={{0,4},{1,5},{2,6},{3,7},{4,0},{5,1},{6,2},{7,3},{8,12},{9,13},{10,... | collective-permute-start | bytes 393224 | tf_op jit(solution)/shard_map/ppermute | solution.py:306
  106.6 1.6 %collective-permute-start.7 = (bf16[16,32,128]{2,1,0:T(8,128)(2,1)S(1)}, bf16[16,32,128]{2,1,0:T(8,128)(2,1)S(1)}, u32[]{:S(2)}, u32[]{:S(2)}) collective-permute-start(bf16[16,32,128]{2,1,0:T(8,128)(2,1)S(1)} %get-tuple-element.58), channel_id=1, source_target_pairs={{0,6},{1,7},{2,0},{3,1},{4,2},{5,3},{6,4},{7,5},{8,14},{9,15},{10,... | collective-permute-start | bytes 393224 | tf_op jit(solution)/shard_map/ppermute | solution.py:306
  108.2 8.2 %book_grad.4.rest_1_ = f32[64,4096]{1,0:T(8,128)} custom-call(bf16[128,2048]{1,0:T(8,128)(2,1)S(1)} %get-tuple-element.64.w_ref, bf16[2048,8192]{1,0:T(8,128)(2,1)} %get-tuple-element.46.ds_ref, bf16[2048,8192]{1,0:T(8,128)(2,1)} %get-tuple-element.47.e_ref, f32[64,4096]{1,0:T(8,128)S(1)} %collective-permute-done.4.rest_0_), custom_call_target="tpu_custom_call" | custom-call | flops 4294967296 | bytes 16777216 | tf_op jit(solution)/shard_map/book_grad/pallas_call | solution.py:255
  116.4 0.0 collective-permute-done.5.refs_1_
  116.4 0.0 collective-permute-done.6.refs_2_
  116.4 0.0 collective-permute-done.7.refs_3_
  116.4 0.6 sums.1.refs_0_
  117.0 0.9 collective-permute-start.10
  117.9 0.9 collective-permute-start.9
  118.8 0.8 collective-permute-start.8
  119.6 8.2 %book_grad.5 = f32[64,4096]{1,0:T(8,128)} custom-call(bf16[128,2048]{1,0:T(8,128)(2,1)S(1)} %get-tuple-element.64.w_ref, bf16[2048,8192]{1,0:T(8,128)(2,1)} %get-tuple-element.46.ds_ref, bf16[2048,8192]{1,0:T(8,128)(2,1)} %get-tuple-element.47.e_ref, f32[64,4096]{1,0:T(8,128)S(1)} %collective-permute-done.4.rest_0_, ...), custom_call_target="tpu_custom_call", output_to_operand_aliasing={{}: (4, {})} | custom-call | flops 4294967296 | bytes 16777216 | tf_op jit(solution)/shard_map/book_grad/pallas_call | solution.py:255
  127.8 0.0 collective-permute-done.10.refs_3_
  127.8 0.0 collective-permute-done.9.refs_2_
  127.8 0.0 collective-permute-done.8.refs_1_
  127.8 2.1 %collective-permute-start.11 = (bf16[16,32,128]{2,1,0:T(8,128)(2,1)S(1)}, bf16[16,32,128]{2,1,0:T(8,128)(2,1)S(1)}, u32[]{:S(2)}, u32[]{:S(2)}) collective-permute-start(bf16[16,32,128]{2,1,0:T(8,128)(2,1)S(1)} %sums.1.refs_0_), channel_id=1, source_target_pairs={{0,1},{1,0},{2,3},{3,2},{4,5},{5,4},{6,7},{7,6},{8,9},{9,8},{10,11... | collective-permute-start | bytes 393224 | tf_op jit(solution)/shard_map/ppermute | solution.py:306
  129.9 0.1 collective-permute-start.12
  130.0 0.4 collective-permute-start.13
  130.4 0.1 collective-permute-start.14
  130.5 0.4 collective-permute-done.11.refs_4_
  130.9 0.4 collective-permute-done.12.refs_5_
  131.3 0.2 collective-permute-done.13.refs_6_
  131.5 0.3 collective-permute-done.14.refs_7_
  131.8 1.8 %spread.1 = (bf16[256,1024]{1,0:T(8,128)(2,1)}, bf16[256,1024]{1,0:T(8,128)(2,1)}) custom-call(s32[2]{0:T(128)S(1)} %pad_add_fusion.place_ref, bf16[16,32,128]{2,1,0:T(8,128)(2,1)S(1)} %sums.1.refs_0_, bf16[16,32,128]{2,1,0:T(8,128)(2,1)S(1)} %collective-permute-done.8.refs_1_, bf16[16,32,128]{2,1,0:T(8,128)(2,1)S(1)} %collective-permute-done.9.refs_2_, ...), custom_call_target="tpu_custom_call" | custom-call | flops 100000000 | bytes 2097152 | tf_op jit(solution)/shard_map/spread/pallas_call | solution.py:337
Async XLA Ops:
  0.6 12.1 %collective-permute-start = (bf16[64,4096]{1,0:T(8,128)(2,1)}, bf16[64,4096]{1,0:T(8,128)(2,1)S(1)}, u32[]{:S(2)}, u32[]{:S(2)}) collective-permute-start(bf16[64,4096]{1,0:T(8,128)(2,1)} %bitcast.7), channel_id=1, source_target_pairs={{0,1},{1,0},{2,3},{3,2},{4,5},{5,4},{6,7},{7,6},{8,9},{9,8},{10,11... | collective-permute-start | bytes 1572872 | tf_op jit(solution)/shard_map/ppermute | solution.py:306
  2.2 1.0 copy-start
  3.2 1.0 copy-start.1
  5.8 17.0 %all-to-all-start = ((bf16[16,128,128]{2,1,0:T(8,128)(2,1)}), bf16[16,128,128]{2,1,0:T(8,128)(2,1)S(1)}, u32[]{:S(2)}, u32[]{:S(2)}) async-start(bf16[16,128,128]{2,1,0:T(8,128)(2,1)} %pack.1), calls=%async_computation | async-start | bytes 1048576 | tf_op jit(solution)/shard_map/all_to_all | solution.py:312
  12.7 1.0 copy-start.2
  14.9 1.3 %copy-start.3 = (bf16[8192,128]{1,0:T(8,128)(2,1)}, bf16[8192,128]{1,0:T(8,128)(2,1)S(1)}, u32[]{:S(2)}) copy-start(bf16[8192,128]{1,0:T(8,128)(2,1)S(1)} %get-tuple-element.39.bookt_ref) | copy-start | bytes 6291460
  22.8 1.6 %copy-start.4 = (bf16[8192,128]{1,0:T(8,128)(2,1)S(1)}, bf16[8192,128]{1,0:T(8,128)(2,1)}, u32[]{:S(2)}) copy-start(bf16[8192,128]{1,0:T(8,128)(2,1)} %copy-done.3) | copy-start | bytes 6291460
  70.0 5.1 %collective-permute-start.3 = (f32[8,2048]{1,0:T(8,128)S(1)}, f32[8,2048]{1,0:T(8,128)S(1)}, u32[]{:S(2)}, u32[]{:S(2)}) collective-permute-start(f32[8,2048]{1,0:T(8,128)S(1)} %get-tuple-element.43.own_ref), channel_id=1, source_target_pairs={{0,6},{1,7},{2,0},{3,1},{4,2},{5,3},{6,4},{7,5},{8,14},{9,15},{10,... | collective-permute-start | bytes 196616 | tf_op jit(solution)/shard_map/ppermute | solution.py:306
  73.8 4.7 %collective-permute-start.2 = (f32[8,2048]{1,0:T(8,128)S(1)}, f32[8,2048]{1,0:T(8,128)S(1)}, u32[]{:S(2)}, u32[]{:S(2)}) collective-permute-start(f32[8,2048]{1,0:T(8,128)S(1)} %get-tuple-element.43.own_ref), channel_id=1, source_target_pairs={{0,4},{1,5},{2,6},{3,7},{4,0},{5,1},{6,2},{7,3},{8,12},{9,13},{10,... | collective-permute-start | bytes 196616 | tf_op jit(solution)/shard_map/ppermute | solution.py:306
  73.8 5.0 %collective-permute-start.1 = (f32[8,2048]{1,0:T(8,128)S(1)}, f32[8,2048]{1,0:T(8,128)S(1)}, u32[]{:S(2)}, u32[]{:S(2)}) collective-permute-start(f32[8,2048]{1,0:T(8,128)S(1)} %get-tuple-element.43.own_ref), channel_id=1, source_target_pairs={{0,2},{1,3},{2,4},{3,5},{4,6},{5,7},{6,0},{7,1},{8,10},{9,11},{10,... | collective-permute-start | bytes 196616 | tf_op jit(solution)/shard_map/ppermute | solution.py:306
  82.3 17.1 %all-to-all-start.1 = ((bf16[16,128,128]{2,1,0:T(8,128)(2,1)}), bf16[16,128,128]{2,1,0:T(8,128)(2,1)S(1)}, u32[]{:S(2)}, u32[]{:S(2)}) async-start(bf16[16,128,128]{2,1,0:T(8,128)(2,1)} %bitcast.4), calls=%async_computation.1 | async-start | bytes 1048576 | tf_op jit(solution)/shard_map/all_to_all | solution.py:322
  99.5 5.3 %collective-permute-start.4 = (f32[64,4096]{1,0:T(8,128)S(1)}, f32[64,4096]{1,0:T(8,128)S(1)}, u32[]{:S(2)}, u32[]{:S(2)}) collective-permute-start(f32[64,4096]{1,0:T(8,128)S(1)} %book_grad.3), channel_id=1, source_target_pairs={{0,1},{1,0},{2,3},{3,2},{4,5},{5,4},{6,7},{7,6},{8,9},{9,8},{10,11... | collective-permute-start | bytes 3145736 | tf_op jit(solution)/shard_map/ppermute | solution.py:306
  104.8 11.6 %collective-permute-start.5 = (bf16[16,32,128]{2,1,0:T(8,128)(2,1)S(1)}, bf16[16,32,128]{2,1,0:T(8,128)(2,1)S(1)}, u32[]{:S(2)}, u32[]{:S(2)}) collective-permute-start(bf16[16,32,128]{2,1,0:T(8,128)(2,1)S(1)} %get-tuple-element.56), channel_id=1, source_target_pairs={{0,2},{1,3},{2,4},{3,5},{4,6},{5,7},{6,0},{7,1},{8,10},{9,11},{10,... | collective-permute-start | bytes 393224 | tf_op jit(solution)/shard_map/ppermute | solution.py:306
  104.8 11.6 %collective-permute-start.6 = (bf16[16,32,128]{2,1,0:T(8,128)(2,1)S(1)}, bf16[16,32,128]{2,1,0:T(8,128)(2,1)S(1)}, u32[]{:S(2)}, u32[]{:S(2)}) collective-permute-start(bf16[16,32,128]{2,1,0:T(8,128)(2,1)S(1)} %get-tuple-element.57), channel_id=1, source_target_pairs={{0,4},{1,5},{2,6},{3,7},{4,0},{5,1},{6,2},{7,3},{8,12},{9,13},{10,... | collective-permute-start | bytes 393224 | tf_op jit(solution)/shard_map/ppermute | solution.py:306
  106.6 9.8 %collective-permute-start.7 = (bf16[16,32,128]{2,1,0:T(8,128)(2,1)S(1)}, bf16[16,32,128]{2,1,0:T(8,128)(2,1)S(1)}, u32[]{:S(2)}, u32[]{:S(2)}) collective-permute-start(bf16[16,32,128]{2,1,0:T(8,128)(2,1)S(1)} %get-tuple-element.58), channel_id=1, source_target_pairs={{0,6},{1,7},{2,0},{3,1},{4,2},{5,3},{6,4},{7,5},{8,14},{9,15},{10,... | collective-permute-start | bytes 393224 | tf_op jit(solution)/shard_map/ppermute | solution.py:306
  117.0 10.8 %collective-permute-start.10 = (bf16[16,32,128]{2,1,0:T(8,128)(2,1)S(1)}, bf16[16,32,128]{2,1,0:T(8,128)(2,1)S(1)}, u32[]{:S(2)}, u32[]{:S(2)}) collective-permute-start(bf16[16,32,128]{2,1,0:T(8,128)(2,1)S(1)} %sums.1.refs_0_), channel_id=1, source_target_pairs={{0,6},{1,7},{2,0},{3,1},{4,2},{5,3},{6,4},{7,5},{8,14},{9,15},{10,... | collective-permute-start | bytes 393224 | tf_op jit(solution)/shard_map/ppermute | solution.py:306
  117.9 9.9 %collective-permute-start.9 = (bf16[16,32,128]{2,1,0:T(8,128)(2,1)S(1)}, bf16[16,32,128]{2,1,0:T(8,128)(2,1)S(1)}, u32[]{:S(2)}, u32[]{:S(2)}) collective-permute-start(bf16[16,32,128]{2,1,0:T(8,128)(2,1)S(1)} %sums.1.refs_0_), channel_id=1, source_target_pairs={{0,4},{1,5},{2,6},{3,7},{4,0},{5,1},{6,2},{7,3},{8,12},{9,13},{10,... | collective-permute-start | bytes 393224 | tf_op jit(solution)/shard_map/ppermute | solution.py:306
  118.8 9.0 %collective-permute-start.8 = (bf16[16,32,128]{2,1,0:T(8,128)(2,1)S(1)}, bf16[16,32,128]{2,1,0:T(8,128)(2,1)S(1)}, u32[]{:S(2)}, u32[]{:S(2)}) collective-permute-start(bf16[16,32,128]{2,1,0:T(8,128)(2,1)S(1)} %sums.1.refs_0_), channel_id=1, source_target_pairs={{0,2},{1,3},{2,4},{3,5},{4,6},{5,7},{6,0},{7,1},{8,10},{9,11},{10,... | collective-permute-start | bytes 393224 | tf_op jit(solution)/shard_map/ppermute | solution.py:306
  127.8 3.1 %collective-permute-start.11 = (bf16[16,32,128]{2,1,0:T(8,128)(2,1)S(1)}, bf16[16,32,128]{2,1,0:T(8,128)(2,1)S(1)}, u32[]{:S(2)}, u32[]{:S(2)}) collective-permute-start(bf16[16,32,128]{2,1,0:T(8,128)(2,1)S(1)} %sums.1.refs_0_), channel_id=1, source_target_pairs={{0,1},{1,0},{2,3},{3,2},{4,5},{5,4},{6,7},{7,6},{8,9},{9,8},{10,11... | collective-permute-start | bytes 393224 | tf_op jit(solution)/shard_map/ppermute | solution.py:306
  129.9 1.3 %collective-permute-start.12 = (bf16[16,32,128]{2,1,0:T(8,128)(2,1)S(1)}, bf16[16,32,128]{2,1,0:T(8,128)(2,1)S(1)}, u32[]{:S(2)}, u32[]{:S(2)}) collective-permute-start(bf16[16,32,128]{2,1,0:T(8,128)(2,1)S(1)} %collective-permute-done.8.refs_1_), channel_id=1, source_target_pairs={{0,1},{1,0},{2,3},{3,2},{4,5},{5,4},{6,7},{7,6},{8,9},{9,8},{10,11... | collective-permute-start | bytes 393224 | tf_op jit(solution)/shard_map/ppermute | solution.py:306
  130.0 1.4 %collective-permute-start.13 = (bf16[16,32,128]{2,1,0:T(8,128)(2,1)S(1)}, bf16[16,32,128]{2,1,0:T(8,128)(2,1)S(1)}, u32[]{:S(2)}, u32[]{:S(2)}) collective-permute-start(bf16[16,32,128]{2,1,0:T(8,128)(2,1)S(1)} %collective-permute-done.9.refs_2_), channel_id=1, source_target_pairs={{0,1},{1,0},{2,3},{3,2},{4,5},{5,4},{6,7},{7,6},{8,9},{9,8},{10,11... | collective-permute-start | bytes 393224 | tf_op jit(solution)/shard_map/ppermute | solution.py:306
  130.4 1.3 %collective-permute-start.14 = (bf16[16,32,128]{2,1,0:T(8,128)(2,1)S(1)}, bf16[16,32,128]{2,1,0:T(8,128)(2,1)S(1)}, u32[]{:S(2)}, u32[]{:S(2)}) collective-permute-start(bf16[16,32,128]{2,1,0:T(8,128)(2,1)S(1)} %collective-permute-done.10.refs_3_), channel_id=1, source_target_pairs={{0,1},{1,0},{2,3},{3,2},{4,5},{5,4},{6,7},{7,6},{8,9},{9,8},{10,11... | collective-permute-start | bytes 393224 | tf_op jit(solution)/shard_map/ppermute | solution.py:306

commit v3 on v2

v3 whole, which is shorter than its diff:
```python
import functools

import jax
import jax.numpy as jnp
from jax import lax
from jax.experimental import pallas as pl
from jax.experimental.pallas import tpu as pltpu
from jax.sharding import PartitionSpec as P

BF16 = jnp.bfloat16
F32 = jnp.float32
DS = 64
LANES = 128
SCALE = 0.25
LOG2E = 1.4426950408889634
MIB = 2**20
PASS_MIB = 34
WHOLE = pl.BlockSpec(memory_space=pltpu.VMEM)
FAR = pl.BlockSpec(memory_space=pltpu.HBM)
SCALAR = pl.BlockSpec(memory_space=pltpu.SMEM)


def span(start, size):
    return pl.ds(pl.multiple_of(start, size), size)


def small(body, name, n_in, outs, flops=10**8):
    return pl.pallas_call(
        body,
        in_specs=[SCALAR] + [WHOLE] * n_in,
        out_specs=[WHOLE] * len(outs),
        out_shape=outs,
        compiler_params=pltpu.CompilerParams(vmem_limit_bytes=12 * MIB),
        cost_estimate=pl.CostEstimate(flops=flops, bytes_accessed=2**21, transcendentals=0),
        name=name,
    )


def pack_body(place_ref, x_hbm, g_hbm, out_ref, x_ref, g_ref, sems):
    subs, rows, _ = out_ref.shape
    at = span(place_ref[0] * rows, rows)
    copies = [
        pltpu.make_async_copy(src.at[at], dst, sems.at[k])
        for k, (src, dst) in enumerate(((x_hbm, x_ref), (g_hbm, g_ref)))
    ]
    for copy in copies:
        copy.start()
    for copy in copies:
        copy.wait()
    for k in range(0, subs, 2):
        cols = slice(k * DS, (k + 2) * DS)
        x, g = x_ref[:, cols], g_ref[:, cols]
        out_ref[k] = jnp.concatenate([x[:, :DS], g[:, :DS]], axis=1)
        out_ref[k + 1] = jnp.concatenate([x[:, DS:], g[:, DS:]], axis=1)


def pack(place, x, g, subs):
    rows, width = x.shape[0] // 2, x.shape[1]
    far = lambda v: pltpu.with_memory_space_constraint(v, pltpu.HBM)
    return pl.pallas_call(
        pack_body,
        in_specs=[SCALAR, FAR, FAR],
        out_specs=WHOLE,
        out_shape=jax.ShapeDtypeStruct((subs, rows, LANES), BF16),
        scratch_shapes=[pltpu.VMEM((rows, width), BF16)] * 2 + [pltpu.SemaphoreType.DMA((2,))],
        compiler_params=pltpu.CompilerParams(vmem_limit_bytes=8 * MIB),
        cost_estimate=pl.CostEstimate(flops=10**8, bytes_accessed=2**21, transcendentals=0),
        name="pack",
    )(place, far(x), far(g))


def book_body_prep(place_ref, own_ref, mate_ref, book_ref, bookt_ref):
    width = own_ref.shape[1]
    step = 512
    lane = lax.broadcasted_iota(jnp.int32, (step, LANES), 1)
    for n, ref in enumerate((own_ref, mate_ref)):
        book_ref[:, n * width : (n + 1) * width] = ref[...]
        for c in range(0, width, step):
            v = ref[:, c : c + step].astype(F32)
            turned = jnp.concatenate([v, jnp.zeros_like(v)], axis=0).T
            bookt_ref[n * width + c : n * width + c + step, :] = jnp.where(lane == DS, 1.0, turned).astype(BF16)


def local_pass_body(chunk, parts, xg_ref, book_ref, bookt_ref, *rest):
    e_refs, rest = rest[: len(parts)], rest[len(parts) :]
    ds_hbm, part_ref, dx_ref, stat_ref, xgt_ref, *scratch = rest
    s_slots, m_slots, gq_slots, d_slots, ds_slots, e_slots = (scratch[k : k + 2] for k in range(0, 12, 2))
    e_sems, ds_sems = scratch[12:]
    tile, codes = s_slots[0].shape
    tiles = xg_ref.shape[0] // tile
    steps = codes // chunk
    rows = lambda t: span(t * tile, tile)

    def e_at(t, n, c):
        for ref, (first, width, kept, place) in zip(e_refs, parts):
            at = c * chunk - first
            if 0 <= at < width:
                if kept:
                    return ref, (rows(t), slice(at, at + chunk))
                return e_slots[n], (slice(None), slice(place + at, place + at + chunk))

    def e_copies(t, n):
        return [
            pltpu.make_async_copy(e_slots[n].at[:, place : place + width], ref.at[rows(t)], e_sems.at[n, k])
            for k, (ref, (_, width, kept, place)) in enumerate(zip(e_refs, parts))
            if not kept
        ]

    def ds_copy(t, n):
        return pltpu.make_async_copy(ds_slots[n], ds_hbm.at[rows(t)], ds_sems.at[n])

    def look(t, n):
        x = xg_ref[rows(t), :][:, :DS]
        most = None

        def one(c):
            nonlocal most
            if c == steps:
                return
            s = jnp.dot(x, book_ref[:, c * chunk : (c + 1) * chunk], preferred_element_type=F32)
            s_slots[n][:, c * chunk : (c + 1) * chunk] = s
            for k in range(0, chunk, LANES):
                piece = s[:, k : k + LANES]
                most = piece if most is None else jnp.maximum(most, piece)

        def end():
            top = jnp.max(most, axis=1, keepdims=True) * (SCALE * LOG2E)
            m_slots[n][...] = jnp.broadcast_to(top, (tile, LANES))

        return one, end

    def weigh(t, n):
        top = m_slots[n][...]
        wide = jnp.concatenate([top] * (chunk // LANES), axis=1)
        acc = jnp.zeros((tile, LANES), F32)

        def one(c):
            nonlocal acc
            if c == steps:
                return
            at = slice(c * chunk, (c + 1) * chunk)
            e = jnp.exp2(s_slots[n][:, at] * (SCALE * LOG2E) - wide).astype(BF16)
            ref, place = e_at(t, n, c)
            ref[place] = e
            acc = acc + jnp.dot(e, bookt_ref[at, :], preferred_element_type=F32)

        def end():
            part_ref[rows(t), :] = acc
            lane = lax.broadcasted_iota(jnp.int32, (tile, LANES), 1)
            total = jnp.sum(jnp.where(lane == DS, acc, 0.0), axis=1, keepdims=True)
            xg = xg_ref[rows(t), :]
            h = jnp.sum(acc[:, :DS] * xg[:, DS:].astype(F32), axis=1, keepdims=True)
            gq = h / total
            gq_slots[n][...] = jnp.broadcast_to(gq, (tile, LANES))
            stat = jnp.where(lane == 0, top, jnp.where(lane == 1, total, jnp.where(lane == 2, h, gq)))
            stat_ref[:, rows(t)] = stat.T[:8]
            xgt_ref[:, rows(t)] = xg.T
            for copy in e_copies(t, n):
                copy.start()

        return one, end

    def lean(t, n):
        g = xg_ref[rows(t), :][:, DS:]
        wide = jnp.concatenate([gq_slots[n][...]] * (chunk // LANES), axis=1)
        acc = jnp.zeros((tile, LANES), F32)

        def one(c):
            nonlocal acc
            if c < steps:
                at = slice(c * chunk, (c + 1) * chunk)
                d_slots[c % 2][...] = jnp.dot(g, book_ref[:, at], preferred_element_type=F32) - wide
            if c > 0:
                at = slice((c - 1) * chunk, c * chunk)
                ref, place = e_at(t, n, c - 1)
                ds = (d_slots[(c - 1) % 2][...] * ref[place].astype(F32)).astype(BF16)
                ds_slots[n][:, at] = ds
                acc = acc + jnp.dot(ds, bookt_ref[at, :], preferred_element_type=F32)

        def end():
            dx_ref[rows(t), :] = acc
            ds_copy(t, n).start()

        return one, end

    def wait_e(t, n):
        for copy in e_copies(t, n):
            copy.wait()

    def run(*works):
        for c in range(steps + 1):
            for one, _ in works:
                one(c)
        for _, end in works:
            end()

    run(look(0, 0))
    run(look(1, 1), weigh(0, 0))

    def two(i, carry):
        for n in range(2):
            t = 2 + 2 * i + n
            if n == 0:

                @pl.when(i > 0)
                def _():
                    wait_e(t - 3, 1)
                    ds_copy(t - 4, 0).wait()

            else:
                wait_e(t - 3, 0)

                @pl.when(i > 0)
                def _():
                    ds_copy(t - 4, 1).wait()

            run(look(t, n), weigh(t - 1, 1 - n), lean(t - 2, n))
        return carry

    lax.fori_loop(0, tiles // 2 - 1, two, 0)
    wait_e(tiles - 3, 1)
    ds_copy(tiles - 4, 0).wait()
    run(weigh(tiles - 1, 1), lean(tiles - 2, 0))
    ds_copy(tiles - 3, 1).wait()
    run(lean(tiles - 1, 1))
    wait_e(tiles - 2, 0)
    wait_e(tiles - 1, 1)
    ds_copy(tiles - 2, 0).wait()
    ds_copy(tiles - 1, 1).wait()


def local_pass(xg, book, bookt, parts, tile=128, chunk=1024):
    rows, codes = xg.shape[0], book.shape[1]
    pairs = rows * codes
    staged, placed = 0, []
    for first, width, kept in parts:
        placed.append((first, width, kept, staged))
        staged += 0 if kept else width
    wide, narrow, short = pltpu.VMEM((tile, codes), F32), pltpu.VMEM((tile, LANES), F32), pltpu.VMEM((tile, codes), BF16)
    return pl.pallas_call(
        functools.partial(local_pass_body, chunk, tuple(placed)),
        in_specs=[WHOLE] * 3,
        out_specs=[WHOLE if kept else FAR for _, _, kept in parts] + [FAR] + [WHOLE] * 4,
        out_shape=[(pltpu.VMEM if kept else pltpu.HBM)((rows, width), BF16) for _, width, kept in parts]
        + [
            pltpu.HBM((rows, codes), BF16),
            jax.ShapeDtypeStruct((rows, LANES), F32),
            jax.ShapeDtypeStruct((rows, LANES), F32),
            jax.ShapeDtypeStruct((8, rows), F32),
            jax.ShapeDtypeStruct((LANES, rows), BF16),
        ],
        scratch_shapes=[wide, wide, narrow, narrow, narrow, narrow]
        + [pltpu.VMEM((tile, chunk), F32)] * 2
        + [short, short]
        + [pltpu.VMEM((tile, max(staged, LANES)), BF16)] * 2
        + [pltpu.SemaphoreType.DMA((2, len(parts))), pltpu.SemaphoreType.DMA((2,))],
        compiler_params=pltpu.CompilerParams(vmem_limit_bytes=PASS_MIB * MIB),
        cost_estimate=pl.CostEstimate(flops=pairs * 2048, bytes_accessed=pairs * 4, transcendentals=pairs),
        name="local_pass",
    )(xg, book, bookt)


def mix_body(part_ref, dx_ref, xgt_ref, own_ref, o1, o2, o3, out_ref, w_ref):
    rows = part_ref.shape[0]
    stats = [r[...] for r in (own_ref, o1, o2, o3)]
    top = functools.reduce(jnp.maximum, [s[0:1] for s in stats])
    rel = [jnp.exp2(s[0:1] - top) for s in stats]
    z = sum(r * s[1:2] for r, s in zip(rel, stats))
    gq = sum(r * s[2:3] for r, s in zip(rel, stats)) / z
    f_row = rel[0] / z
    off_row = stats[0][3:4] - gq
    x, g = xgt_ref[:DS].astype(F32), xgt_ref[DS:].astype(F32)
    w_ref[:DS] = (x * (SCALE * f_row)).astype(BF16)
    w_ref[DS:] = ((g + (SCALE * off_row) * x) * f_row).astype(BF16)
    step = LANES
    sub = lax.broadcasted_iota(jnp.int32, (8, step), 0)
    for r in range(0, rows, step):
        at = slice(r, r + step)
        turned = jnp.where(sub == 0, f_row[:, at], off_row[:, at]).T
        f, off = turned[:, 0:1], turned[:, 1:2]
        part = part_ref[at, :]
        q = (part * f)[:, :DS]
        dx = ((dx_ref[at, :] + part * off) * (SCALE * f))[:, :DS]
        out_ref[at, :] = jnp.concatenate([q, dx], axis=1).astype(BF16)


def mix(part, dx, xgt, stats):
    rows = part.shape[0]
    return pl.pallas_call(
        mix_body,
        in_specs=[WHOLE] * 7,
        out_specs=[WHOLE] * 2,
        out_shape=[jax.ShapeDtypeStruct((rows, LANES), BF16), jax.ShapeDtypeStruct((LANES, rows), BF16)],
        compiler_params=pltpu.CompilerParams(vmem_limit_bytes=12 * MIB),
        cost_estimate=pl.CostEstimate(flops=10**8, bytes_accessed=2**22, transcendentals=0),
        name="mix",
    )(part, dx, xgt, *stats)


def book_body(first, tile, kept, extra, w_ref, ds_hbm, e_ref, *rest):
    out_ref = rest[extra]

    def one(ds_ref, *more):
        at = span(pl.program_id(0) * tile, tile)
        e = e_ref[:, at] if kept else more[0][...]
        grad = jnp.dot(w_ref[:DS], ds_ref[...], preferred_element_type=F32)
        grad += jnp.dot(w_ref[DS:], e, preferred_element_type=F32)
        if extra:
            grad += rest[0][:, at]
        out_ref[:, at] = grad

    rows, width = e_ref.shape
    specs = [pl.BlockSpec((rows, tile), lambda t: (0, first // tile + t))]
    if not kept:
        specs.append(pl.BlockSpec((rows, tile), lambda t: (0, t)))
    pltpu.emit_pipeline(one, grid=(width // tile,), in_specs=specs)(ds_hbm, *([] if kept else [e_ref]))


def book_grad(w, ds, e, part, other=None):
    first, width, kept = part
    tile = 1024 if width > 2048 else 512
    rows = e.shape[0]
    pairs = rows * width
    more = [] if other is None else [other]
    space = pltpu.VMEM if kept else pltpu.HBM
    return pl.pallas_call(
        functools.partial(book_body, first, tile, kept, len(more)),
        in_specs=[WHOLE, FAR, WHOLE if kept else FAR] + [WHOLE] * len(more),
        out_specs=WHOLE,
        out_shape=jax.ShapeDtypeStruct((DS, width), F32),
        compiler_params=pltpu.CompilerParams(vmem_limit_bytes=(14 if kept else 24) * MIB),
        cost_estimate=pl.CostEstimate(flops=pairs * 1024, bytes_accessed=pairs * 4, transcendentals=0),
        name="book_grad",
    )(w, pltpu.with_memory_space_constraint(ds, pltpu.HBM), pltpu.with_memory_space_constraint(e, space), *more)


def pieces_body(n_z, place_ref, a_ref, own_ref, *send_refs):
    part = own_ref.shape[1]
    for d, out in enumerate((own_ref, *send_refs)):
        out[...] = a_ref[:, span(lax.rem(place_ref[1] + d, n_z) * part, part)]


def sum_body(place_ref, *refs):
    *ins, out = refs
    out[...] = sum(r[...].astype(F32) for r in ins).astype(BF16)


def spread_body(n_z, place_ref, near_1, near_2, from_far, *refs):
    *ins, q_ref, dx_ref, book_ref = refs
    width = near_1.shape[1]
    book_ref[:, :width] = near_1[...] + from_far[:, :width]
    book_ref[:, width:] = near_2[...] + from_far[:, width:]
    subs, part, _ = ins[0].shape
    for n, ref in enumerate(ins):
        swap, d = n // n_z, n % n_z
        core = place_ref[0] if swap == 0 else 1 - place_ref[0]
        at = span((core * n_z + lax.rem(place_ref[1] + n_z - d, n_z)) * part, part)
        for k in range(0, subs, 2):
            a, b = ref[k], ref[k + 1]
            cols = slice(k * DS, (k + 2) * DS)
            q_ref[at, cols] = jnp.concatenate([a[:, :DS], b[:, :DS]], axis=1)
            dx_ref[at, cols] = jnp.concatenate([a[:, DS:], b[:, DS:]], axis=1)


def local(n_sub, n_code, inputs, upstream, codebook):
    n_z = n_code // 2
    index = lax.axis_index("code")
    place = jnp.stack([index % 2, index // 2]).astype(jnp.int32)
    n_rows, width_all = inputs.shape
    mine = n_rows // 2
    shaped = jax.ShapeDtypeStruct
    then = lax.optimization_barrier

    def to_peer(v, d, swap=0):
        pairs = [(j, ((j // 2 + d) % n_z) * 2 + (j % 2 ^ swap)) for j in range(n_code)]
        return lax.ppermute(v, "code", pairs)

    own_book = codebook[0]
    width = own_book.shape[1]
    mate_book = to_peer(own_book, 0, 1)
    xg = pack(place, inputs, upstream, n_sub)
    xg = lax.all_to_all(xg, "sub", 0, 0, tiled=True)
    book, bookt = small(
        book_body_prep, "books", 2, [shaped((DS, 2 * width), BF16), shaped((2 * width, LANES), BF16)], 10**10
    )(place, own_book, mate_book)

    xg = xg.reshape(n_sub * mine, LANES)
    parts = [(width, width, False), (0, width // 2, False), (width // 2, width // 2, False)]
    *es, ds, part, dxl, stat, xgt = local_pass(xg, book, bookt, parts)
    stats = [stat] + [to_peer(stat, d) for d in range(1, n_z)]
    out, w = mix(part, dxl, xgt, stats)

    moved = lax.all_to_all(out.reshape(n_sub, mine, LANES), "sub", 0, 0, tiled=True)
    far = book_grad(w, ds, es[0], parts[0])
    moved, far = then((moved, far))
    from_far = to_peer(far, 0, 1)
    piece = shaped((n_sub, mine // n_z, LANES), BF16)
    own, *sends = small(functools.partial(pieces_body, n_z), "pieces", 1, [piece] * n_z)(place, moved)
    w, own, sends = then((w, own, sends))
    near_1 = book_grad(w, ds, es[1], parts[1])
    got, near_1 = then(([to_peer(v, d) for d, v in enumerate(sends, 1)], near_1))
    (total,) = small(sum_body, "sums", n_z, [piece])(place, own, *got)
    w, total = then((w, total))
    near_2 = book_grad(w, ds, es[2], parts[2])
    ring = [total] + [to_peer(total, d) for d in range(1, n_z)]
    ring, near_2 = then((ring, near_2))
    every = ring + [to_peer(v, 0, 1) for v in ring]
    quantized, grads, grad_book = small(
        functools.partial(spread_body, n_z),
        "spread",
        n_code + 3,
        [shaped(inputs.shape, BF16)] * 2 + [shaped((DS, width), F32)],
    )(place, near_1, near_2, from_far, *every)
    return quantized, grads, grad_book[None]


def solution(mesh):
    in_specs = (P("sub", None), P("sub", None), P("sub", None, "code"))
    out_specs = (P("sub", None), P("sub", None), P("sub", None, "code"))
    body = functools.partial(local, mesh.shape["sub"], mesh.shape["code"])
    return jax.shard_map(body, mesh=mesh, in_specs=in_specs, out_specs=out_specs, check_vma=False)
```

time: 134 us -> 128 us (0.955)
  Pallas kernels: 84 us -> 81.8 us
  local copies, waits for them, and re-layouts: 6.05 us -> 3.95 us
    pallas_call x6, Pallas kernels: 78.2 us -> 75.8 us  [the longest x1 42.9 us: local_pass(): pl.pallas_call(functools.partial(local_pass_body, chunk, tuple(placed)),...]
    unnamed x10 -> x6, local copies, waits for them, and re-layouts: 6.05 us -> 3.95 us
  transfers between devices with their start and end apart: 17 -> 17, of which waited for: 9 -> 9; matrix products, arithmetic and copies ran while one was open for 0% -> 0% of each run, Pallas kernels for 24% -> 26%
where the time goes in v3:
time: 128 us; the launch traced here: 127 us
  Pallas kernels  81.8 us (64%)
  starting transfers between devices  28 us (22%)
  waiting for transfers between devices  12.8 us (10%)
  local copies, waits for them, and re-layouts  3.95 us (3%)
    pallas_call x1, Pallas kernels, local_pass(): pl.pallas_call(functools.partial(local_pass_body, chunk, tuple(placed)),...  42.9 us
    pallas_call x3, Pallas kernels, book_grad(): pl.pallas_call(functools.partial(book_body, first, tile, kept, len(more))...  28.1 us
    ppermute x15, starting transfers between devices, to_peer(): return lax.ppermute(v, 'code', pairs)  16.8 us
    all_to_all x1, starting transfers between devices, local(): xg = lax.all_to_all(xg, 'sub', 0, 0, tiled=True)  6.85 us
    all_to_all x1, waiting for transfers between devices, local(): xg = lax.all_to_all(xg, 'sub', 0, 0, tiled=True)  6.56 us
    ppermute x15, waiting for transfers between devices, to_peer(): return lax.ppermute(v, 'code', pairs)  6.28 us
    all_to_all x1, starting transfers between devices, local(): lax.all_to_all(out.reshape(n_sub, mine, LANES), 'sub', 0, 0, tiled=True)  4.35 us
    unnamed x6, local copies, waits for them, and re-layouts  3.95 us
  transfers between devices with their start and end apart: 17, of which 9 were waited for; matrix products, arithmetic and copies ran while one was open for 0% of the time, Pallas kernels for 26%

profile of v3, /device:TPU:1, one launch (start us, length us, event | category | flops | bytes accessed | tf_op | source)
XLA Modules:
  0.0 127.4 jit_solution(9889538059406492988)
XLA Ops:
  0.6 1.5 %collective-permute-start = (bf16[64,4096]{1,0:T(8,128)(2,1)}, bf16[64,4096]{1,0:T(8,128)(2,1)S(1)}, u32[]{:S(2)}, u32[]{:S(2)}) collective-permute-start(bf16[64,4096]{1,0:T(8,128)(2,1)} %bitcast.7), channel_id=1, source_target_pairs={{0,1},{1,0},{2,3},{3,2},{4,5},{5,4},{6,7},{7,6},{8,9},{9,8},{10,11... | collective-permute-start | bytes 1572872 | tf_op jit(solution)/shard_map/ppermute | solution.py:376
  2.1 0.1 pad_add_fusion.place_ref
  2.2 2.6 %pack.1 = bf16[16,128,128]{2,1,0:T(8,128)(2,1)} custom-call(s32[2]{0:T(128)S(1)} %pad_add_fusion.place_ref, bf16[256,1024]{1,0:T(8,128)(2,1)} %x_hbm.1, bf16[256,1024]{1,0:T(8,128)(2,1)} %g_hbm.1), custom_call_target="tpu_custom_call" | custom-call | flops 100000000 | bytes 2097152 | tf_op jit(solution)/shard_map/pack/pallas_call | solution.py:60
  4.8 6.8 %all-to-all-start = ((bf16[16,128,128]{2,1,0:T(8,128)(2,1)}), bf16[16,128,128]{2,1,0:T(8,128)(2,1)S(1)}, u32[]{:S(2)}, u32[]{:S(2)}) async-start(bf16[16,128,128]{2,1,0:T(8,128)(2,1)} %pack.1), calls=%async_computation | async-start | bytes 1048576 | tf_op jit(solution)/shard_map/all_to_all | solution.py:382
  11.7 0.0 collective-permute-done.mate_ref
  11.7 0.0 copy-start
  11.7 1.0 copy-done
  12.7 1.2 books.1
  13.9 0.0 copy-start.1
  13.9 1.3 %copy-done.1 = bf16[8192,128]{1,0:T(8,128)(2,1)} copy-done((bf16[8192,128]{1,0:T(8,128)(2,1)}, bf16[8192,128]{1,0:T(8,128)(2,1)S(1)}, u32[]{:S(2)}) %copy-start.1) | copy-done | bytes 2097176
  15.2 6.6 %all-to-all-done = bf16[16,128,128]{2,1,0:T(8,128)(2,1)S(1)} async-done(((bf16[16,128,128]{2,1,0:T(8,128)(2,1)}), bf16[16,128,128]{2,1,0:T(8,128)(2,1)S(1)}, u32[]{:S(2)}, u32[]{:S(2)}) %all-to-all-start) | async-done | bytes 524320 | tf_op jit(solution)/shard_map/all_to_all | solution.py:382
  21.8 0.0 copy-start.2
  21.8 1.6 %copy-done.2 = bf16[8192,128]{1,0:T(8,128)(2,1)S(1)} copy-done((bf16[8192,128]{1,0:T(8,128)(2,1)S(1)}, bf16[8192,128]{1,0:T(8,128)(2,1)}, u32[]{:S(2)}) %copy-start.2) | copy-done | bytes 2097176
  23.4 42.9 %local_pass.1 = (bf16[2048,4096]{1,0:T(8,128)(2,1)}, bf16[2048,2048]{1,0:T(8,128)(2,1)}, bf16[2048,2048]{1,0:T(8,128)(2,1)}, bf16[2048,8192]{1,0:T(8,128)(2,1)},...) custom-call(bf16[2048,128]{1,0:T(8,128)(2,1)S(1)} %bitcast.6, ...), custom_call_target="tpu_custom_call" | custom-call | flops 34359738368 | bytes 67108864 | tf_op jit(solution)/shard_map/local_pass/pallas_call | solution.py:240
  66.3 3.8 %collective-permute-start.3 = (f32[8,2048]{1,0:T(8,128)S(1)}, f32[8,2048]{1,0:T(8,128)S(1)}, u32[]{:S(2)}, u32[]{:S(2)}) collective-permute-start(f32[8,2048]{1,0:T(8,128)S(1)} %get-tuple-element.45.own_ref), channel_id=1, source_target_pairs={{0,6},{1,7},{2,0},{3,1},{4,2},{5,3},{6,4},{7,5},{8,14},{9,15},{10,... | collective-permute-start | bytes 196616 | tf_op jit(solution)/shard_map/ppermute | solution.py:376
  70.1 0.0 collective-permute-start.2
  70.1 0.7 collective-permute-start.1
  70.8 0.6 collective-permute-done.3.o3
  71.4 3.4 %collective-permute-done.2.o2 = f32[8,2048]{1,0:T(8,128)S(1)} collective-permute-done((f32[8,2048]{1,0:T(8,128)S(1)}, f32[8,2048]{1,0:T(8,128)S(1)}, u32[]{:S(2)}, u32[]{:S(2)}) %collective-permute-start.2) | collective-permute-done | bytes 65568 | tf_op jit(solution)/shard_map/ppermute | solution.py:376
  74.8 0.3 collective-permute-done.1.o1
  75.1 3.6 %mix.1 = (bf16[2048,128]{1,0:T(8,128)(2,1)}, bf16[128,2048]{1,0:T(8,128)(2,1)S(1)}) custom-call(f32[2048,128]{1,0:T(8,128)S(1)} %get-tuple-element.42.part_ref, f32[2048,128]{1,0:T(8,128)S(1)} %get-tuple-element.43.dx_ref, bf16[128,2048]{1,0:T(8,128)(2,1)S(1)} %get-tuple-element.44.xgt_ref, f32[8,2048]{1,0:T(8,128)S(1)} %get-tuple-element.45.own_ref, ...), custom_call_target="tpu_custom_call" | custom-call | flops 100000000 | bytes 4194304 | tf_op jit(solution)/shard_map/mix/pallas_call | solution.py:289
  78.7 4.4 %all-to-all-start.1 = ((bf16[16,128,128]{2,1,0:T(8,128)(2,1)}), bf16[16,128,128]{2,1,0:T(8,128)(2,1)S(1)}, u32[]{:S(2)}, u32[]{:S(2)}) async-start(bf16[16,128,128]{2,1,0:T(8,128)(2,1)} %bitcast.4), calls=%async_computation.1 | async-start | bytes 1048576 | tf_op jit(solution)/shard_map/all_to_all | solution.py:393
  83.1 12.7 %book_grad.3 = f32[64,4096]{1,0:T(8,128)S(1)} custom-call(bf16[128,2048]{1,0:T(8,128)(2,1)S(1)} %get-tuple-element.66.w_ref, bf16[2048,8192]{1,0:T(8,128)(2,1)} %get-tuple-element.48.ds_hbm, bf16[2048,4096]{1,0:T(8,128)(2,1)} %get-tuple-element.49.e_ref), custom_call_target="tpu_custom_call" | custom-call | flops 8589934592 | bytes 33554432 | tf_op jit(solution)/shard_map/book_grad/pallas_call | solution.py:326
  95.8 0.0 all-to-all-done.1.a_ref
  95.8 3.1 %collective-permute-start.10 = (f32[64,4096]{1,0:T(8,128)S(1)}, f32[64,4096]{1,0:T(8,128)S(1)}, u32[]{:S(2)}, u32[]{:S(2)}) collective-permute-start(f32[64,4096]{1,0:T(8,128)S(1)} %book_grad.3), channel_id=1, source_target_pairs={{0,1},{1,0},{2,3},{3,2},{4,5},{5,4},{6,7},{7,6},{8,9},{9,8},{10,11... | collective-permute-start | bytes 3145736 | tf_op jit(solution)/shard_map/ppermute | solution.py:376
  98.9 0.6 pieces.1
  99.5 0.1 collective-permute-start.4
  99.6 1.7 %collective-permute-start.5 = (bf16[16,32,128]{2,1,0:T(8,128)(2,1)S(1)}, bf16[16,32,128]{2,1,0:T(8,128)(2,1)S(1)}, u32[]{:S(2)}, u32[]{:S(2)}) collective-permute-start(bf16[16,32,128]{2,1,0:T(8,128)(2,1)S(1)} %get-tuple-element.56), channel_id=1, source_target_pairs={{0,4},{1,5},{2,6},{3,7},{4,0},{5,1},{6,2},{7,3},{8,12},{9,13},{10,... | collective-permute-start | bytes 393224 | tf_op jit(solution)/shard_map/ppermute | solution.py:376
  101.3 1.7 %collective-permute-start.6 = (bf16[16,32,128]{2,1,0:T(8,128)(2,1)S(1)}, bf16[16,32,128]{2,1,0:T(8,128)(2,1)S(1)}, u32[]{:S(2)}, u32[]{:S(2)}) collective-permute-start(bf16[16,32,128]{2,1,0:T(8,128)(2,1)S(1)} %get-tuple-element.57), channel_id=1, source_target_pairs={{0,6},{1,7},{2,0},{3,1},{4,2},{5,3},{6,4},{7,5},{8,14},{9,15},{10,... | collective-permute-start | bytes 393224 | tf_op jit(solution)/shard_map/ppermute | solution.py:376
  102.9 7.7 %book_grad.4.near_1 = f32[64,2048]{1,0:T(8,128)S(1)} custom-call(bf16[128,2048]{1,0:T(8,128)(2,1)S(1)} %get-tuple-element.66.w_ref, bf16[2048,8192]{1,0:T(8,128)(2,1)} %get-tuple-element.48.ds_hbm, bf16[2048,2048]{1,0:T(8,128)(2,1)} %get-tuple-element.59.e_ref), custom_call_target="tpu_custom_call" | custom-call | flops 4294967296 | bytes 16777216 | tf_op jit(solution)/shard_map/book_grad/pallas_call | solution.py:326
  110.6 0.0 collective-permute-done.4.refs_1_
  110.7 0.0 collective-permute-done.5.refs_2_
  110.7 0.0 collective-permute-done.6.refs_3_
  110.7 0.6 sums.1.refs_0_
  111.3 1.3 %collective-permute-start.9 = (bf16[16,32,128]{2,1,0:T(8,128)(2,1)S(1)}, bf16[16,32,128]{2,1,0:T(8,128)(2,1)S(1)}, u32[]{:S(2)}, u32[]{:S(2)}) collective-permute-start(bf16[16,32,128]{2,1,0:T(8,128)(2,1)S(1)} %sums.1.refs_0_), channel_id=1, source_target_pairs={{0,6},{1,7},{2,0},{3,1},{4,2},{5,3},{6,4},{7,5},{8,14},{9,15},{10,... | collective-permute-start | bytes 393224 | tf_op jit(solution)/shard_map/ppermute | solution.py:376
  112.6 0.5 collective-permute-start.8
  113.1 0.8 collective-permute-start.7
  113.9 7.7 %book_grad.5.near_2 = f32[64,2048]{1,0:T(8,128)S(1)} custom-call(bf16[128,2048]{1,0:T(8,128)(2,1)S(1)} %get-tuple-element.66.w_ref, bf16[2048,8192]{1,0:T(8,128)(2,1)} %get-tuple-element.48.ds_hbm, bf16[2048,2048]{1,0:T(8,128)(2,1)} %get-tuple-element.67.e_ref), custom_call_target="tpu_custom_call" | custom-call | flops 4294967296 | bytes 16777216 | tf_op jit(solution)/shard_map/book_grad/pallas_call | solution.py:326
  121.6 0.0 collective-permute-done.9.refs_3_
  121.6 0.0 collective-permute-done.8.refs_2_
  121.6 0.7 collective-permute-done.7.refs_1_
  122.3 1.1 collective-permute-start.11
  123.4 0.1 collective-permute-start.12
  123.5 0.4 collective-permute-start.13
  123.9 0.1 collective-permute-start.14
  124.0 0.4 collective-permute-done.11.refs_4_
  124.4 0.4 collective-permute-done.12.refs_5_
  124.7 0.2 collective-permute-done.13.refs_6_
  124.9 0.3 collective-permute-done.14.refs_7_
  125.2 0.0 collective-permute-done.10.from_far
  125.2 2.2 %spread.1 = (bf16[256,1024]{1,0:T(8,128)(2,1)}, bf16[256,1024]{1,0:T(8,128)(2,1)}, f32[64,4096]{1,0:T(8,128)}) custom-call(s32[2]{0:T(128)S(1)} %pad_add_fusion.place_ref, f32[64,2048]{1,0:T(8,128)S(1)} %book_grad.4.near_1, f32[64,2048]{1,0:T(8,128)S(1)} %book_grad.5.near_2, f32[64,4096]{1,0:T(8,128)S(1)} %collective-permute-done.10.from_far, ...), custom_call_target="tpu_custom_call" | custom-call | flops 100000000 | bytes 2097152 | tf_op jit(solution)/shard_map/spread/pallas_call | solution.py:408
Async XLA Ops:
  0.6 11.0 %collective-permute-start = (bf16[64,4096]{1,0:T(8,128)(2,1)}, bf16[64,4096]{1,0:T(8,128)(2,1)S(1)}, u32[]{:S(2)}, u32[]{:S(2)}) collective-permute-start(bf16[64,4096]{1,0:T(8,128)(2,1)} %bitcast.7), channel_id=1, source_target_pairs={{0,1},{1,0},{2,3},{3,2},{4,5},{5,4},{6,7},{7,6},{8,9},{9,8},{10,11... | collective-permute-start | bytes 1572872 | tf_op jit(solution)/shard_map/ppermute | solution.py:376
  4.8 17.0 %all-to-all-start = ((bf16[16,128,128]{2,1,0:T(8,128)(2,1)}), bf16[16,128,128]{2,1,0:T(8,128)(2,1)S(1)}, u32[]{:S(2)}, u32[]{:S(2)}) async-start(bf16[16,128,128]{2,1,0:T(8,128)(2,1)} %pack.1), calls=%async_computation | async-start | bytes 1048576 | tf_op jit(solution)/shard_map/all_to_all | solution.py:382
  11.7 1.0 copy-start
  13.9 1.3 %copy-start.1 = (bf16[8192,128]{1,0:T(8,128)(2,1)}, bf16[8192,128]{1,0:T(8,128)(2,1)S(1)}, u32[]{:S(2)}) copy-start(bf16[8192,128]{1,0:T(8,128)(2,1)S(1)} %get-tuple-element.41.bookt_ref) | copy-start | bytes 6291460
  21.8 1.6 %copy-start.2 = (bf16[8192,128]{1,0:T(8,128)(2,1)S(1)}, bf16[8192,128]{1,0:T(8,128)(2,1)}, u32[]{:S(2)}) copy-start(bf16[8192,128]{1,0:T(8,128)(2,1)} %copy-done.1) | copy-start | bytes 6291460
  66.3 5.1 %collective-permute-start.3 = (f32[8,2048]{1,0:T(8,128)S(1)}, f32[8,2048]{1,0:T(8,128)S(1)}, u32[]{:S(2)}, u32[]{:S(2)}) collective-permute-start(f32[8,2048]{1,0:T(8,128)S(1)} %get-tuple-element.45.own_ref), channel_id=1, source_target_pairs={{0,6},{1,7},{2,0},{3,1},{4,2},{5,3},{6,4},{7,5},{8,14},{9,15},{10,... | collective-permute-start | bytes 196616 | tf_op jit(solution)/shard_map/ppermute | solution.py:376
  70.1 4.7 %collective-permute-start.2 = (f32[8,2048]{1,0:T(8,128)S(1)}, f32[8,2048]{1,0:T(8,128)S(1)}, u32[]{:S(2)}, u32[]{:S(2)}) collective-permute-start(f32[8,2048]{1,0:T(8,128)S(1)} %get-tuple-element.45.own_ref), channel_id=1, source_target_pairs={{0,4},{1,5},{2,6},{3,7},{4,0},{5,1},{6,2},{7,3},{8,12},{9,13},{10,... | collective-permute-start | bytes 196616 | tf_op jit(solution)/shard_map/ppermute | solution.py:376
  70.1 5.0 %collective-permute-start.1 = (f32[8,2048]{1,0:T(8,128)S(1)}, f32[8,2048]{1,0:T(8,128)S(1)}, u32[]{:S(2)}, u32[]{:S(2)}) collective-permute-start(f32[8,2048]{1,0:T(8,128)S(1)} %get-tuple-element.45.own_ref), channel_id=1, source_target_pairs={{0,2},{1,3},{2,4},{3,5},{4,6},{5,7},{6,0},{7,1},{8,10},{9,11},{10,... | collective-permute-start | bytes 196616 | tf_op jit(solution)/shard_map/ppermute | solution.py:376
  78.7 17.1 %all-to-all-start.1 = ((bf16[16,128,128]{2,1,0:T(8,128)(2,1)}), bf16[16,128,128]{2,1,0:T(8,128)(2,1)S(1)}, u32[]{:S(2)}, u32[]{:S(2)}) async-start(bf16[16,128,128]{2,1,0:T(8,128)(2,1)} %bitcast.4), calls=%async_computation.1 | async-start | bytes 1048576 | tf_op jit(solution)/shard_map/all_to_all | solution.py:393
  95.8 29.4 %collective-permute-start.10 = (f32[64,4096]{1,0:T(8,128)S(1)}, f32[64,4096]{1,0:T(8,128)S(1)}, u32[]{:S(2)}, u32[]{:S(2)}) collective-permute-start(f32[64,4096]{1,0:T(8,128)S(1)} %book_grad.3), channel_id=1, source_target_pairs={{0,1},{1,0},{2,3},{3,2},{4,5},{5,4},{6,7},{7,6},{8,9},{9,8},{10,11... | collective-permute-start | bytes 3145736 | tf_op jit(solution)/shard_map/ppermute | solution.py:376
  99.5 11.2 %collective-permute-start.4 = (bf16[16,32,128]{2,1,0:T(8,128)(2,1)S(1)}, bf16[16,32,128]{2,1,0:T(8,128)(2,1)S(1)}, u32[]{:S(2)}, u32[]{:S(2)}) collective-permute-start(bf16[16,32,128]{2,1,0:T(8,128)(2,1)S(1)} %get-tuple-element.55), channel_id=1, source_target_pairs={{0,2},{1,3},{2,4},{3,5},{4,6},{5,7},{6,0},{7,1},{8,10},{9,11},{10,... | collective-permute-start | bytes 393224 | tf_op jit(solution)/shard_map/ppermute | solution.py:376
  99.6 11.1 %collective-permute-start.5 = (bf16[16,32,128]{2,1,0:T(8,128)(2,1)S(1)}, bf16[16,32,128]{2,1,0:T(8,128)(2,1)S(1)}, u32[]{:S(2)}, u32[]{:S(2)}) collective-permute-start(bf16[16,32,128]{2,1,0:T(8,128)(2,1)S(1)} %get-tuple-element.56), channel_id=1, source_target_pairs={{0,4},{1,5},{2,6},{3,7},{4,0},{5,1},{6,2},{7,3},{8,12},{9,13},{10,... | collective-permute-start | bytes 393224 | tf_op jit(solution)/shard_map/ppermute | solution.py:376
  101.3 9.4 %collective-permute-start.6 = (bf16[16,32,128]{2,1,0:T(8,128)(2,1)S(1)}, bf16[16,32,128]{2,1,0:T(8,128)(2,1)S(1)}, u32[]{:S(2)}, u32[]{:S(2)}) collective-permute-start(bf16[16,32,128]{2,1,0:T(8,128)(2,1)S(1)} %get-tuple-element.57), channel_id=1, source_target_pairs={{0,6},{1,7},{2,0},{3,1},{4,2},{5,3},{6,4},{7,5},{8,14},{9,15},{10,... | collective-permute-start | bytes 393224 | tf_op jit(solution)/shard_map/ppermute | solution.py:376
  111.3 10.3 %collective-permute-start.9 = (bf16[16,32,128]{2,1,0:T(8,128)(2,1)S(1)}, bf16[16,32,128]{2,1,0:T(8,128)(2,1)S(1)}, u32[]{:S(2)}, u32[]{:S(2)}) collective-permute-start(bf16[16,32,128]{2,1,0:T(8,128)(2,1)S(1)} %sums.1.refs_0_), channel_id=1, source_target_pairs={{0,6},{1,7},{2,0},{3,1},{4,2},{5,3},{6,4},{7,5},{8,14},{9,15},{10,... | collective-permute-start | bytes 393224 | tf_op jit(solution)/shard_map/ppermute | solution.py:376
  112.6 8.9 %collective-permute-start.8 = (bf16[16,32,128]{2,1,0:T(8,128)(2,1)S(1)}, bf16[16,32,128]{2,1,0:T(8,128)(2,1)S(1)}, u32[]{:S(2)}, u32[]{:S(2)}) collective-permute-start(bf16[16,32,128]{2,1,0:T(8,128)(2,1)S(1)} %sums.1.refs_0_), channel_id=1, source_target_pairs={{0,4},{1,5},{2,6},{3,7},{4,0},{5,1},{6,2},{7,3},{8,12},{9,13},{10,... | collective-permute-start | bytes 393224 | tf_op jit(solution)/shard_map/ppermute | solution.py:376
  113.1 9.2 %collective-permute-start.7 = (bf16[16,32,128]{2,1,0:T(8,128)(2,1)S(1)}, bf16[16,32,128]{2,1,0:T(8,128)(2,1)S(1)}, u32[]{:S(2)}, u32[]{:S(2)}) collective-permute-start(bf16[16,32,128]{2,1,0:T(8,128)(2,1)S(1)} %sums.1.refs_0_), channel_id=1, source_target_pairs={{0,2},{1,3},{2,4},{3,5},{4,6},{5,7},{6,0},{7,1},{8,10},{9,11},{10,... | collective-permute-start | bytes 393224 | tf_op jit(solution)/shard_map/ppermute | solution.py:376
  122.3 2.1 %collective-permute-start.11 = (bf16[16,32,128]{2,1,0:T(8,128)(2,1)S(1)}, bf16[16,32,128]{2,1,0:T(8,128)(2,1)S(1)}, u32[]{:S(2)}, u32[]{:S(2)}) collective-permute-start(bf16[16,32,128]{2,1,0:T(8,128)(2,1)S(1)} %sums.1.refs_0_), channel_id=1, source_target_pairs={{0,1},{1,0},{2,3},{3,2},{4,5},{5,4},{6,7},{7,6},{8,9},{9,8},{10,11... | collective-permute-start | bytes 393224 | tf_op jit(solution)/shard_map/ppermute | solution.py:376
  123.4 1.3 %collective-permute-start.12 = (bf16[16,32,128]{2,1,0:T(8,128)(2,1)S(1)}, bf16[16,32,128]{2,1,0:T(8,128)(2,1)S(1)}, u32[]{:S(2)}, u32[]{:S(2)}) collective-permute-start(bf16[16,32,128]{2,1,0:T(8,128)(2,1)S(1)} %collective-permute-done.7.refs_1_), channel_id=1, source_target_pairs={{0,1},{1,0},{2,3},{3,2},{4,5},{5,4},{6,7},{7,6},{8,9},{9,8},{10,11... | collective-permute-start | bytes 393224 | tf_op jit(solution)/shard_map/ppermute | solution.py:376
  123.5 1.4 %collective-permute-start.13 = (bf16[16,32,128]{2,1,0:T(8,128)(2,1)S(1)}, bf16[16,32,128]{2,1,0:T(8,128)(2,1)S(1)}, u32[]{:S(2)}, u32[]{:S(2)}) collective-permute-start(bf16[16,32,128]{2,1,0:T(8,128)(2,1)S(1)} %collective-permute-done.8.refs_2_), channel_id=1, source_target_pairs={{0,1},{1,0},{2,3},{3,2},{4,5},{5,4},{6,7},{7,6},{8,9},{9,8},{10,11... | collective-permute-start | bytes 393224 | tf_op jit(solution)/shard_map/ppermute | solution.py:376
  123.9 1.3 %collective-permute-start.14 = (bf16[16,32,128]{2,1,0:T(8,128)(2,1)S(1)}, bf16[16,32,128]{2,1,0:T(8,128)(2,1)S(1)}, u32[]{:S(2)}, u32[]{:S(2)}) collective-permute-start(bf16[16,32,128]{2,1,0:T(8,128)(2,1)S(1)} %collective-permute-done.9.refs_3_), channel_id=1, source_target_pairs={{0,1},{1,0},{2,3},{3,2},{4,5},{5,4},{6,7},{7,6},{8,9},{9,8},{10,11... | collective-permute-start | bytes 393224 | tf_op jit(solution)/shard_map/ppermute | solution.py:376

commit v4 on v3

--- a/solution.py
+++ b/solution.py
@@ -84,8 +84,8 @@
 def local_pass_body(chunk, parts, xg_ref, book_ref, bookt_ref, *rest):
     e_refs, rest = rest[: len(parts)], rest[len(parts) :]
     ds_hbm, part_ref, dx_ref, stat_ref, xgt_ref, *scratch = rest
-    s_slots, m_slots, gq_slots, d_slots, ds_slots, e_slots = (scratch[k : k + 2] for k in range(0, 12, 2))
-    e_sems, ds_sems = scratch[12:]
+    s_slots, m_slots, top_slots, sum_slots, d_slots, ds_slots, e_slots = (scratch[k : k + 2] for k in range(0, 14, 2))
+    e_sems, ds_sems = scratch[14:]
     tile, codes = s_slots[0].shape
     tiles = xg_ref.shape[0] // tile
     steps = codes // chunk
@@ -124,13 +124,13 @@
                 most = piece if most is None else jnp.maximum(most, piece)
 
         def end():
-            top = jnp.max(most, axis=1, keepdims=True) * (SCALE * LOG2E)
-            m_slots[n][...] = jnp.broadcast_to(top, (tile, LANES))
+            m_slots[n][...] = most
 
         return one, end
 
     def weigh(t, n):
-        top = m_slots[n][...]
+        top = jnp.max(m_slots[n][...], axis=1, keepdims=True) * (SCALE * LOG2E)
+        top = jnp.broadcast_to(top, (tile, LANES))
         wide = jnp.concatenate([top] * (chunk // LANES), axis=1)
         acc = jnp.zeros((tile, LANES), F32)
 
@@ -145,24 +145,22 @@
             acc = acc + jnp.dot(e, bookt_ref[at, :], preferred_element_type=F32)
 
         def end():
-            part_ref[rows(t), :] = acc
-            lane = lax.broadcasted_iota(jnp.int32, (tile, LANES), 1)
-            total = jnp.sum(jnp.where(lane == DS, acc, 0.0), axis=1, keepdims=True)
-            xg = xg_ref[rows(t), :]
-            h = jnp.sum(acc[:, :DS] * xg[:, DS:].astype(F32), axis=1, keepdims=True)
-            gq = h / total
-            gq_slots[n][...] = jnp.broadcast_to(gq, (tile, LANES))
-            stat = jnp.where(lane == 0, top, jnp.where(lane == 1, total, jnp.where(lane == 2, h, gq)))
-            stat_ref[:, rows(t)] = stat.T[:8]
-            xgt_ref[:, rows(t)] = xg.T
+            sum_slots[n][...] = acc
+            top_slots[n][...] = top
             for copy in e_copies(t, n):
                 copy.start()
 
         return one, end
 
     def lean(t, n):
-        g = xg_ref[rows(t), :][:, DS:]
-        wide = jnp.concatenate([gq_slots[n][...]] * (chunk // LANES), axis=1)
+        xg = xg_ref[rows(t), :]
+        g = xg[:, DS:]
+        sums = sum_slots[n][...]
+        lane = lax.broadcasted_iota(jnp.int32, (tile, LANES), 1)
+        total = jnp.sum(jnp.where(lane == DS, sums, 0.0), axis=1, keepdims=True)
+        h = jnp.sum(sums[:, :DS] * g.astype(F32), axis=1, keepdims=True)
+        gq = jnp.broadcast_to(h / total, (tile, LANES))
+        wide = jnp.concatenate([gq] * (chunk // LANES), axis=1)
         acc = jnp.zeros((tile, LANES), F32)
 
         def one(c):
@@ -170,6 +168,11 @@
             if c < steps:
                 at = slice(c * chunk, (c + 1) * chunk)
                 d_slots[c % 2][...] = jnp.dot(g, book_ref[:, at], preferred_element_type=F32) - wide
+            if c == 2:
+                stat = jnp.where(lane == 0, top_slots[n][...], jnp.where(lane == 1, total, jnp.where(lane == 2, h, gq)))
+                stat_ref[:, rows(t)] = stat.T[:8]
+                xgt_ref[:, rows(t)] = xg.T
+                part_ref[rows(t), :] = jnp.concatenate([sums[:, :DS]] * 2, axis=1)
             if c > 0:
                 at = slice((c - 1) * chunk, c * chunk)
                 ref, place = e_at(t, n, c - 1)
@@ -249,7 +252,7 @@
             jax.ShapeDtypeStruct((8, rows), F32),
             jax.ShapeDtypeStruct((LANES, rows), BF16),
         ],
-        scratch_shapes=[wide, wide, narrow, narrow, narrow, narrow]
+        scratch_shapes=[wide, wide] + [narrow] * 6
         + [pltpu.VMEM((tile, chunk), F32)] * 2
         + [short, short]
         + [pltpu.VMEM((tile, max(staged, LANES)), BF16)] * 2
@@ -274,14 +277,15 @@
     w_ref[DS:] = ((g + (SCALE * off_row) * x) * f_row).astype(BF16)
     step = LANES
     sub = lax.broadcasted_iota(jnp.int32, (8, step), 0)
+    lane = lax.broadcasted_iota(jnp.int32, (step, LANES), 1)
     for r in range(0, rows, step):
         at = slice(r, r + step)
         turned = jnp.where(sub == 0, f_row[:, at], off_row[:, at]).T
         f, off = turned[:, 0:1], turned[:, 1:2]
         part = part_ref[at, :]
-        q = (part * f)[:, :DS]
-        dx = ((dx_ref[at, :] + part * off) * (SCALE * f))[:, :DS]
-        out_ref[at, :] = jnp.concatenate([q, dx], axis=1).astype(BF16)
+        dx = dx_ref[at, :][:, :DS]
+        lean = (jnp.concatenate([dx, dx], axis=1) + part * off) * SCALE
+        out_ref[at, :] = (jnp.where(lane < DS, part, lean) * f).astype(BF16)
 
 
 def mix(part, dx, xgt, stats):
@@ -297,41 +301,49 @@
     )(part, dx, xgt, *stats)
 
 
-def book_body(first, tile, kept, extra, w_ref, ds_hbm, e_ref, *rest):
-    out_ref = rest[extra]
-
-    def one(ds_ref, *more):
-        at = span(pl.program_id(0) * tile, tile)
-        e = e_ref[:, at] if kept else more[0][...]
-        grad = jnp.dot(w_ref[:DS], ds_ref[...], preferred_element_type=F32)
-        grad += jnp.dot(w_ref[DS:], e, preferred_element_type=F32)
-        if extra:
-            grad += rest[0][:, at]
-        out_ref[:, at] = grad
-
-    rows, width = e_ref.shape
-    specs = [pl.BlockSpec((rows, tile), lambda t: (0, first // tile + t))]
-    if not kept:
-        specs.append(pl.BlockSpec((rows, tile), lambda t: (0, t)))
-    pltpu.emit_pipeline(one, grid=(width // tile,), in_specs=specs)(ds_hbm, *([] if kept else [e_ref]))
-
-
-def book_grad(w, ds, e, part, other=None):
-    first, width, kept = part
-    tile = 1024 if width > 2048 else 512
-    rows = e.shape[0]
-    pairs = rows * width
-    more = [] if other is None else [other]
-    space = pltpu.VMEM if kept else pltpu.HBM
+def book_body(first, tile, cuts, w_ref, ds_hbm, e_hbm, out_ref):
+    rows, width = e_hbm.shape
+    chunk = rows // cuts
+
+    def one(ds_ref, e_ref):
+        t, r = pl.program_id(0), pl.program_id(1)
+        at = span(t * tile, tile)
+        w = w_ref[:, span(r * chunk, chunk)]
+        grad = jnp.dot(w[:DS], ds_ref[...], preferred_element_type=F32)
+        grad += jnp.dot(w[DS:], e_ref[...], preferred_element_type=F32)
+        if cuts == 1:
+            out_ref[:, at] = grad
+            return
+
+        @pl.when(r == 0)
+        def _():
+            out_ref[:, at] = grad
+
+        @pl.when(r > 0)
+        def _():
+            out_ref[:, at] += grad
+
+    specs = [
+        pl.BlockSpec((chunk, tile), lambda t, r: (r, first // tile + t)),
+        pl.BlockSpec((chunk, tile), lambda t, r: (r, t)),
+    ]
+    pltpu.emit_pipeline(one, grid=(width // tile, cuts), in_specs=specs)(ds_hbm, e_hbm)
+
+
+def book_grad(w, ds, e, part):
+    first, width, _ = part
+    pairs = e.shape[0] * width
+    far = lambda v: pltpu.with_memory_space_constraint(v, pltpu.HBM)
+    tile, cuts = (1024, 1) if width > 2048 else (512, 1)
     return pl.pallas_call(
-        functools.partial(book_body, first, tile, kept, len(more)),
-        in_specs=[WHOLE, FAR, WHOLE if kept else FAR] + [WHOLE] * len(more),
+        functools.partial(book_body, first, tile, cuts),
+        in_specs=[WHOLE, FAR, FAR],
         out_specs=WHOLE,
         out_shape=jax.ShapeDtypeStruct((DS, width), F32),
-        compiler_params=pltpu.CompilerParams(vmem_limit_bytes=(14 if kept else 24) * MIB),
+        compiler_params=pltpu.CompilerParams(vmem_limit_bytes=24 * MIB),
         cost_estimate=pl.CostEstimate(flops=pairs * 1024, bytes_accessed=pairs * 4, transcendentals=0),
         name="book_grad",
-    )(w, pltpu.with_memory_space_constraint(ds, pltpu.HBM), pltpu.with_memory_space_constraint(e, space), *more)
+    )(w, far(ds), far(e))
 
 
 def pieces_body(n_z, place_ref, a_ref, own_ref, *send_refs):
@@ -403,8 +415,9 @@
     w, total = then((w, total))
     near_2 = book_grad(w, ds, es[2], parts[2])
     ring = [total] + [to_peer(total, d) for d in range(1, n_z)]
-    ring, near_2 = then((ring, near_2))
-    every = ring + [to_peer(v, 0, 1) for v in ring]
+    mate_total = to_peer(total, 0, 1)
+    ring, mate_total, near_2 = then((ring, mate_total, near_2))
+    every = ring + [mate_total] + [to_peer(v, 0, 1) for v in ring[1:]]
     quantized, grads, grad_book = small(
         functools.partial(spread_body, n_z),
         "spread",

time: 128 us -> 126 us (0.984)
  Pallas kernels: 81.8 us -> 80.5 us
    pallas_call x1, Pallas kernels: 3.6 us -> 2.12 us  [mix(): pl.pallas_call(mix_body, in_specs=[WHOLE] * 7, out_specs=[WHOLE] * 2, out...]
  transfers between devices with their start and end apart: 17 -> 17, of which waited for: 9 -> 8; matrix products, arithmetic and copies ran while one was open for 0% -> 0% of each run, Pallas kernels for 26% -> 26%
where the time goes in v4:
time: 126 us
  Pallas kernels  80.5 us (64%)
  starting transfers between devices  28.3 us (22%)
  waiting for transfers between devices  12.3 us (10%)
  local copies, waits for them, and re-layouts  3.95 us (3%)
    pallas_call x1, Pallas kernels, local_pass(): pl.pallas_call(functools.partial(local_pass_body, chunk, tuple(placed)),...  43.1 us
    pallas_call x3, Pallas kernels, book_grad(): pl.pallas_call(functools.partial(book_body, first, tile, cuts), in_specs=...  28.1 us
    ppermute x15, starting transfers between devices, to_peer(): return lax.ppermute(v, 'code', pairs)  17.1 us
    all_to_all x1, starting transfers between devices, local(): xg = lax.all_to_all(xg, 'sub', 0, 0, tiled=True)  6.85 us
    all_to_all x1, waiting for transfers between devices, local(): xg = lax.all_to_all(xg, 'sub', 0, 0, tiled=True)  6.56 us
    ppermute x15, waiting for transfers between devices, to_peer(): return lax.ppermute(v, 'code', pairs)  5.78 us
    all_to_all x1, starting transfers between devices, local(): lax.all_to_all(out.reshape(n_sub, mine, LANES), 'sub', 0, 0, tiled=True)  4.34 us
    unnamed x6, local copies, waits for them, and re-layouts  3.95 us
  transfers between devices with their start and end apart: 17, of which 8 were waited for; matrix products, arithmetic and copies ran while one was open for 0% of the time, Pallas kernels for 26%

profile of v4, /device:TPU:1, one launch (start us, length us, event | category | flops | bytes accessed | tf_op | source)
XLA Modules:
  0.0 126.0 jit_solution(4147290786517465966)
XLA Ops:
  0.6 1.5 %collective-permute-start = (bf16[64,4096]{1,0:T(8,128)(2,1)}, bf16[64,4096]{1,0:T(8,128)(2,1)S(1)}, u32[]{:S(2)}, u32[]{:S(2)}) collective-permute-start(bf16[64,4096]{1,0:T(8,128)(2,1)} %bitcast.7), channel_id=1, source_target_pairs={{0,1},{1,0},{2,3},{3,2},{4,5},{5,4},{6,7},{7,6},{8,9},{9,8},{10,11... | collective-permute-start | bytes 1572872 | tf_op jit(solution)/shard_map/ppermute | solution.py:388
  2.1 0.1 pad_add_fusion.place_ref
  2.2 2.6 %pack.1 = bf16[16,128,128]{2,1,0:T(8,128)(2,1)} custom-call(s32[2]{0:T(128)S(1)} %pad_add_fusion.place_ref, bf16[256,1024]{1,0:T(8,128)(2,1)} %x_hbm.1, bf16[256,1024]{1,0:T(8,128)(2,1)} %g_hbm.1), custom_call_target="tpu_custom_call" | custom-call | flops 100000000 | bytes 2097152 | tf_op jit(solution)/shard_map/pack/pallas_call | solution.py:60
  4.8 6.8 %all-to-all-start = ((bf16[16,128,128]{2,1,0:T(8,128)(2,1)}), bf16[16,128,128]{2,1,0:T(8,128)(2,1)S(1)}, u32[]{:S(2)}, u32[]{:S(2)}) async-start(bf16[16,128,128]{2,1,0:T(8,128)(2,1)} %pack.1), calls=%async_computation | async-start | bytes 1048576 | tf_op jit(solution)/shard_map/all_to_all | solution.py:394
  11.7 0.0 collective-permute-done.mate_ref
  11.7 0.0 copy-start
  11.7 1.0 copy-done
  12.7 1.2 books.1
  13.9 0.0 copy-start.1
  13.9 1.3 %copy-done.1 = bf16[8192,128]{1,0:T(8,128)(2,1)} copy-done((bf16[8192,128]{1,0:T(8,128)(2,1)}, bf16[8192,128]{1,0:T(8,128)(2,1)S(1)}, u32[]{:S(2)}) %copy-start.1) | copy-done | bytes 2097176
  15.2 6.6 %all-to-all-done = bf16[16,128,128]{2,1,0:T(8,128)(2,1)S(1)} async-done(((bf16[16,128,128]{2,1,0:T(8,128)(2,1)}), bf16[16,128,128]{2,1,0:T(8,128)(2,1)S(1)}, u32[]{:S(2)}, u32[]{:S(2)}) %all-to-all-start) | async-done | bytes 524320 | tf_op jit(solution)/shard_map/all_to_all | solution.py:394
  21.8 0.0 copy-start.2
  21.8 1.6 %copy-done.2 = bf16[8192,128]{1,0:T(8,128)(2,1)S(1)} copy-done((bf16[8192,128]{1,0:T(8,128)(2,1)S(1)}, bf16[8192,128]{1,0:T(8,128)(2,1)}, u32[]{:S(2)}) %copy-start.2) | copy-done | bytes 2097176
  23.4 43.1 %local_pass.1 = (bf16[2048,4096]{1,0:T(8,128)(2,1)}, bf16[2048,2048]{1,0:T(8,128)(2,1)}, bf16[2048,2048]{1,0:T(8,128)(2,1)}, bf16[2048,8192]{1,0:T(8,128)(2,1)},...) custom-call(bf16[2048,128]{1,0:T(8,128)(2,1)S(1)} %bitcast.6, ...), custom_call_target="tpu_custom_call" | custom-call | flops 34359738368 | bytes 67108864 | tf_op jit(solution)/shard_map/local_pass/pallas_call | solution.py:243
  66.5 3.8 %collective-permute-start.3 = (f32[8,2048]{1,0:T(8,128)S(1)}, f32[8,2048]{1,0:T(8,128)S(1)}, u32[]{:S(2)}, u32[]{:S(2)}) collective-permute-start(f32[8,2048]{1,0:T(8,128)S(1)} %get-tuple-element.46.own_ref), channel_id=1, source_target_pairs={{0,6},{1,7},{2,0},{3,1},{4,2},{5,3},{6,4},{7,5},{8,14},{9,15},{10,... | collective-permute-start | bytes 196616 | tf_op jit(solution)/shard_map/ppermute | solution.py:388
  70.3 0.0 collective-permute-start.2
  70.3 0.7 collective-permute-start.1
  71.0 0.6 collective-permute-done.3.o3
  71.7 3.4 %collective-permute-done.2.o2 = f32[8,2048]{1,0:T(8,128)S(1)} collective-permute-done((f32[8,2048]{1,0:T(8,128)S(1)}, f32[8,2048]{1,0:T(8,128)S(1)}, u32[]{:S(2)}, u32[]{:S(2)}) %collective-permute-start.2) | collective-permute-done | bytes 65568 | tf_op jit(solution)/shard_map/ppermute | solution.py:388
  75.1 0.3 collective-permute-done.1.o1
  75.4 2.1 %mix.1 = (bf16[2048,128]{1,0:T(8,128)(2,1)}, bf16[128,2048]{1,0:T(8,128)(2,1)S(1)}) custom-call(f32[2048,128]{1,0:T(8,128)S(1)} %get-tuple-element.43.part_ref, f32[2048,128]{1,0:T(8,128)S(1)} %get-tuple-element.44.dx_ref, bf16[128,2048]{1,0:T(8,128)(2,1)S(1)} %get-tuple-element.45.xgt_ref, f32[8,2048]{1,0:T(8,128)S(1)} %get-tuple-element.46.own_ref, ...), custom_call_target="tpu_custom_call" | custom-call | flops 100000000 | bytes 4194304 | tf_op jit(solution)/shard_map/mix/pallas_call | solution.py:293
  77.5 4.3 %all-to-all-start.1 = ((bf16[16,128,128]{2,1,0:T(8,128)(2,1)}), bf16[16,128,128]{2,1,0:T(8,128)(2,1)S(1)}, u32[]{:S(2)}, u32[]{:S(2)}) async-start(bf16[16,128,128]{2,1,0:T(8,128)(2,1)} %bitcast.4), calls=%async_computation.1 | async-start | bytes 1048576 | tf_op jit(solution)/shard_map/all_to_all | solution.py:405
  81.8 12.7 %book_grad.3 = f32[64,4096]{1,0:T(8,128)S(1)} custom-call(bf16[128,2048]{1,0:T(8,128)(2,1)S(1)} %get-tuple-element.67.w_ref, bf16[2048,8192]{1,0:T(8,128)(2,1)} %get-tuple-element.49.ds_hbm, bf16[2048,4096]{1,0:T(8,128)(2,1)} %get-tuple-element.50.e_hbm), custom_call_target="tpu_custom_call" | custom-call | flops 8589934592 | bytes 33554432 | tf_op jit(solution)/shard_map/book_grad/pallas_call | solution.py:338
  94.6 0.0 all-to-all-done.1.a_ref
  94.6 3.1 %collective-permute-start.11 = (f32[64,4096]{1,0:T(8,128)S(1)}, f32[64,4096]{1,0:T(8,128)S(1)}, u32[]{:S(2)}, u32[]{:S(2)}) collective-permute-start(f32[64,4096]{1,0:T(8,128)S(1)} %book_grad.3), channel_id=1, source_target_pairs={{0,1},{1,0},{2,3},{3,2},{4,5},{5,4},{6,7},{7,6},{8,9},{9,8},{10,11... | collective-permute-start | bytes 3145736 | tf_op jit(solution)/shard_map/ppermute | solution.py:388
  97.6 0.6 pieces.1
  98.2 0.1 collective-permute-start.4
  98.3 1.7 %collective-permute-start.5 = (bf16[16,32,128]{2,1,0:T(8,128)(2,1)S(1)}, bf16[16,32,128]{2,1,0:T(8,128)(2,1)S(1)}, u32[]{:S(2)}, u32[]{:S(2)}) collective-permute-start(bf16[16,32,128]{2,1,0:T(8,128)(2,1)S(1)} %get-tuple-element.57), channel_id=1, source_target_pairs={{0,4},{1,5},{2,6},{3,7},{4,0},{5,1},{6,2},{7,3},{8,12},{9,13},{10,... | collective-permute-start | bytes 393224 | tf_op jit(solution)/shard_map/ppermute | solution.py:388
  100.1 1.7 %collective-permute-start.6 = (bf16[16,32,128]{2,1,0:T(8,128)(2,1)S(1)}, bf16[16,32,128]{2,1,0:T(8,128)(2,1)S(1)}, u32[]{:S(2)}, u32[]{:S(2)}) collective-permute-start(bf16[16,32,128]{2,1,0:T(8,128)(2,1)S(1)} %get-tuple-element.58), channel_id=1, source_target_pairs={{0,6},{1,7},{2,0},{3,1},{4,2},{5,3},{6,4},{7,5},{8,14},{9,15},{10,... | collective-permute-start | bytes 393224 | tf_op jit(solution)/shard_map/ppermute | solution.py:388
  101.7 7.7 %book_grad.4.near_1 = f32[64,2048]{1,0:T(8,128)S(1)} custom-call(bf16[128,2048]{1,0:T(8,128)(2,1)S(1)} %get-tuple-element.67.w_ref, bf16[2048,8192]{1,0:T(8,128)(2,1)} %get-tuple-element.49.ds_hbm, bf16[2048,2048]{1,0:T(8,128)(2,1)} %get-tuple-element.60.e_hbm), custom_call_target="tpu_custom_call" | custom-call | flops 4294967296 | bytes 16777216 | tf_op jit(solution)/shard_map/book_grad/pallas_call | solution.py:338
  109.4 0.0 collective-permute-done.4.refs_1_
  109.4 0.0 collective-permute-done.5.refs_2_
  109.4 0.0 collective-permute-done.6.refs_3_
  109.4 0.6 sums.1.refs_0_
  110.1 0.9 collective-permute-start.10
  111.0 0.9 collective-permute-start.9
  111.9 0.7 collective-permute-start.8
  112.6 0.9 collective-permute-start.7
  113.5 7.7 %book_grad.5.near_2 = f32[64,2048]{1,0:T(8,128)S(1)} custom-call(bf16[128,2048]{1,0:T(8,128)(2,1)S(1)} %get-tuple-element.67.w_ref, bf16[2048,8192]{1,0:T(8,128)(2,1)} %get-tuple-element.49.ds_hbm, bf16[2048,2048]{1,0:T(8,128)(2,1)} %get-tuple-element.68.e_hbm), custom_call_target="tpu_custom_call" | custom-call | flops 4294967296 | bytes 16777216 | tf_op jit(solution)/shard_map/book_grad/pallas_call | solution.py:338
  121.2 0.0 collective-permute-done.10.refs_4_
  121.2 0.0 collective-permute-done.9.refs_3_
  121.2 0.0 collective-permute-done.8.refs_2_
  121.2 0.4 collective-permute-done.7.refs_1_
  121.6 0.6 collective-permute-start.12
  122.2 0.1 collective-permute-start.13
  122.3 0.4 collective-permute-start.14
  122.7 0.5 collective-permute-done.12.refs_5_
  123.2 0.4 collective-permute-done.13.refs_6_
  123.6 0.2 collective-permute-done.14.refs_7_
  123.8 0.0 collective-permute-done.11.from_far
  123.8 2.2 %spread.1 = (bf16[256,1024]{1,0:T(8,128)(2,1)}, bf16[256,1024]{1,0:T(8,128)(2,1)}, f32[64,4096]{1,0:T(8,128)}) custom-call(s32[2]{0:T(128)S(1)} %pad_add_fusion.place_ref, f32[64,2048]{1,0:T(8,128)S(1)} %book_grad.4.near_1, f32[64,2048]{1,0:T(8,128)S(1)} %book_grad.5.near_2, f32[64,4096]{1,0:T(8,128)S(1)} %collective-permute-done.11.from_far, ...), custom_call_target="tpu_custom_call" | custom-call | flops 100000000 | bytes 2097152 | tf_op jit(solution)/shard_map/spread/pallas_call | solution.py:421
Async XLA Ops:
  0.6 11.0 %collective-permute-start = (bf16[64,4096]{1,0:T(8,128)(2,1)}, bf16[64,4096]{1,0:T(8,128)(2,1)S(1)}, u32[]{:S(2)}, u32[]{:S(2)}) collective-permute-start(bf16[64,4096]{1,0:T(8,128)(2,1)} %bitcast.7), channel_id=1, source_target_pairs={{0,1},{1,0},{2,3},{3,2},{4,5},{5,4},{6,7},{7,6},{8,9},{9,8},{10,11... | collective-permute-start | bytes 1572872 | tf_op jit(solution)/shard_map/ppermute | solution.py:388
  4.8 17.0 %all-to-all-start = ((bf16[16,128,128]{2,1,0:T(8,128)(2,1)}), bf16[16,128,128]{2,1,0:T(8,128)(2,1)S(1)}, u32[]{:S(2)}, u32[]{:S(2)}) async-start(bf16[16,128,128]{2,1,0:T(8,128)(2,1)} %pack.1), calls=%async_computation | async-start | bytes 1048576 | tf_op jit(solution)/shard_map/all_to_all | solution.py:394
  11.7 1.0 copy-start
  13.9 1.3 %copy-start.1 = (bf16[8192,128]{1,0:T(8,128)(2,1)}, bf16[8192,128]{1,0:T(8,128)(2,1)S(1)}, u32[]{:S(2)}) copy-start(bf16[8192,128]{1,0:T(8,128)(2,1)S(1)} %get-tuple-element.42.bookt_ref) | copy-start | bytes 6291460
  21.8 1.6 %copy-start.2 = (bf16[8192,128]{1,0:T(8,128)(2,1)S(1)}, bf16[8192,128]{1,0:T(8,128)(2,1)}, u32[]{:S(2)}) copy-start(bf16[8192,128]{1,0:T(8,128)(2,1)} %copy-done.1) | copy-start | bytes 6291460
  66.5 5.2 %collective-permute-start.3 = (f32[8,2048]{1,0:T(8,128)S(1)}, f32[8,2048]{1,0:T(8,128)S(1)}, u32[]{:S(2)}, u32[]{:S(2)}) collective-permute-start(f32[8,2048]{1,0:T(8,128)S(1)} %get-tuple-element.46.own_ref), channel_id=1, source_target_pairs={{0,6},{1,7},{2,0},{3,1},{4,2},{5,3},{6,4},{7,5},{8,14},{9,15},{10,... | collective-permute-start | bytes 196616 | tf_op jit(solution)/shard_map/ppermute | solution.py:388
  70.3 4.7 %collective-permute-start.2 = (f32[8,2048]{1,0:T(8,128)S(1)}, f32[8,2048]{1,0:T(8,128)S(1)}, u32[]{:S(2)}, u32[]{:S(2)}) collective-permute-start(f32[8,2048]{1,0:T(8,128)S(1)} %get-tuple-element.46.own_ref), channel_id=1, source_target_pairs={{0,4},{1,5},{2,6},{3,7},{4,0},{5,1},{6,2},{7,3},{8,12},{9,13},{10,... | collective-permute-start | bytes 196616 | tf_op jit(solution)/shard_map/ppermute | solution.py:388
  70.3 5.0 %collective-permute-start.1 = (f32[8,2048]{1,0:T(8,128)S(1)}, f32[8,2048]{1,0:T(8,128)S(1)}, u32[]{:S(2)}, u32[]{:S(2)}) collective-permute-start(f32[8,2048]{1,0:T(8,128)S(1)} %get-tuple-element.46.own_ref), channel_id=1, source_target_pairs={{0,2},{1,3},{2,4},{3,5},{4,6},{5,7},{6,0},{7,1},{8,10},{9,11},{10,... | collective-permute-start | bytes 196616 | tf_op jit(solution)/shard_map/ppermute | solution.py:388
  77.5 17.1 %all-to-all-start.1 = ((bf16[16,128,128]{2,1,0:T(8,128)(2,1)}), bf16[16,128,128]{2,1,0:T(8,128)(2,1)S(1)}, u32[]{:S(2)}, u32[]{:S(2)}) async-start(bf16[16,128,128]{2,1,0:T(8,128)(2,1)} %bitcast.4), calls=%async_computation.1 | async-start | bytes 1048576 | tf_op jit(solution)/shard_map/all_to_all | solution.py:405
  94.6 29.2 %collective-permute-start.11 = (f32[64,4096]{1,0:T(8,128)S(1)}, f32[64,4096]{1,0:T(8,128)S(1)}, u32[]{:S(2)}, u32[]{:S(2)}) collective-permute-start(f32[64,4096]{1,0:T(8,128)S(1)} %book_grad.3), channel_id=1, source_target_pairs={{0,1},{1,0},{2,3},{3,2},{4,5},{5,4},{6,7},{7,6},{8,9},{9,8},{10,11... | collective-permute-start | bytes 3145736 | tf_op jit(solution)/shard_map/ppermute | solution.py:388
  98.2 11.2 %collective-permute-start.4 = (bf16[16,32,128]{2,1,0:T(8,128)(2,1)S(1)}, bf16[16,32,128]{2,1,0:T(8,128)(2,1)S(1)}, u32[]{:S(2)}, u32[]{:S(2)}) collective-permute-start(bf16[16,32,128]{2,1,0:T(8,128)(2,1)S(1)} %get-tuple-element.56), channel_id=1, source_target_pairs={{0,2},{1,3},{2,4},{3,5},{4,6},{5,7},{6,0},{7,1},{8,10},{9,11},{10,... | collective-permute-start | bytes 393224 | tf_op jit(solution)/shard_map/ppermute | solution.py:388
  98.3 11.1 %collective-permute-start.5 = (bf16[16,32,128]{2,1,0:T(8,128)(2,1)S(1)}, bf16[16,32,128]{2,1,0:T(8,128)(2,1)S(1)}, u32[]{:S(2)}, u32[]{:S(2)}) collective-permute-start(bf16[16,32,128]{2,1,0:T(8,128)(2,1)S(1)} %get-tuple-element.57), channel_id=1, source_target_pairs={{0,4},{1,5},{2,6},{3,7},{4,0},{5,1},{6,2},{7,3},{8,12},{9,13},{10,... | collective-permute-start | bytes 393224 | tf_op jit(solution)/shard_map/ppermute | solution.py:388
  100.1 9.4 %collective-permute-start.6 = (bf16[16,32,128]{2,1,0:T(8,128)(2,1)S(1)}, bf16[16,32,128]{2,1,0:T(8,128)(2,1)S(1)}, u32[]{:S(2)}, u32[]{:S(2)}) collective-permute-start(bf16[16,32,128]{2,1,0:T(8,128)(2,1)S(1)} %get-tuple-element.58), channel_id=1, source_target_pairs={{0,6},{1,7},{2,0},{3,1},{4,2},{5,3},{6,4},{7,5},{8,14},{9,15},{10,... | collective-permute-start | bytes 393224 | tf_op jit(solution)/shard_map/ppermute | solution.py:388
  110.1 11.1 %collective-permute-start.10 = (bf16[16,32,128]{2,1,0:T(8,128)(2,1)S(1)}, bf16[16,32,128]{2,1,0:T(8,128)(2,1)S(1)}, u32[]{:S(2)}, u32[]{:S(2)}) collective-permute-start(bf16[16,32,128]{2,1,0:T(8,128)(2,1)S(1)} %sums.1.refs_0_), channel_id=1, source_target_pairs={{0,1},{1,0},{2,3},{3,2},{4,5},{5,4},{6,7},{7,6},{8,9},{9,8},{10,11... | collective-permute-start | bytes 393224 | tf_op jit(solution)/shard_map/ppermute | solution.py:388
  111.0 10.2 %collective-permute-start.9 = (bf16[16,32,128]{2,1,0:T(8,128)(2,1)S(1)}, bf16[16,32,128]{2,1,0:T(8,128)(2,1)S(1)}, u32[]{:S(2)}, u32[]{:S(2)}) collective-permute-start(bf16[16,32,128]{2,1,0:T(8,128)(2,1)S(1)} %sums.1.refs_0_), channel_id=1, source_target_pairs={{0,6},{1,7},{2,0},{3,1},{4,2},{5,3},{6,4},{7,5},{8,14},{9,15},{10,... | collective-permute-start | bytes 393224 | tf_op jit(solution)/shard_map/ppermute | solution.py:388
  111.9 9.3 %collective-permute-start.8 = (bf16[16,32,128]{2,1,0:T(8,128)(2,1)S(1)}, bf16[16,32,128]{2,1,0:T(8,128)(2,1)S(1)}, u32[]{:S(2)}, u32[]{:S(2)}) collective-permute-start(bf16[16,32,128]{2,1,0:T(8,128)(2,1)S(1)} %sums.1.refs_0_), channel_id=1, source_target_pairs={{0,4},{1,5},{2,6},{3,7},{4,0},{5,1},{6,2},{7,3},{8,12},{9,13},{10,... | collective-permute-start | bytes 393224 | tf_op jit(solution)/shard_map/ppermute | solution.py:388
  112.6 9.0 %collective-permute-start.7 = (bf16[16,32,128]{2,1,0:T(8,128)(2,1)S(1)}, bf16[16,32,128]{2,1,0:T(8,128)(2,1)S(1)}, u32[]{:S(2)}, u32[]{:S(2)}) collective-permute-start(bf16[16,32,128]{2,1,0:T(8,128)(2,1)S(1)} %sums.1.refs_0_), channel_id=1, source_target_pairs={{0,2},{1,3},{2,4},{3,5},{4,6},{5,7},{6,0},{7,1},{8,10},{9,11},{10,... | collective-permute-start | bytes 393224 | tf_op jit(solution)/shard_map/ppermute | solution.py:388
  121.6 1.6 %collective-permute-start.12 = (bf16[16,32,128]{2,1,0:T(8,128)(2,1)S(1)}, bf16[16,32,128]{2,1,0:T(8,128)(2,1)S(1)}, u32[]{:S(2)}, u32[]{:S(2)}) collective-permute-start(bf16[16,32,128]{2,1,0:T(8,128)(2,1)S(1)} %collective-permute-done.7.refs_1_), channel_id=1, source_target_pairs={{0,1},{1,0},{2,3},{3,2},{4,5},{5,4},{6,7},{7,6},{8,9},{9,8},{10,11... | collective-permute-start | bytes 393224 | tf_op jit(solution)/shard_map/ppermute | solution.py:388
  122.2 1.3 %collective-permute-start.13 = (bf16[16,32,128]{2,1,0:T(8,128)(2,1)S(1)}, bf16[16,32,128]{2,1,0:T(8,128)(2,1)S(1)}, u32[]{:S(2)}, u32[]{:S(2)}) collective-permute-start(bf16[16,32,128]{2,1,0:T(8,128)(2,1)S(1)} %collective-permute-done.8.refs_2_), channel_id=1, source_target_pairs={{0,1},{1,0},{2,3},{3,2},{4,5},{5,4},{6,7},{7,6},{8,9},{9,8},{10,11... | collective-permute-start | bytes 393224 | tf_op jit(solution)/shard_map/ppermute | solution.py:388
  122.3 1.4 %collective-permute-start.14 = (bf16[16,32,128]{2,1,0:T(8,128)(2,1)S(1)}, bf16[16,32,128]{2,1,0:T(8,128)(2,1)S(1)}, u32[]{:S(2)}, u32[]{:S(2)}) collective-permute-start(bf16[16,32,128]{2,1,0:T(8,128)(2,1)S(1)} %collective-permute-done.9.refs_3_), channel_id=1, source_target_pairs={{0,1},{1,0},{2,3},{3,2},{4,5},{5,4},{6,7},{7,6},{8,9},{9,8},{10,11... | collective-permute-start | bytes 393224 | tf_op jit(solution)/shard_map/ppermute | solution.py:388

commit v5 on v4

--- a/solution.py
+++ b/solution.py
@@ -170,7 +170,7 @@
                 d_slots[c % 2][...] = jnp.dot(g, book_ref[:, at], preferred_element_type=F32) - wide
             if c == 2:
                 stat = jnp.where(lane == 0, top_slots[n][...], jnp.where(lane == 1, total, jnp.where(lane == 2, h, gq)))
-                stat_ref[:, rows(t)] = stat.T[:8]
+                stat_ref[:, rows(t)] = stat.T[:4]
                 xgt_ref[:, rows(t)] = xg.T
                 part_ref[rows(t), :] = jnp.concatenate([sums[:, :DS]] * 2, axis=1)
             if c > 0:
@@ -249,7 +249,7 @@
             pltpu.HBM((rows, codes), BF16),
             jax.ShapeDtypeStruct((rows, LANES), F32),
             jax.ShapeDtypeStruct((rows, LANES), F32),
-            jax.ShapeDtypeStruct((8, rows), F32),
+            jax.ShapeDtypeStruct((4, rows), F32),
             jax.ShapeDtypeStruct((LANES, rows), BF16),
         ],
         scratch_shapes=[wide, wide] + [narrow] * 6

time: 126 us -> 126 us (level)
  transfers between devices with their start and end apart: 17 -> 17, of which waited for: 8 -> 7; matrix products, arithmetic and copies ran while one was open for 0% -> 0% of each run, Pallas kernels for 26% -> 26%
where the time goes in v5:
time: 126 us; the launch traced here: 125 us
  Pallas kernels  80.6 us (64%)
  starting transfers between devices  28.3 us (22%)
  waiting for transfers between devices  11.6 us (9%)
  local copies, waits for them, and re-layouts  3.95 us (3%)
    pallas_call x1, Pallas kernels, local_pass(): pl.pallas_call(functools.partial(local_pass_body, chunk, tuple(placed)),...  43.1 us
    pallas_call x3, Pallas kernels, book_grad(): pl.pallas_call(functools.partial(book_body, first, tile, cuts), in_specs=...  28.1 us
    ppermute x15, starting transfers between devices, to_peer(): return lax.ppermute(v, 'code', pairs)  17.1 us
    all_to_all x1, starting transfers between devices, local(): xg = lax.all_to_all(xg, 'sub', 0, 0, tiled=True)  6.85 us
    all_to_all x1, waiting for transfers between devices, local(): xg = lax.all_to_all(xg, 'sub', 0, 0, tiled=True)  6.56 us
    ppermute x15, waiting for transfers between devices, to_peer(): return lax.ppermute(v, 'code', pairs)  5.08 us
    all_to_all x1, starting transfers between devices, local(): lax.all_to_all(out.reshape(n_sub, mine, LANES), 'sub', 0, 0, tiled=True)  4.34 us
    unnamed x6, local copies, waits for them, and re-layouts  3.95 us
  transfers between devices with their start and end apart: 17, of which 7 were waited for; matrix products, arithmetic and copies ran while one was open for 0% of the time, Pallas kernels for 26%

profile of v5, /device:TPU:1, one launch (start us, length us, event | category | flops | bytes accessed | tf_op | source)
XLA Modules:
  0.0 125.3 jit_solution(17341896402944227424)
XLA Ops:
  0.6 1.5 %collective-permute-start = (bf16[64,4096]{1,0:T(8,128)(2,1)}, bf16[64,4096]{1,0:T(8,128)(2,1)S(1)}, u32[]{:S(2)}, u32[]{:S(2)}) collective-permute-start(bf16[64,4096]{1,0:T(8,128)(2,1)} %bitcast.7), channel_id=1, source_target_pairs={{0,1},{1,0},{2,3},{3,2},{4,5},{5,4},{6,7},{7,6},{8,9},{9,8},{10,11... | collective-permute-start | bytes 1572872 | tf_op jit(solution)/shard_map/ppermute | solution.py:388
  2.1 0.1 pad_add_fusion.place_ref
  2.2 2.6 %pack.1 = bf16[16,128,128]{2,1,0:T(8,128)(2,1)} custom-call(s32[2]{0:T(128)S(1)} %pad_add_fusion.place_ref, bf16[256,1024]{1,0:T(8,128)(2,1)} %x_hbm.1, bf16[256,1024]{1,0:T(8,128)(2,1)} %g_hbm.1), custom_call_target="tpu_custom_call" | custom-call | flops 100000000 | bytes 2097152 | tf_op jit(solution)/shard_map/pack/pallas_call | solution.py:60
  4.8 6.8 %all-to-all-start = ((bf16[16,128,128]{2,1,0:T(8,128)(2,1)}), bf16[16,128,128]{2,1,0:T(8,128)(2,1)S(1)}, u32[]{:S(2)}, u32[]{:S(2)}) async-start(bf16[16,128,128]{2,1,0:T(8,128)(2,1)} %pack.1), calls=%async_computation | async-start | bytes 1048576 | tf_op jit(solution)/shard_map/all_to_all | solution.py:394
  11.7 0.0 collective-permute-done.mate_ref
  11.7 0.0 copy-start
  11.7 1.0 copy-done
  12.7 1.2 books.1
  13.9 0.0 copy-start.1
  13.9 1.3 %copy-done.1 = bf16[8192,128]{1,0:T(8,128)(2,1)} copy-done((bf16[8192,128]{1,0:T(8,128)(2,1)}, bf16[8192,128]{1,0:T(8,128)(2,1)S(1)}, u32[]{:S(2)}) %copy-start.1) | copy-done | bytes 2097176
  15.2 6.6 %all-to-all-done = bf16[16,128,128]{2,1,0:T(8,128)(2,1)S(1)} async-done(((bf16[16,128,128]{2,1,0:T(8,128)(2,1)}), bf16[16,128,128]{2,1,0:T(8,128)(2,1)S(1)}, u32[]{:S(2)}, u32[]{:S(2)}) %all-to-all-start) | async-done | bytes 524320 | tf_op jit(solution)/shard_map/all_to_all | solution.py:394
  21.8 0.0 copy-start.2
  21.8 1.6 %copy-done.2 = bf16[8192,128]{1,0:T(8,128)(2,1)S(1)} copy-done((bf16[8192,128]{1,0:T(8,128)(2,1)S(1)}, bf16[8192,128]{1,0:T(8,128)(2,1)}, u32[]{:S(2)}) %copy-start.2) | copy-done | bytes 2097176
  23.4 43.1 %local_pass.1 = (bf16[2048,4096]{1,0:T(8,128)(2,1)}, bf16[2048,2048]{1,0:T(8,128)(2,1)}, bf16[2048,2048]{1,0:T(8,128)(2,1)}, bf16[2048,8192]{1,0:T(8,128)(2,1)},...) custom-call(bf16[2048,128]{1,0:T(8,128)(2,1)S(1)} %bitcast.6, ...), custom_call_target="tpu_custom_call" | custom-call | flops 34359738368 | bytes 67108864 | tf_op jit(solution)/shard_map/local_pass/pallas_call | solution.py:243
  66.5 3.8 %collective-permute-start.3 = (f32[4,2048]{1,0:T(4,128)S(1)}, f32[4,2048]{1,0:T(4,128)S(1)}, u32[]{:S(2)}, u32[]{:S(2)}) collective-permute-start(f32[4,2048]{1,0:T(4,128)S(1)} %get-tuple-element.46.own_ref), channel_id=1, source_target_pairs={{0,6},{1,7},{2,0},{3,1},{4,2},{5,3},{6,4},{7,5},{8,14},{9,15},{10,... | collective-permute-start | bytes 98312 | tf_op jit(solution)/shard_map/ppermute | solution.py:388
  70.3 0.0 collective-permute-start.2
  70.3 0.7 collective-permute-start.1
  71.0 0.3 collective-permute-done.3.o3
  71.4 3.3 %collective-permute-done.2.o2 = f32[4,2048]{1,0:T(4,128)S(1)} collective-permute-done((f32[4,2048]{1,0:T(4,128)S(1)}, f32[4,2048]{1,0:T(4,128)S(1)}, u32[]{:S(2)}, u32[]{:S(2)}) %collective-permute-start.2) | collective-permute-done | bytes 32800 | tf_op jit(solution)/shard_map/ppermute | solution.py:388
  74.7 0.0 collective-permute-done.1.o1
  74.7 2.1 %mix.1 = (bf16[2048,128]{1,0:T(8,128)(2,1)}, bf16[128,2048]{1,0:T(8,128)(2,1)S(1)}) custom-call(f32[2048,128]{1,0:T(8,128)S(1)} %get-tuple-element.43.part_ref, f32[2048,128]{1,0:T(8,128)S(1)} %get-tuple-element.44.dx_ref, bf16[128,2048]{1,0:T(8,128)(2,1)S(1)} %get-tuple-element.45.xgt_ref, f32[4,2048]{1,0:T(4,128)S(1)} %get-tuple-element.46.own_ref, ...), custom_call_target="tpu_custom_call" | custom-call | flops 100000000 | bytes 4194304 | tf_op jit(solution)/shard_map/mix/pallas_call | solution.py:293
  76.8 4.3 %all-to-all-start.1 = ((bf16[16,128,128]{2,1,0:T(8,128)(2,1)}), bf16[16,128,128]{2,1,0:T(8,128)(2,1)S(1)}, u32[]{:S(2)}, u32[]{:S(2)}) async-start(bf16[16,128,128]{2,1,0:T(8,128)(2,1)} %bitcast.4), calls=%async_computation.1 | async-start | bytes 1048576 | tf_op jit(solution)/shard_map/all_to_all | solution.py:405
  81.2 12.7 %book_grad.3 = f32[64,4096]{1,0:T(8,128)S(1)} custom-call(bf16[128,2048]{1,0:T(8,128)(2,1)S(1)} %get-tuple-element.67.w_ref, bf16[2048,8192]{1,0:T(8,128)(2,1)} %get-tuple-element.49.ds_hbm, bf16[2048,4096]{1,0:T(8,128)(2,1)} %get-tuple-element.50.e_hbm), custom_call_target="tpu_custom_call" | custom-call | flops 8589934592 | bytes 33554432 | tf_op jit(solution)/shard_map/book_grad/pallas_call | solution.py:338
  93.9 0.0 all-to-all-done.1.a_ref
  93.9 3.1 %collective-permute-start.11 = (f32[64,4096]{1,0:T(8,128)S(1)}, f32[64,4096]{1,0:T(8,128)S(1)}, u32[]{:S(2)}, u32[]{:S(2)}) collective-permute-start(f32[64,4096]{1,0:T(8,128)S(1)} %book_grad.3), channel_id=1, source_target_pairs={{0,1},{1,0},{2,3},{3,2},{4,5},{5,4},{6,7},{7,6},{8,9},{9,8},{10,11... | collective-permute-start | bytes 3145736 | tf_op jit(solution)/shard_map/ppermute | solution.py:388
  97.0 0.6 pieces.1
  97.6 0.1 collective-permute-start.4
  97.6 1.8 %collective-permute-start.5 = (bf16[16,32,128]{2,1,0:T(8,128)(2,1)S(1)}, bf16[16,32,128]{2,1,0:T(8,128)(2,1)S(1)}, u32[]{:S(2)}, u32[]{:S(2)}) collective-permute-start(bf16[16,32,128]{2,1,0:T(8,128)(2,1)S(1)} %get-tuple-element.57), channel_id=1, source_target_pairs={{0,4},{1,5},{2,6},{3,7},{4,0},{5,1},{6,2},{7,3},{8,12},{9,13},{10,... | collective-permute-start | bytes 393224 | tf_op jit(solution)/shard_map/ppermute | solution.py:388
  99.4 2.0 %collective-permute-start.6 = (bf16[16,32,128]{2,1,0:T(8,128)(2,1)S(1)}, bf16[16,32,128]{2,1,0:T(8,128)(2,1)S(1)}, u32[]{:S(2)}, u32[]{:S(2)}) collective-permute-start(bf16[16,32,128]{2,1,0:T(8,128)(2,1)S(1)} %get-tuple-element.58), channel_id=1, source_target_pairs={{0,6},{1,7},{2,0},{3,1},{4,2},{5,3},{6,4},{7,5},{8,14},{9,15},{10,... | collective-permute-start | bytes 393224 | tf_op jit(solution)/shard_map/ppermute | solution.py:388
  101.4 7.7 %book_grad.4.near_1 = f32[64,2048]{1,0:T(8,128)S(1)} custom-call(bf16[128,2048]{1,0:T(8,128)(2,1)S(1)} %get-tuple-element.67.w_ref, bf16[2048,8192]{1,0:T(8,128)(2,1)} %get-tuple-element.49.ds_hbm, bf16[2048,2048]{1,0:T(8,128)(2,1)} %get-tuple-element.60.e_hbm), custom_call_target="tpu_custom_call" | custom-call | flops 4294967296 | bytes 16777216 | tf_op jit(solution)/shard_map/book_grad/pallas_call | solution.py:338
  109.1 0.0 collective-permute-done.4.refs_1_
  109.1 0.0 collective-permute-done.5.refs_2_
  109.1 0.0 collective-permute-done.6.refs_3_
  109.1 0.6 sums.1.refs_0_
  109.7 0.9 collective-permute-start.10
  110.7 0.6 collective-permute-start.9
  111.2 0.7 collective-permute-start.8
  112.0 0.9 collective-permute-start.7
  112.8 7.7 %book_grad.5.near_2 = f32[64,2048]{1,0:T(8,128)S(1)} custom-call(bf16[128,2048]{1,0:T(8,128)(2,1)S(1)} %get-tuple-element.67.w_ref, bf16[2048,8192]{1,0:T(8,128)(2,1)} %get-tuple-element.49.ds_hbm, bf16[2048,2048]{1,0:T(8,128)(2,1)} %get-tuple-element.68.e_hbm), custom_call_target="tpu_custom_call" | custom-call | flops 4294967296 | bytes 16777216 | tf_op jit(solution)/shard_map/book_grad/pallas_call | solution.py:338
  120.5 0.0 collective-permute-done.10.refs_4_
  120.5 0.0 collective-permute-done.9.refs_3_
  120.5 0.0 collective-permute-done.8.refs_2_
  120.6 0.4 collective-permute-done.7.refs_1_
  121.0 0.6 collective-permute-start.12
  121.6 0.1 collective-permute-start.13
  121.6 0.4 collective-permute-start.14
  122.1 0.5 collective-permute-done.12.refs_5_
  122.5 0.4 collective-permute-done.13.refs_6_
  122.9 0.2 collective-permute-done.14.refs_7_
  123.1 0.0 collective-permute-done.11.from_far
  123.1 2.2 %spread.1 = (bf16[256,1024]{1,0:T(8,128)(2,1)}, bf16[256,1024]{1,0:T(8,128)(2,1)}, f32[64,4096]{1,0:T(8,128)}) custom-call(s32[2]{0:T(128)S(1)} %pad_add_fusion.place_ref, f32[64,2048]{1,0:T(8,128)S(1)} %book_grad.4.near_1, f32[64,2048]{1,0:T(8,128)S(1)} %book_grad.5.near_2, f32[64,4096]{1,0:T(8,128)S(1)} %collective-permute-done.11.from_far, ...), custom_call_target="tpu_custom_call" | custom-call | flops 100000000 | bytes 2097152 | tf_op jit(solution)/shard_map/spread/pallas_call | solution.py:421
Async XLA Ops:
  0.6 11.0 %collective-permute-start = (bf16[64,4096]{1,0:T(8,128)(2,1)}, bf16[64,4096]{1,0:T(8,128)(2,1)S(1)}, u32[]{:S(2)}, u32[]{:S(2)}) collective-permute-start(bf16[64,4096]{1,0:T(8,128)(2,1)} %bitcast.7), channel_id=1, source_target_pairs={{0,1},{1,0},{2,3},{3,2},{4,5},{5,4},{6,7},{7,6},{8,9},{9,8},{10,11... | collective-permute-start | bytes 1572872 | tf_op jit(solution)/shard_map/ppermute | solution.py:388
  4.8 17.0 %all-to-all-start = ((bf16[16,128,128]{2,1,0:T(8,128)(2,1)}), bf16[16,128,128]{2,1,0:T(8,128)(2,1)S(1)}, u32[]{:S(2)}, u32[]{:S(2)}) async-start(bf16[16,128,128]{2,1,0:T(8,128)(2,1)} %pack.1), calls=%async_computation | async-start | bytes 1048576 | tf_op jit(solution)/shard_map/all_to_all | solution.py:394
  11.7 1.0 copy-start
  13.9 1.3 %copy-start.1 = (bf16[8192,128]{1,0:T(8,128)(2,1)}, bf16[8192,128]{1,0:T(8,128)(2,1)S(1)}, u32[]{:S(2)}) copy-start(bf16[8192,128]{1,0:T(8,128)(2,1)S(1)} %get-tuple-element.42.bookt_ref) | copy-start | bytes 6291460
  21.8 1.6 %copy-start.2 = (bf16[8192,128]{1,0:T(8,128)(2,1)S(1)}, bf16[8192,128]{1,0:T(8,128)(2,1)}, u32[]{:S(2)}) copy-start(bf16[8192,128]{1,0:T(8,128)(2,1)} %copy-done.1) | copy-start | bytes 6291460
  66.5 4.8 %collective-permute-start.3 = (f32[4,2048]{1,0:T(4,128)S(1)}, f32[4,2048]{1,0:T(4,128)S(1)}, u32[]{:S(2)}, u32[]{:S(2)}) collective-permute-start(f32[4,2048]{1,0:T(4,128)S(1)} %get-tuple-element.46.own_ref), channel_id=1, source_target_pairs={{0,6},{1,7},{2,0},{3,1},{4,2},{5,3},{6,4},{7,5},{8,14},{9,15},{10,... | collective-permute-start | bytes 98312 | tf_op jit(solution)/shard_map/ppermute | solution.py:388
  70.3 4.3 %collective-permute-start.2 = (f32[4,2048]{1,0:T(4,128)S(1)}, f32[4,2048]{1,0:T(4,128)S(1)}, u32[]{:S(2)}, u32[]{:S(2)}) collective-permute-start(f32[4,2048]{1,0:T(4,128)S(1)} %get-tuple-element.46.own_ref), channel_id=1, source_target_pairs={{0,4},{1,5},{2,6},{3,7},{4,0},{5,1},{6,2},{7,3},{8,12},{9,13},{10,... | collective-permute-start | bytes 98312 | tf_op jit(solution)/shard_map/ppermute | solution.py:388
  70.3 4.3 %collective-permute-start.1 = (f32[4,2048]{1,0:T(4,128)S(1)}, f32[4,2048]{1,0:T(4,128)S(1)}, u32[]{:S(2)}, u32[]{:S(2)}) collective-permute-start(f32[4,2048]{1,0:T(4,128)S(1)} %get-tuple-element.46.own_ref), channel_id=1, source_target_pairs={{0,2},{1,3},{2,4},{3,5},{4,6},{5,7},{6,0},{7,1},{8,10},{9,11},{10,... | collective-permute-start | bytes 98312 | tf_op jit(solution)/shard_map/ppermute | solution.py:388
  76.8 17.1 %all-to-all-start.1 = ((bf16[16,128,128]{2,1,0:T(8,128)(2,1)}), bf16[16,128,128]{2,1,0:T(8,128)(2,1)S(1)}, u32[]{:S(2)}, u32[]{:S(2)}) async-start(bf16[16,128,128]{2,1,0:T(8,128)(2,1)} %bitcast.4), calls=%async_computation.1 | async-start | bytes 1048576 | tf_op jit(solution)/shard_map/all_to_all | solution.py:405
  93.9 29.2 %collective-permute-start.11 = (f32[64,4096]{1,0:T(8,128)S(1)}, f32[64,4096]{1,0:T(8,128)S(1)}, u32[]{:S(2)}, u32[]{:S(2)}) collective-permute-start(f32[64,4096]{1,0:T(8,128)S(1)} %book_grad.3), channel_id=1, source_target_pairs={{0,1},{1,0},{2,3},{3,2},{4,5},{5,4},{6,7},{7,6},{8,9},{9,8},{10,11... | collective-permute-start | bytes 3145736 | tf_op jit(solution)/shard_map/ppermute | solution.py:388
  97.6 11.5 %collective-permute-start.4 = (bf16[16,32,128]{2,1,0:T(8,128)(2,1)S(1)}, bf16[16,32,128]{2,1,0:T(8,128)(2,1)S(1)}, u32[]{:S(2)}, u32[]{:S(2)}) collective-permute-start(bf16[16,32,128]{2,1,0:T(8,128)(2,1)S(1)} %get-tuple-element.56), channel_id=1, source_target_pairs={{0,2},{1,3},{2,4},{3,5},{4,6},{5,7},{6,0},{7,1},{8,10},{9,11},{10,... | collective-permute-start | bytes 393224 | tf_op jit(solution)/shard_map/ppermute | solution.py:388
  97.6 11.5 %collective-permute-start.5 = (bf16[16,32,128]{2,1,0:T(8,128)(2,1)S(1)}, bf16[16,32,128]{2,1,0:T(8,128)(2,1)S(1)}, u32[]{:S(2)}, u32[]{:S(2)}) collective-permute-start(bf16[16,32,128]{2,1,0:T(8,128)(2,1)S(1)} %get-tuple-element.57), channel_id=1, source_target_pairs={{0,4},{1,5},{2,6},{3,7},{4,0},{5,1},{6,2},{7,3},{8,12},{9,13},{10,... | collective-permute-start | bytes 393224 | tf_op jit(solution)/shard_map/ppermute | solution.py:388
  99.4 9.7 %collective-permute-start.6 = (bf16[16,32,128]{2,1,0:T(8,128)(2,1)S(1)}, bf16[16,32,128]{2,1,0:T(8,128)(2,1)S(1)}, u32[]{:S(2)}, u32[]{:S(2)}) collective-permute-start(bf16[16,32,128]{2,1,0:T(8,128)(2,1)S(1)} %get-tuple-element.58), channel_id=1, source_target_pairs={{0,6},{1,7},{2,0},{3,1},{4,2},{5,3},{6,4},{7,5},{8,14},{9,15},{10,... | collective-permute-start | bytes 393224 | tf_op jit(solution)/shard_map/ppermute | solution.py:388
  109.7 10.8 %collective-permute-start.10 = (bf16[16,32,128]{2,1,0:T(8,128)(2,1)S(1)}, bf16[16,32,128]{2,1,0:T(8,128)(2,1)S(1)}, u32[]{:S(2)}, u32[]{:S(2)}) collective-permute-start(bf16[16,32,128]{2,1,0:T(8,128)(2,1)S(1)} %sums.1.refs_0_), channel_id=1, source_target_pairs={{0,1},{1,0},{2,3},{3,2},{4,5},{5,4},{6,7},{7,6},{8,9},{9,8},{10,11... | collective-permute-start | bytes 393224 | tf_op jit(solution)/shard_map/ppermute | solution.py:388
  110.7 9.9 %collective-permute-start.9 = (bf16[16,32,128]{2,1,0:T(8,128)(2,1)S(1)}, bf16[16,32,128]{2,1,0:T(8,128)(2,1)S(1)}, u32[]{:S(2)}, u32[]{:S(2)}) collective-permute-start(bf16[16,32,128]{2,1,0:T(8,128)(2,1)S(1)} %sums.1.refs_0_), channel_id=1, source_target_pairs={{0,6},{1,7},{2,0},{3,1},{4,2},{5,3},{6,4},{7,5},{8,14},{9,15},{10,... | collective-permute-start | bytes 393224 | tf_op jit(solution)/shard_map/ppermute | solution.py:388
  111.2 9.3 %collective-permute-start.8 = (bf16[16,32,128]{2,1,0:T(8,128)(2,1)S(1)}, bf16[16,32,128]{2,1,0:T(8,128)(2,1)S(1)}, u32[]{:S(2)}, u32[]{:S(2)}) collective-permute-start(bf16[16,32,128]{2,1,0:T(8,128)(2,1)S(1)} %sums.1.refs_0_), channel_id=1, source_target_pairs={{0,4},{1,5},{2,6},{3,7},{4,0},{5,1},{6,2},{7,3},{8,12},{9,13},{10,... | collective-permute-start | bytes 393224 | tf_op jit(solution)/shard_map/ppermute | solution.py:388
  112.0 9.0 %collective-permute-start.7 = (bf16[16,32,128]{2,1,0:T(8,128)(2,1)S(1)}, bf16[16,32,128]{2,1,0:T(8,128)(2,1)S(1)}, u32[]{:S(2)}, u32[]{:S(2)}) collective-permute-start(bf16[16,32,128]{2,1,0:T(8,128)(2,1)S(1)} %sums.1.refs_0_), channel_id=1, source_target_pairs={{0,2},{1,3},{2,4},{3,5},{4,6},{5,7},{6,0},{7,1},{8,10},{9,11},{10,... | collective-permute-start | bytes 393224 | tf_op jit(solution)/shard_map/ppermute | solution.py:388
  121.0 1.6 %collective-permute-start.12 = (bf16[16,32,128]{2,1,0:T(8,128)(2,1)S(1)}, bf16[16,32,128]{2,1,0:T(8,128)(2,1)S(1)}, u32[]{:S(2)}, u32[]{:S(2)}) collective-permute-start(bf16[16,32,128]{2,1,0:T(8,128)(2,1)S(1)} %collective-permute-done.7.refs_1_), channel_id=1, source_target_pairs={{0,1},{1,0},{2,3},{3,2},{4,5},{5,4},{6,7},{7,6},{8,9},{9,8},{10,11... | collective-permute-start | bytes 393224 | tf_op jit(solution)/shard_map/ppermute | solution.py:388
  121.6 1.3 %collective-permute-start.13 = (bf16[16,32,128]{2,1,0:T(8,128)(2,1)S(1)}, bf16[16,32,128]{2,1,0:T(8,128)(2,1)S(1)}, u32[]{:S(2)}, u32[]{:S(2)}) collective-permute-start(bf16[16,32,128]{2,1,0:T(8,128)(2,1)S(1)} %collective-permute-done.8.refs_2_), channel_id=1, source_target_pairs={{0,1},{1,0},{2,3},{3,2},{4,5},{5,4},{6,7},{7,6},{8,9},{9,8},{10,11... | collective-permute-start | bytes 393224 | tf_op jit(solution)/shard_map/ppermute | solution.py:388
  121.6 1.4 %collective-permute-start.14 = (bf16[16,32,128]{2,1,0:T(8,128)(2,1)S(1)}, bf16[16,32,128]{2,1,0:T(8,128)(2,1)S(1)}, u32[]{:S(2)}, u32[]{:S(2)}) collective-permute-start(bf16[16,32,128]{2,1,0:T(8,128)(2,1)S(1)} %collective-permute-done.9.refs_3_), channel_id=1, source_target_pairs={{0,1},{1,0},{2,3},{3,2},{4,5},{5,4},{6,7},{7,6},{8,9},{9,8},{10,11... | collective-permute-start | bytes 393224 | tf_op jit(solution)/shard_map/ppermute | solution.py:388
